TPU v7x, 128 devices: a whole 4x4x4 slice. The times are simulated.
128 devices in a mesh: lat: 32 (over y, x, core), lon: 4 (over z).
Axes of the slice: x: 4, y: 4, z: 4, core: 2. Of those that a mesh axis runs over, the one named last changes fastest.
Arguments:
- terminal: float32 [2, 256, 100, 2048], P(None, 'lat', None, 'lon'), may hold values from -6 to 6
- courant: float32 [4, 256, 100, 2048], P(None, 'lat', None, 'lon'), may hold values from 0.02 to 0.24
- inverse: float32 [256, 100, 100], P('lat'), may hold values from -1.5 to 1.5
- land_mask: int32 [256, 2048], P('lat', 'lon'), may hold values 0 or 1
- obs_values: float32 [262144, 128], P(('lat', 'lon')), may hold values from -6 to 6
- obs_owner: int32 [262144, 1], P(('lat', 'lon')), may hold values from 0 to 127; in each aligned block of 2048 rows (0 to 2047, 2048 to 4095, ...) at most 32 rows name the same one
- obs_cell: int32 [262144], P(('lat', 'lon')), may hold values from 0 to 6399
Outputs:
- adjoint: float32 [2, 256, 100, 2048], P(None, 'lat', None, 'lon')
Inputs may be any that keep to these rules, and one draw needn't show every extreme that they name: `obs_owner`: among the 2048 blocks of one device at most 32 name the same tile, a bound that some block reaches of them.
All inputs are finite; a program needn't handle non-finite values. No bound on the sum of `land_mask` on one device may be relied on, other than what follows from the above.
Results may differ from a plain program's by a relative error of at most 0.0001.
Values sent between devices are 32-bit elements; how exact they have to be, the bound alone decides.
No kernel may reach another device: no remote copies, remote signals or barrier semaphores. Data moves between devices by JAX's collectives and lax.ppermute only.
A program may use at most 128 MiB of HBM per device.

v0:
```python
import functools

import jax
import jax.numpy as jnp
from jax import lax
from jax.experimental import pallas as pl
from jax.experimental.pallas import tpu as pltpu
from jax.sharding import PartitionSpec as P

STEPS = 2
LANES = 128
SLOTS = 33
BANKS = 4
MIB = 1 << 20


def padded_levels(levels):
    return -(-levels // 8) * 8


VMEM = pl.BlockSpec(memory_space=pltpu.VMEM)
SMEM = pl.BlockSpec(memory_space=pltpu.SMEM)
HBM = pl.BlockSpec(memory_space=pltpu.HBM)


def pack_kernel(geometry, owner_hbm, cell_hbm, values_hbm, send_ref, slot_ref, owner_ref, cell_ref, values_ref, slots, pay, sems):
    levels, high, columns, devices = geometry
    per_row = levels * columns
    chunks = owner_ref.shape[0]
    f32, bf16 = jnp.float32, jnp.bfloat16
    get_owner = pltpu.make_async_copy(owner_hbm, owner_ref, sems.at[0])
    get_cell = pltpu.make_async_copy(cell_hbm, cell_ref, sems.at[1])
    get_values = pltpu.make_async_copy(values_hbm, values_ref, sems.at[2])
    get_owner.start()
    get_cell.start()
    get_values.start()
    sub = lax.broadcasted_iota(jnp.int32, (LANES, LANES), 0)
    lane = lax.broadcasted_iota(jnp.int32, (LANES, LANES), 1)
    before = jnp.concatenate(
        [jnp.where(sub < lane, 1.0, 0.0), jnp.ones((LANES, LANES), f32)], axis=1
    ).astype(bf16)
    get_owner.wait()
    get_cell.wait()
    cells = cell_ref[...]
    tile_row = ((cells >> 4) * 5243) >> 17
    rest = cells - tile_row * per_row
    level = rest >> 2
    column = rest & 3
    place = (tile_row * columns + column) * high + level
    upper, lower = (place >> 6).astype(f32), (place & 63).astype(f32)
    carry = jnp.zeros((LANES, LANES), f32)
    total = jnp.zeros((LANES, LANES), f32)
    for i in range(chunks):
        own = owner_ref[i : i + 1, :]
        hot = jnp.where(sub == own, 1.0, 0.0)
        hot16 = hot.astype(bf16)
        counted = jnp.dot(hot16, before, preferred_element_type=f32)
        rank = jnp.sum(hot * (counted[:, :LANES] + carry), axis=0, keepdims=True)
        carry = carry + counted[:, LANES:]
        rank_i = rank.astype(jnp.int32)
        slots[i : i + 1, :] = own * SLOTS + rank_i
        near_sub = sub[:64]
        parts = jnp.where(
            near_sub == rank_i,
            jnp.broadcast_to(upper[i : i + 1, :], (64, LANES)),
            jnp.where(near_sub == rank_i + 32, jnp.broadcast_to(lower[i : i + 1, :], (64, LANES)), 0.0),
        )
        parts = jnp.concatenate([parts, jnp.zeros_like(parts)], axis=0).astype(bf16)
        total = total + lax.dot_general(
            hot16, parts, (((1,), (1,)), ((), ())), preferred_element_type=f32
        )
    copy = pltpu.make_async_copy(slots, slot_ref, sems.at[3])
    copy.start()
    places = total * 64.0 + pltpu.roll(total, LANES - 32, 1)
    dump = f32(2 * 8 * columns * high)
    pay[...] = jnp.where(
        lane < 32, jnp.where(lane.astype(f32) < carry, places, dump), carry
    )
    for o in range(devices):
        send_ref[o * SLOTS + 32] = pay[o : o + 1, :]
    get_values.wait()
    copy.wait()
    unroll = 32
    for i in range(chunks):

        @pl.loop(0, LANES // unroll)
        def _(c):
            base = c * unroll
            for u in range(unroll):
                send_ref[slot_ref[i, base + u]] = values_ref[i * LANES + base + u]


def pack(owner, cell, values, levels, high, columns, devices):
    rows = values.shape[0]
    chunks = rows // LANES
    return pl.pallas_call(
        functools.partial(pack_kernel, (levels, high, columns, devices)),
        out_shape=jax.ShapeDtypeStruct((devices * SLOTS, 1, LANES), jnp.float32),
        in_specs=[HBM] * 3,
        out_specs=VMEM,
        scratch_shapes=[
            pltpu.SMEM((chunks, LANES), jnp.int32),
            pltpu.VMEM((chunks, LANES), jnp.int32),
            pltpu.VMEM((chunks, LANES), jnp.int32),
            pltpu.VMEM((rows, 1, LANES), jnp.float32),
            pltpu.VMEM((chunks, LANES), jnp.int32),
            pltpu.VMEM((LANES, LANES), jnp.float32),
            pltpu.SemaphoreType.DMA((4,)),
        ],
        compiler_params=pltpu.CompilerParams(vmem_limit_bytes=12 * MIB),
    )(owner.reshape(chunks, LANES), cell.reshape(chunks, LANES), values.reshape(rows, 1, LANES))


def vertical(weight, cells):
    high = cells.shape[0]
    whole = cells.astype(jnp.bfloat16).astype(jnp.float32)
    both = jnp.concatenate([whole, cells - whole], axis=0).astype(jnp.bfloat16)
    product = jnp.dot(weight, both, preferred_element_type=jnp.float32)
    return product[:high] + product[high:]


def keep_ends(row, first, last, west, east):
    lane = lax.broadcasted_iota(jnp.int32, first.shape, 1)
    west[...] = jnp.where(lane == row, pltpu.roll(first, row, 1), west[...])
    east[...] = jnp.where(lane == row, pltpu.roll(last, (row + 1) % LANES, 1), east[...])


def hand_out(odd_ref, field, west, east, near_ref, far_ref, pair_ref, other_ref):
    last = field.shape[1] - 1
    for axis, (low, top, mine, others) in enumerate((
        (field.at[:, 0], field.at[:, last], near_ref, far_ref),
        (west, east, pair_ref, other_ref),
    )):
        odd = odd_ref[axis]

        @pl.when(odd == 0)
        def _():
            mine[...] = top[...]
            others[...] = low[...]

        @pl.when(odd != 0)
        def _():
            mine[...] = low[...]
            others[...] = top[...]


def start_kernel(geometry, odd_ref, got_ref, base_hbm, weight_hbm, courant_ref,
                 out_ref, near_ref, far_ref, pair_ref, other_ref, *scratch):
    tracers, rows, high, columns, devices = geometry
    banks, addr_v, addr_s, base_ref, weight_ref, west, east, sems = scratch[:BANKS], *scratch[BANKS:]
    get_base = pltpu.make_async_copy(base_hbm, base_ref, sems.at[1])
    get_weight = pltpu.make_async_copy(weight_hbm, weight_ref, sems.at[2])
    get_base.start()
    get_weight.start()
    for o in range(devices):
        addr_v[o : o + 1, :] = got_ref[o * SLOTS + 32].astype(jnp.int32)
    copy = pltpu.make_async_copy(addr_v, addr_s, sems.at[0])
    copy.start()
    clear = 64
    for bank in banks:

        @pl.loop(0, bank.shape[0] // clear)
        def _(i):
            bank[pl.ds(pl.multiple_of(i * clear, clear), clear), :] = jnp.zeros((clear, LANES), jnp.float32)

    west[...] = jnp.zeros_like(west)
    east[...] = jnp.zeros_like(east)
    copy.wait()

    @pl.loop(0, devices // BANKS)
    def _(group):
        first = group * BANKS
        most = addr_s[first, 32]
        for b in range(1, BANKS):
            most = jnp.maximum(most, addr_s[first + b, 32])

        @pl.loop(0, (most + 3) // 4)
        def _(c):
            for u in range(4):
                for b, bank in enumerate(banks):
                    place = addr_s[first + b, c * 4 + u]
                    bank[pl.ds(place, 1), :] += got_ref[(first + b) * SLOTS + c * 4 + u]

    get_base.wait()
    get_weight.wait()
    for j in range(rows):
        weight = weight_ref[j]
        for t in range(tracers):
            row = t * rows + j
            done = []
            for half in range(columns // 2):
                pieces = []
                for c in (2 * half, 2 * half + 1):
                    at = (row * columns + c) * high
                    piece = base_ref[at : at + high, :]
                    for bank in banks:
                        piece = piece + bank[at : at + high, :]
                    pieces.append(piece)
                level = vertical(weight, jnp.concatenate(pieces, axis=1))
                out_ref[t, j, :, half * 2 * LANES : (half + 1) * 2 * LANES] = level
                done.append(level)
            keep_ends(row, done[0][:, :LANES], done[-1][:, LANES:], west, east)
    hand_out(odd_ref, out_ref, west, east, near_ref, far_ref, pair_ref, other_ref)


def shapes_of(tracers, rows, high, wide):
    f32 = jnp.float32
    edge = jax.ShapeDtypeStruct((tracers, high, wide), f32)
    end = jax.ShapeDtypeStruct((high, LANES), f32)
    return jax.ShapeDtypeStruct((tracers, rows, high, wide), f32), edge, edge, end, end


def start(odd, got, base, weight, courant, tracers, rows, high, columns, devices):
    f32 = jnp.float32
    places = tracers * rows * columns * high
    return pl.pallas_call(
        functools.partial(start_kernel, (tracers, rows, high, columns, devices)),
        out_shape=shapes_of(tracers, rows, high, columns * LANES),
        in_specs=[SMEM, VMEM, HBM, HBM, VMEM],
        out_specs=(VMEM,) * 5,
        scratch_shapes=[pltpu.VMEM((places + 64, LANES), f32) for _ in range(BANKS)]
        + [
            pltpu.VMEM((devices, LANES), jnp.int32),
            pltpu.SMEM((devices, LANES), jnp.int32),
            pltpu.VMEM(base.shape, f32),
            pltpu.VMEM(weight.shape, weight.dtype),
            pltpu.VMEM((high, LANES), f32),
            pltpu.VMEM((high, LANES), f32),
            pltpu.SemaphoreType.DMA((3,)),
        ],
        compiler_params=pltpu.CompilerParams(vmem_limit_bytes=40 * MIB),
    )(odd, got, base, weight, courant)


def ends_in_place(odd_ref, pair_ref, other_ref, west, east):
    odd = odd_ref[1] != 0
    pair, other = pair_ref[...], other_ref[...]
    west[...] = jnp.where(odd, pair, other)
    east[...] = jnp.where(odd, other, pair)


def transported(t, j, levels, field, courant_ref, mask, lat, west, east, store):
    rows, wide = field.shape[1], field.shape[3]
    row = t * rows + j
    tiles = [slice(c * LANES, (c + 1) * LANES) for c in range(wide // LANES)]
    for at in range(0, levels, 8):
        count = min(8, levels - at)
        strip = slice(at, at + count)
        lane = lax.broadcasted_iota(jnp.int32, (count, LANES), 1)
        here = [field[t, j, strip, tile] for tile in tiles]
        left = [pltpu.roll(x, LANES - 1, 1) for x in here]
        left.append(pltpu.roll(east[strip, :], LANES - 1 - row, 1))
        right = [pltpu.roll(west[strip, :], (LANES - row) % LANES, 1)]
        right += [pltpu.roll(x, 1, 1) for x in here]
        for c, tile in enumerate(tiles):
            v = here[c]
            e = jnp.where(lane == LANES - 1, left[c + 1], left[c])
            w = jnp.where(lane == 0, right[c], right[c + 1])
            n = lat[0](t, strip, tile) if j == rows - 1 else field[t, j + 1, strip, tile]
            s = lat[1](t, strip, tile) if j == 0 else field[t, j - 1, strip, tile]
            moved = (
                v
                + courant_ref[0, j, strip, tile] * (e - v)
                + courant_ref[1, j, strip, tile] * (w - v)
                + courant_ref[2, j, strip, tile] * (n - v)
                + courant_ref[3, j, strip, tile] * (s - v)
            )
            store(strip, tile, mask[c] * moved)


def mask_row(mask_ref, j):
    wide = mask_ref.shape[1]
    return [mask_ref[j : j + 1, c : c + LANES].astype(jnp.float32) for c in range(0, wide, LANES)]


def by_side(odd_ref, near_ref, far_ref):
    odd = odd_ref[0] != 0
    north = lambda t, strip, tile: jnp.where(odd, far_ref[t, strip, tile], near_ref[t, strip, tile])
    south = lambda t, strip, tile: jnp.where(odd, near_ref[t, strip, tile], far_ref[t, strip, tile])
    return north, south


def advance(rows_done, levels, lat, field, courant_ref, mask_ref, hw, he, weight_ref, out_ref, west, east, state):
    tracers, rows, high, wide = field.shape
    for slot in range(state.shape[0]):
        state[slot, levels:high, :] = jnp.zeros((high - levels, wide), jnp.float32)
    for j in rows_done:
        mask = mask_row(mask_ref, j)
        weight = weight_ref[j]
        for t in range(tracers):
            slot = (j * tracers + t) % state.shape[0]

            def store(strip, tile, value):
                state[slot, strip, tile] = value

            transported(t, j, levels, field, courant_ref, mask, lat, hw, he, store)
            done = []
            for at in range(0, wide, 2 * LANES):
                level = vertical(weight, state[slot, :, at : at + 2 * LANES])
                out_ref[t, j, :, at : at + 2 * LANES] = level
                done.append(level)
            keep_ends(t * rows + j, done[0][:, :LANES], done[-1][:, LANES:], west, east)


def inner_kernel(levels, odd_ref, pair_ref, other_ref, field, courant_ref, mask_ref, weight_ref,
                 out_ref, west, east, hw, he, state):
    ends_in_place(odd_ref, pair_ref, other_ref, hw, he)
    west[...] = jnp.zeros_like(west)
    east[...] = jnp.zeros_like(east)
    rows = field.shape[1]
    advance(range(1, rows - 1), levels, None, field, courant_ref, mask_ref, hw, he, weight_ref, out_ref, west, east, state)


def edge_kernel(levels, odd_ref, pair_ref, other_ref, field, courant_ref, mask_ref, weight_ref, near_in, far_in,
                part_ref, west_in, east_in, out_ref, near_ref, far_ref, pair_out, other_out, hw, he, west, east, state):
    ends_in_place(odd_ref, pair_ref, other_ref, hw, he)
    west[...] = west_in[...]
    east[...] = east_in[...]
    rows = field.shape[1]
    lat = by_side(odd_ref, near_in, far_in)
    advance((0, rows - 1), levels, lat, field, courant_ref, mask_ref, hw, he, weight_ref, out_ref, west, east, state)
    hand_out(odd_ref, out_ref, west, east, near_ref, far_ref, pair_out, other_out)


def step(levels, odd, field, courant, mask, weight, halos):
    f32 = jnp.float32
    near, far, pair, other = halos
    tracers, rows, high, wide = field.shape
    field_shape, edge, _, end, _ = shapes_of(tracers, rows, high, wide)
    ends = [pltpu.VMEM((high, LANES), f32)] * 2
    state = [pltpu.VMEM((2, high, wide), f32)]
    params = pltpu.CompilerParams(vmem_limit_bytes=20 * MIB)
    cost = lambda n: pl.CostEstimate(flops=n * 500_000_000, bytes_accessed=n * 1_000_000, transcendentals=0)
    part, west, east = pl.pallas_call(
        functools.partial(inner_kernel, levels),
        out_shape=(field_shape, end, end),
        in_specs=[SMEM] + [VMEM] * 6,
        out_specs=(VMEM,) * 3,
        scratch_shapes=ends + state,
        compiler_params=params,
        cost_estimate=cost(rows - 2),
    )(odd, pair, other, field, courant, mask, weight)
    return pl.pallas_call(
        functools.partial(edge_kernel, levels),
        out_shape=(field_shape, edge, edge, end, end),
        in_specs=[SMEM] + [VMEM] * 11,
        out_specs=(VMEM,) * 5,
        scratch_shapes=ends + ends + state,
        input_output_aliases={9: 0},
        compiler_params=params,
        cost_estimate=cost(2),
    )(odd, pair, other, field, courant, mask, weight, near, far, part, west, east)


def finish(rows_done, levels, lat, field, courant_ref, mask_ref, hw, he, out_ref, state, sems):
    tracers = field.shape[0]
    slots = state.shape[0]
    flying = {}
    for k, (j, t) in enumerate((j, t) for j in rows_done for t in range(tracers)):
        slot = k % slots
        if slot in flying:
            flying.pop(slot).wait()

        def store(strip, tile, value):
            state[slot, strip, tile] = value

        transported(t, j, levels, field, courant_ref, mask_row(mask_ref, j), lat, hw, he, store)
        copy = pltpu.make_async_copy(state.at[slot], out_ref.at[t, :, j, :], sems.at[slot])
        copy.start()
        flying[slot] = copy
    for copy in flying.values():
        copy.wait()


def final_inner_kernel(levels, odd_ref, pair_ref, other_ref, field, courant_ref, mask_ref, out_ref, hw, he, state, sems):
    ends_in_place(odd_ref, pair_ref, other_ref, hw, he)
    rows = field.shape[1]
    finish(range(1, rows - 1), levels, None, field, courant_ref, mask_ref, hw, he, out_ref, state, sems)


def final_edge_kernel(levels, odd_ref, pair_ref, other_ref, field, courant_ref, mask_ref, near_in, far_in, part_ref,
                      out_ref, hw, he, state, sems):
    ends_in_place(odd_ref, pair_ref, other_ref, hw, he)
    rows = field.shape[1]
    lat = by_side(odd_ref, near_in, far_in)
    finish((0, rows - 1), levels, lat, field, courant_ref, mask_ref, hw, he, out_ref, state, sems)


def last_step(levels, odd, field, courant, mask, halos):
    f32 = jnp.float32
    near, far, pair, other = halos
    tracers, rows, high, wide = field.shape
    slots = 4
    scratch = [pltpu.VMEM((high, LANES), f32)] * 2 + [
        pltpu.VMEM((slots, levels, wide), f32),
        pltpu.SemaphoreType.DMA((slots,)),
    ]
    shape = jax.ShapeDtypeStruct((tracers, levels, rows, wide), f32)
    params = pltpu.CompilerParams(vmem_limit_bytes=20 * MIB)
    cost = lambda n: pl.CostEstimate(flops=n * 500_000_000, bytes_accessed=n * 1_000_000, transcendentals=0)
    part = pl.pallas_call(
        functools.partial(final_inner_kernel, levels),
        out_shape=shape,
        in_specs=[SMEM] + [VMEM] * 5,
        out_specs=HBM,
        scratch_shapes=scratch,
        compiler_params=params,
        cost_estimate=cost(rows - 2),
    )(odd, pair, other, field, courant, mask)
    return pl.pallas_call(
        functools.partial(final_edge_kernel, levels),
        out_shape=shape,
        in_specs=[SMEM] + [VMEM] * 7 + [HBM],
        out_specs=HBM,
        scratch_shapes=scratch,
        input_output_aliases={8: 0},
        compiler_params=params,
        cost_estimate=cost(2),
    )(odd, pair, other, field, courant, mask, near, far, part)


def weights(inverse, high):
    rows, levels, _ = inverse.shape
    turned = jnp.swapaxes(inverse, 1, 2)
    pad = ((0, 0), (0, high - levels), (0, high - levels))
    whole = jnp.pad(lax.reduce_precision(turned, 8, 7), pad)
    rest = jnp.pad(turned, pad) - whole
    return jnp.concatenate(
        [jnp.concatenate([whole, whole], 2), jnp.concatenate([rest, rest], 2)], 1
    ).astype(jnp.bfloat16)


def exchange(near, far, pair, other):
    lat = lax.axis_size("lat")
    lon = lax.axis_size("lon")
    next_pair = [(i, i + 1 if i % 2 else i - 1) for i in range(1, lat - 1)]
    other = lax.ppermute(other, "lon", [(i, (i + 1 if i % 2 else i - 1) % lon) for i in range(lon)])
    pair = lax.ppermute(pair, "lon", [(i, i ^ 1) for i in range(lon)])
    far = lax.ppermute(far, "lat", next_pair)
    near = lax.ppermute(near, "lat", [(i, i ^ 1) for i in range(lat)])
    return near, far, pair, other


def local(terminal, courant, inverse, land_mask, obs_values, obs_owner, obs_cell):
    devices = lax.axis_size("lat") * lax.axis_size("lon")
    tracers, rows, levels, wide = terminal.shape
    high = padded_levels(levels)
    columns = wide // LANES
    odd = jnp.stack([lax.axis_index("lat") % 2, lax.axis_index("lon") % 2]).astype(jnp.int32)
    send = pack(obs_owner, obs_cell, obs_values, levels, high, columns, devices)
    got = lax.all_to_all(send, ("lat", "lon"), split_axis=0, concat_axis=0, tiled=True)
    base = terminal.reshape(tracers * rows, levels, columns, LANES)
    base = jnp.pad(jnp.swapaxes(base, 1, 2), ((0, 0), (0, 0), (0, high - levels), (0, 0)))
    base = base.reshape(tracers * rows * columns * high, LANES)
    weight = weights(inverse, high)
    field, *edges = start(odd, got, base, weight, courant, tracers, rows, high, columns, devices)
    for _ in range(STEPS - 1):
        field, *edges = step(levels, odd, field, courant, land_mask, weight, exchange(*edges))
    out = last_step(levels, odd, field, courant, land_mask, exchange(*edges))
    return jnp.swapaxes(out, 1, 2)


def solution(mesh):
    placed = (
        P(None, "lat", None, "lon"),
        P(None, "lat", None, "lon"),
        P("lat", None, None),
        P("lat", "lon"),
        P(("lat", "lon"), None),
        P(("lat", "lon"), None),
        P(("lat", "lon")),
    )
    return jax.shard_map(
        local, mesh=mesh, in_specs=placed, out_specs=P(None, "lat", None, "lon"), check_vma=False
    )
```

profile of v0, /device:TPU:8, one launch (start us, length us, event | category | flops | bytes accessed | tf_op | source)
XLA Modules:
  0.0 102.6 jit_solution(11661151151388258007)
XLA Ops:
  0.0 1.2 %copy-done.1 = f32[2048,128]{1,0:T(8,128)S(1)} copy-done((f32[2048,128]{1,0:T(8,128)S(1)}, f32[2048,128]{1,0:T(8,128)}, u32[]{:S(2)}) %copy-start.1) | copy-done | bytes 1048600
  1.2 0.7 copy-done.3
  1.9 0.7 copy-done.4
  2.6 7.6 %shard_map.73 = f32[4224,1,128]{2,1,0:T(1,128)} custom-call(s32[16,128]{1,0:T(8,128)S(1)} %bitcast.18, s32[16,128]{1,0:T(8,128)S(1)} %bitcast.19, f32[2048,1,128]{2,1,0:T(1,128)S(1)} %bitcast.17), custom_call_target="tpu_custom_call" | custom-call | tf_op jit(solution)/shard_map/pallas_call | solution.py:96
  10.3 10.9 %all-to-all-start = ((f32[4224,1,128]{2,1,0:T(1,128)}), f32[4224,1,128]{2,1,0:T(1,128)}, u32[]{:S(2)}, u32[]{:S(2)}) async-start(f32[4224,1,128]{2,1,0:T(1,128)} %shard_map.73), calls=%async_computation | async-start | bytes 4325376 | tf_op jit(solution)/shard_map/all_to_all | solution.py:451
  21.2 1.0 copy.18
  22.1 2.4 %copy.16 = f32[2,8,100,512]{3,1,0,2:T(8,128)S(1)} copy(f32[2,8,100,512]{3,1,2,0:T(8,128)} %param.7) | data formatting | bytes 6553600 | tf_op args[0]
  24.5 2.3 %reshape.18 = f32[16,100,4,128]{3,2,0,1:T(4,128)} reshape(f32[2,8,100,512]{3,1,0,2:T(8,128)S(1)} %copy.16) | data formatting | bytes 6553600 | tf_op jit(solution)/shard_map/reshape | solution.py:452
  26.9 3.8 %copy.24 = f32[16,4,100,128]{3,2,1,0:T(8,128)S(1)} copy(f32[16,4,100,128]{3,1,0,2:T(4,128)} %bitcast.20) | data formatting | bytes 6553600
  30.7 9.5 %copy.19.courant_ref = f32[4,8,100,512]{3,2,1,0:T(8,128)} copy(f32[4,8,100,512]{3,1,2,0:T(8,128)} %param.8) | data formatting | bytes 13107200 | tf_op args[1]
  40.2 2.0 %pad.11.clone = f32[16,4,104,128]{3,2,1,0:T(8,128)} pad(f32[16,4,100,128]{3,2,1,0:T(8,128)S(1)} %copy.24, f32[]{:T(128)} %constant.28.clone.1), padding=0_0x0_0x0_4x0_0 | pad | bytes 6684676 | tf_op jit(solution)/shard_map/jit(_pad)/pad | solution.py:453
  42.2 0.1 pad_add_fusion.odd_ref
  42.5 0.4 maximum_maximum_fusion.weight_hbm.weight_ref
  42.8 8.2 %all-to-all-done.got_ref = f32[4224,1,128]{2,1,0:T(1,128)} async-done(((f32[4224,1,128]{2,1,0:T(1,128)}), f32[4224,1,128]{2,1,0:T(1,128)}, u32[]{:S(2)}, u32[]{:S(2)}) %all-to-all-start) | async-done | bytes 2162720 | tf_op jit(solution)/shard_map/all_to_all | solution.py:451
  51.1 2.0 %copy-done = f32[16,4,104,128]{3,2,1,0:T(8,128)S(1)} copy-done((f32[16,4,104,128]{3,2,1,0:T(8,128)S(1)}, f32[16,4,104,128]{3,2,1,0:T(8,128)}, u32[]{:S(2)}) %copy-start) | copy-done | bytes 3407896
  53.0 12.1 %shard_map.74 = (f32[2,8,104,512]{3,2,1,0:T(8,128)S(1)}, f32[2,104,512]{2,1,0:T(8,128)S(1)}, f32[2,104,512]{2,1,0:T(8,128)S(1)}, f32[104,128]{1,0:T(8,128)S(1)}, f32[104,128]{1,0:T(8,128)S(1)}) custom-call(s32[2]{0:T(128)S(1)} %pad_add_fusion.odd_ref, f32[4224,1,128]{2,1,0:T(1,128)} %all-to-all-done.got_ref, f32[6656,128]{1,0:T(8,128)S(1)} %bitcast.16, ...), custom_call_target="tpu_custom_call" | custom-call | tf_op jit(solution)/shard_map/pallas_call | solution.py:216
  65.2 0.2 collective-permute-start.2
  65.4 8.0 %collective-permute-start.3 = (f32[2,104,512]{2,1,0:T(8,128)S(1)}, f32[2,104,512]{2,1,0:T(8,128)S(1)}, u32[]{:S(2)}, u32[]{:S(2)}) collective-permute-start(f32[2,104,512]{2,1,0:T(8,128)S(1)} %get-tuple-element.22), channel_id=1, source_target_pairs={{4,8},{8,4},{12,16},{16,12},{20,24},{24,20},{28,32},{32,28},{36,40... | collective-permute-start | bytes 1277960 | tf_op jit(solution)/shard_map/ppermute | solution.py:439
  73.3 0.1 collective-permute-start
  73.4 2.0 %collective-permute-start.1 = (f32[104,128]{1,0:T(8,128)S(1)}, f32[104,128]{1,0:T(8,128)S(1)}, u32[]{:S(2)}, u32[]{:S(2)}) collective-permute-start(f32[104,128]{1,0:T(8,128)S(1)} %get-tuple-element.19), channel_id=1, source_target_pairs={{0,3},{1,2},{2,1},{3,0},{4,7},{5,6},{6,5},{7,4},{8,11},{9,10},{10,... | collective-permute-start | bytes 159752 | tf_op jit(solution)/shard_map/ppermute | solution.py:437
  75.5 2.1 %collective-permute-done.pair_ref = f32[104,128]{1,0:T(8,128)S(1)} collective-permute-done((f32[104,128]{1,0:T(8,128)S(1)}, f32[104,128]{1,0:T(8,128)S(1)}, u32[]{:S(2)}, u32[]{:S(2)}) %collective-permute-start) | collective-permute-done | bytes 53280 | tf_op jit(solution)/shard_map/ppermute | solution.py:438
  77.6 1.5 %collective-permute-done.1.other_ref = f32[104,128]{1,0:T(8,128)S(1)} collective-permute-done((f32[104,128]{1,0:T(8,128)S(1)}, f32[104,128]{1,0:T(8,128)S(1)}, u32[]{:S(2)}, u32[]{:S(2)}) %collective-permute-start.1) | collective-permute-done | bytes 53280 | tf_op jit(solution)/shard_map/ppermute | solution.py:437
  79.1 5.6 %shard_map.75 = (f32[2,8,104,512]{3,2,1,0:T(8,128)S(1)}, f32[104,128]{1,0:T(8,128)S(1)}, f32[104,128]{1,0:T(8,128)S(1)}) custom-call(s32[2]{0:T(128)S(1)} %pad_add_fusion.odd_ref, f32[104,128]{1,0:T(8,128)S(1)} %collective-permute-done.pair_ref, f32[104,128]{1,0:T(8,128)S(1)} %collective-permute-done.1.other_ref, ...), custom_call_target="tpu_custom_call" | custom-call | flops 3000000000 | bytes 6000000 | tf_op jit(solution)/shard_map/pallas_call | solution.py:334
  84.7 2.0 %shard_map.76 = (f32[2,8,104,512]{3,2,1,0:T(8,128)S(1)}, f32[2,104,512]{2,1,0:T(8,128)S(1)}, f32[2,104,512]{2,1,0:T(8,128)S(1)}, f32[104,128]{1,0:T(8,128)S(1)}, f32[104,128]{1,0:T(8,128)S(1)}) custom-call(s32[2]{0:T(128)S(1)} %pad_add_fusion.odd_ref, f32[104,128]{1,0:T(8,128)S(1)} %collective-permute-done.pair_ref, ...), custom_call_target="tpu_custom_call", output_to_operand_aliasing={{0}: (9, {})} | custom-call | flops 1000000000 | bytes 2000000 | tf_op jit(solution)/shard_map/pallas_call | solution.py:343
  86.7 0.1 collective-permute-start.6
  86.8 3.8 %collective-permute-start.7 = (f32[2,104,512]{2,1,0:T(8,128)S(1)}, f32[2,104,512]{2,1,0:T(8,128)S(1)}, u32[]{:S(2)}, u32[]{:S(2)}) collective-permute-start(f32[2,104,512]{2,1,0:T(8,128)S(1)} %get-tuple-element.30), channel_id=1, source_target_pairs={{4,8},{8,4},{12,16},{16,12},{20,24},{24,20},{28,32},{32,28},{36,40... | collective-permute-start | bytes 1277960 | tf_op jit(solution)/shard_map/ppermute | solution.py:439
  90.6 0.1 collective-permute-start.4
  90.7 0.3 collective-permute-start.5
  91.1 3.8 %collective-permute-done.4.pair_ref = f32[104,128]{1,0:T(8,128)S(1)} collective-permute-done((f32[104,128]{1,0:T(8,128)S(1)}, f32[104,128]{1,0:T(8,128)S(1)}, u32[]{:S(2)}, u32[]{:S(2)}) %collective-permute-start.4) | collective-permute-done | bytes 53280 | tf_op jit(solution)/shard_map/ppermute | solution.py:438
  94.9 1.3 %collective-permute-done.5.other_ref = f32[104,128]{1,0:T(8,128)S(1)} collective-permute-done((f32[104,128]{1,0:T(8,128)S(1)}, f32[104,128]{1,0:T(8,128)S(1)}, u32[]{:S(2)}, u32[]{:S(2)}) %collective-permute-start.5) | collective-permute-done | bytes 53280 | tf_op jit(solution)/shard_map/ppermute | solution.py:437
  96.2 4.0 %shard_map.77.part_ref = f32[2,100,8,512]{3,2,1,0:T(8,128)} custom-call(s32[2]{0:T(128)S(1)} %pad_add_fusion.odd_ref, f32[104,128]{1,0:T(8,128)S(1)} %collective-permute-done.4.pair_ref, f32[104,128]{1,0:T(8,128)S(1)} %collective-permute-done.5.other_ref, f32[2,8,104,512]{3,2,1,0:T(8,128)S(1)} %get-tuple-element.28.field, f32[4,8,100,512]{3,2,1,0:T(8,128)S(1)} %bitcast.15, ...), custom_call_target="tpu_custom_call" | custom-call | flops 3000000000 | bytes 6000000 | tf_op jit(solution)/shard_map/pallas_call | solution.py:401
  100.2 2.2 %shard_map.78 = f32[2,100,8,512]{3,2,1,0:T(8,128)} custom-call(s32[2]{0:T(128)S(1)} %pad_add_fusion.odd_ref, f32[104,128]{1,0:T(8,128)S(1)} %collective-permute-done.4.pair_ref, f32[104,128]{1,0:T(8,128)S(1)} %collective-permute-done.5.other_ref, f32[2,8,104,512]{3,2,1,0:T(8,128)S(1)} %get-tuple-element.28.field, ...), custom_call_target="tpu_custom_call", output_to_operand_aliasing={{}: (8, {})} | custom-call | flops 1000000000 | bytes 2000000 | tf_op jit(solution)/shard_map/pallas_call | solution.py:410
  (22 shorter events, 0.2 us)
Async XLA Ops:
  0.0 1.2 %copy-start.1 = (f32[2048,128]{1,0:T(8,128)S(1)}, f32[2048,128]{1,0:T(8,128)}, u32[]{:S(2)}) copy-start(f32[2048,128]{1,0:T(8,128)} %param.11) | copy-start | bytes 3145732
  1.2 0.7 copy-start.3
  1.9 0.7 copy-start.4
  2.6 18.5 %copy-start.6 = (f32[8,100,100]{2,0,1:T(8,128)S(1)}, f32[8,100,100]{2,0,1:T(8,128)}, u32[]{:S(2)}) copy-start(f32[8,100,100]{2,0,1:T(8,128)} %param.9) | copy-start | bytes 960004
  10.3 40.8 %all-to-all-start = ((f32[4224,1,128]{2,1,0:T(1,128)}), f32[4224,1,128]{2,1,0:T(1,128)}, u32[]{:S(2)}, u32[]{:S(2)}) async-start(f32[4224,1,128]{2,1,0:T(1,128)} %shard_map.73), calls=%async_computation | async-start | bytes 4325376 | tf_op jit(solution)/shard_map/all_to_all | solution.py:451
  40.2 2.1 %copy-start.5 = (f32[8,100,100]{1,2,0:T(8,128)S(1)}, f32[8,100,100]{1,2,0:T(8,128)}, u32[]{:S(2)}) copy-start(f32[8,100,100]{1,2,0:T(8,128)} %copy.18) | copy-start | bytes 960004
  42.4 36.7 %slice-start = ((s8[6815744]{0:T(1024)(128)(4,1)}), s8[2621440]{0:T(1024)(128)(4,1)S(1)}, s32[]{:S(2)}) async-start(s8[6815744]{0:T(1024)(128)(4,1)} %bitcast.14), calls=%async_computation.1 | async-start | bytes 5242880
  51.1 2.0 %copy-start = (f32[16,4,104,128]{3,2,1,0:T(8,128)S(1)}, f32[16,4,104,128]{3,2,1,0:T(8,128)}, u32[]{:S(2)}) copy-start(f32[16,4,104,128]{3,2,1,0:T(8,128)} %pad.11.clone) | copy-start | bytes 10223620
  53.0 26.1 %slice-start.1 = ((s8[6815744]{0:T(1024)(128)(4,1)}), s8[4194304]{0:T(1024)(128)(4,1)S(1)}, s32[]{:S(2)}) async-start(s8[6815744]{0:T(1024)(128)(4,1)} %bitcast.14), calls=%async_computation.2 | async-start | bytes 8388608
  53.0 26.1 %copy-start.2 = (s32[8,512]{1,0:T(8,128)S(1)}, s32[8,512]{1,0:T(8,128)}, u32[]{:S(2)}) copy-start(s32[8,512]{1,0:T(8,128)} %mask_ref.7) | copy-start | bytes 49156
  65.2 19.5 %collective-permute-start.2 = (f32[2,104,512]{2,1,0:T(8,128)S(1)}, f32[2,104,512]{2,1,0:T(8,128)S(1)}, u32[]{:S(2)}, u32[]{:S(2)}) collective-permute-start(f32[2,104,512]{2,1,0:T(8,128)S(1)} %get-tuple-element.21), channel_id=1, source_target_pairs={{0,4},{4,0},{8,12},{12,8},{16,20},{20,16},{24,28},{28,24},{32,36},... | collective-permute-start | bytes 1277960 | tf_op jit(solution)/shard_map/ppermute | solution.py:440
  65.4 19.3 %collective-permute-start.3 = (f32[2,104,512]{2,1,0:T(8,128)S(1)}, f32[2,104,512]{2,1,0:T(8,128)S(1)}, u32[]{:S(2)}, u32[]{:S(2)}) collective-permute-start(f32[2,104,512]{2,1,0:T(8,128)S(1)} %get-tuple-element.22), channel_id=1, source_target_pairs={{4,8},{8,4},{12,16},{16,12},{20,24},{24,20},{28,32},{32,28},{36,40... | collective-permute-start | bytes 1277960 | tf_op jit(solution)/shard_map/ppermute | solution.py:439
  73.3 4.2 %collective-permute-start = (f32[104,128]{1,0:T(8,128)S(1)}, f32[104,128]{1,0:T(8,128)S(1)}, u32[]{:S(2)}, u32[]{:S(2)}) collective-permute-start(f32[104,128]{1,0:T(8,128)S(1)} %get-tuple-element.18), channel_id=1, source_target_pairs={{0,1},{1,0},{2,3},{3,2},{4,5},{5,4},{6,7},{7,6},{8,9},{9,8},{10,11... | collective-permute-start | bytes 159752 | tf_op jit(solution)/shard_map/ppermute | solution.py:438
  73.4 5.6 %collective-permute-start.1 = (f32[104,128]{1,0:T(8,128)S(1)}, f32[104,128]{1,0:T(8,128)S(1)}, u32[]{:S(2)}, u32[]{:S(2)}) collective-permute-start(f32[104,128]{1,0:T(8,128)S(1)} %get-tuple-element.19), channel_id=1, source_target_pairs={{0,3},{1,2},{2,1},{3,0},{4,7},{5,6},{6,5},{7,4},{8,11},{9,10},{10,... | collective-permute-start | bytes 159752 | tf_op jit(solution)/shard_map/ppermute | solution.py:437
  86.7 13.5 %collective-permute-start.6 = (f32[2,104,512]{2,1,0:T(8,128)S(1)}, f32[2,104,512]{2,1,0:T(8,128)S(1)}, u32[]{:S(2)}, u32[]{:S(2)}) collective-permute-start(f32[2,104,512]{2,1,0:T(8,128)S(1)} %get-tuple-element.29), channel_id=1, source_target_pairs={{0,4},{4,0},{8,12},{12,8},{16,20},{20,16},{24,28},{28,24},{32,36},... | collective-permute-start | bytes 1277960 | tf_op jit(solution)/shard_map/ppermute | solution.py:440
  86.8 13.4 %collective-permute-start.7 = (f32[2,104,512]{2,1,0:T(8,128)S(1)}, f32[2,104,512]{2,1,0:T(8,128)S(1)}, u32[]{:S(2)}, u32[]{:S(2)}) collective-permute-start(f32[2,104,512]{2,1,0:T(8,128)S(1)} %get-tuple-element.30), channel_id=1, source_target_pairs={{4,8},{8,4},{12,16},{16,12},{20,24},{24,20},{28,32},{32,28},{36,40... | collective-permute-start | bytes 1277960 | tf_op jit(solution)/shard_map/ppermute | solution.py:439
  90.6 4.2 %collective-permute-start.4 = (f32[104,128]{1,0:T(8,128)S(1)}, f32[104,128]{1,0:T(8,128)S(1)}, u32[]{:S(2)}, u32[]{:S(2)}) collective-permute-start(f32[104,128]{1,0:T(8,128)S(1)} %get-tuple-element.26), channel_id=1, source_target_pairs={{0,1},{1,0},{2,3},{3,2},{4,5},{5,4},{6,7},{7,6},{8,9},{9,8},{10,11... | collective-permute-start | bytes 159752 | tf_op jit(solution)/shard_map/ppermute | solution.py:438
  90.7 5.4 %collective-permute-start.5 = (f32[104,128]{1,0:T(8,128)S(1)}, f32[104,128]{1,0:T(8,128)S(1)}, u32[]{:S(2)}, u32[]{:S(2)}) collective-permute-start(f32[104,128]{1,0:T(8,128)S(1)} %get-tuple-element.27), channel_id=1, source_target_pairs={{0,3},{1,2},{2,1},{3,0},{4,7},{5,6},{6,5},{7,4},{8,11},{9,10},{10,... | collective-permute-start | bytes 159752 | tf_op jit(solution)/shard_map/ppermute | solution.py:437
where the time goes:
time: 103 us
  Pallas kernels  33.6 us (33%)
  local copies, waits for them, and re-layouts  25.7 us (25%)
  starting transfers between devices  25.5 us (25%)
  waiting for transfers between devices  17 us (17%)
    unnamed x22, local copies, waits for them, and re-layouts  21.3 us
    pallas_call x1, Pallas kernels, start(): pl.pallas_call(functools.partial(start_kernel, (tracers, rows, high, colu...  12.1 us
    ppermute x2, starting transfers between devices, exchange(): far = lax.ppermute(far, 'lat', next_pair)  11.8 us
    all_to_all x1, starting transfers between devices, local(): lax.all_to_all(send, ('lat', 'lon'), split_axis=0, concat_axis=0, tiled=T...  10.9 us
    all_to_all x1, waiting for transfers between devices, local(): lax.all_to_all(send, ('lat', 'lon'), split_axis=0, concat_axis=0, tiled=T...  8.24 us
    pallas_call x1, Pallas kernels, pack(): pl.pallas_call(functools.partial(pack_kernel, (levels, high, columns, dev...  7.63 us
    ppermute x2, waiting for transfers between devices, exchange(): pair = lax.ppermute(pair, 'lon', [(i, i ^ 1) for i in range(lon)])  5.9 us
    pallas_call x1, Pallas kernels, step(): pl.pallas_call(functools.partial(inner_kernel, levels), out_shape=(field_...  5.56 us
  transfers between devices with their start and end apart: 9, of which 5 were waited for; matrix products, arithmetic and copies ran while one was open for 21% of the time, Pallas kernels for 9%

commit v1 on v0

--- a/solution.py
+++ b/solution.py
@@ -80,7 +80,7 @@
         send_ref[o * SLOTS + 32] = pay[o : o + 1, :]
     get_values.wait()
     copy.wait()
-    unroll = 32
+    unroll = 64
     for i in range(chunks):
 
         @pl.loop(0, LANES // unroll)
@@ -107,7 +107,7 @@
             pltpu.VMEM((LANES, LANES), jnp.float32),
             pltpu.SemaphoreType.DMA((4,)),
         ],
-        compiler_params=pltpu.CompilerParams(vmem_limit_bytes=12 * MIB),
+        compiler_params=pltpu.CompilerParams(vmem_limit_bytes=60 * MIB),
     )(owner.reshape(chunks, LANES), cell.reshape(chunks, LANES), values.reshape(rows, 1, LANES))
 
 
@@ -119,39 +119,81 @@
     return product[:high] + product[high:]
 
 
-def keep_ends(row, first, last, west, east):
-    lane = lax.broadcasted_iota(jnp.int32, first.shape, 1)
-    west[...] = jnp.where(lane == row, pltpu.roll(first, row, 1), west[...])
-    east[...] = jnp.where(lane == row, pltpu.roll(last, (row + 1) % LANES, 1), east[...])
-
-
-def hand_out(odd_ref, field, west, east, near_ref, far_ref, pair_ref, other_ref):
+def collect_ends(rows_done, field, before):
+    tracers, rows, high, wide = field.shape
+    lane = lax.broadcasted_iota(jnp.int32, (8, LANES), 1)
+    for at in range(0, high, 8):
+        strip = slice(at, at + 8)
+        west, east = before(strip)
+        for t in range(tracers):
+            for j in rows_done:
+                row = t * rows + j
+                first = pltpu.roll(field[t, j, strip, :LANES], row, 1)
+                last = pltpu.roll(field[t, j, strip, wide - LANES :], (row + 1) % LANES, 1)
+                west = jnp.where(lane == row, first, west)
+                east = jnp.where(lane == row, last, east)
+        yield strip, west, east
+
+
+def no_ends(strip):
+    return jnp.zeros((8, LANES), jnp.float32), jnp.zeros((8, LANES), jnp.float32)
+
+
+def hand_out(odd_ref, field, rows_done, before, near_ref, far_ref, pair_ref, other_ref):
+    odd_lon = odd_ref[1] != 0
+    for strip, west, east in collect_ends(rows_done, field, before):
+        pair_ref[strip, :] = jnp.where(odd_lon, west, east)
+        other_ref[strip, :] = jnp.where(odd_lon, east, west)
     last = field.shape[1] - 1
-    for axis, (low, top, mine, others) in enumerate((
-        (field.at[:, 0], field.at[:, last], near_ref, far_ref),
-        (west, east, pair_ref, other_ref),
-    )):
-        odd = odd_ref[axis]
-
-        @pl.when(odd == 0)
-        def _():
-            mine[...] = top[...]
-            others[...] = low[...]
-
-        @pl.when(odd != 0)
-        def _():
-            mine[...] = low[...]
-            others[...] = top[...]
-
-
-def start_kernel(geometry, odd_ref, got_ref, base_hbm, weight_hbm, courant_ref,
-                 out_ref, near_ref, far_ref, pair_ref, other_ref, *scratch):
-    tracers, rows, high, columns, devices = geometry
-    banks, addr_v, addr_s, base_ref, weight_ref, west, east, sems = scratch[:BANKS], *scratch[BANKS:]
-    get_base = pltpu.make_async_copy(base_hbm, base_ref, sems.at[1])
+    odd = odd_ref[0]
+
+    @pl.when(odd == 0)
+    def _():
+        near_ref[...] = field[:, last]
+        far_ref[...] = field[:, 0]
+
+    @pl.when(odd != 0)
+    def _():
+        near_ref[...] = field[:, 0]
+        far_ref[...] = field[:, last]
+
+
+def prepare_kernel(terminal_in, courant_in, terminal_out, courant_out, sems):
+    copies = []
+    for source, target in ((terminal_in, terminal_out), (courant_in, courant_out)):
+        parts, rows = target.shape[:2]
+        for part in range(parts):
+            for j in range(rows):
+                copies.append(
+                    pltpu.make_async_copy(source.at[part, :, j, :], target.at[part, j], sems.at[len(copies)])
+                )
+                copies[-1].start()
+    for copy in copies:
+        copy.wait()
+
+
+def prepare(terminal, courant):
+    rows = terminal.shape[1]
+    return pl.pallas_call(
+        prepare_kernel,
+        out_shape=tuple(jax.ShapeDtypeStruct(x.shape, x.dtype) for x in (terminal, courant)),
+        in_specs=[HBM] * 2,
+        out_specs=(HBM,) * 2,
+        scratch_shapes=[pltpu.SemaphoreType.DMA(((terminal.shape[0] + courant.shape[0]) * rows,))],
+        compiler_params=pltpu.CompilerParams(vmem_limit_bytes=60 * MIB),
+    )(jnp.swapaxes(terminal, 1, 2), jnp.swapaxes(courant, 1, 2))
+
+
+def start_kernel(devices, odd_ref, got_ref, weight_hbm, terminal_hbm, out_ref, near_ref, far_ref, pair_ref, other_ref,
+                 terminal_ref, weight_ref, addr_v, addr_s, state, sems, *banks):
+    tracers, rows, levels, wide = terminal_ref.shape
+    columns = wide // LANES
+    get_terminal = pltpu.make_async_copy(terminal_hbm, terminal_ref, sems.at[1])
     get_weight = pltpu.make_async_copy(weight_hbm, weight_ref, sems.at[2])
-    get_base.start()
+    get_terminal.start()
     get_weight.start()
+    high = state.shape[1]
+    whole = levels // 8 * 8
     for o in range(devices):
         addr_v[o : o + 1, :] = got_ref[o * SLOTS + 32].astype(jnp.int32)
     copy = pltpu.make_async_copy(addr_v, addr_s, sems.at[0])
@@ -163,8 +205,6 @@
         def _(i):
             bank[pl.ds(pl.multiple_of(i * clear, clear), clear), :] = jnp.zeros((clear, LANES), jnp.float32)
 
-    west[...] = jnp.zeros_like(west)
-    east[...] = jnp.zeros_like(east)
     copy.wait()
 
     @pl.loop(0, devices // BANKS)
@@ -181,26 +221,25 @@
                     place = addr_s[first + b, c * 4 + u]
                     bank[pl.ds(place, 1), :] += got_ref[(first + b) * SLOTS + c * 4 + u]
 
-    get_base.wait()
+    for slot in range(state.shape[0]):
+        state[slot, levels:high, :] = jnp.zeros((high - levels, wide), jnp.float32)
+    get_terminal.wait()
     get_weight.wait()
     for j in range(rows):
         weight = weight_ref[j]
         for t in range(tracers):
-            row = t * rows + j
-            done = []
-            for half in range(columns // 2):
-                pieces = []
-                for c in (2 * half, 2 * half + 1):
-                    at = (row * columns + c) * high
-                    piece = base_ref[at : at + high, :]
+            slot = (j * tracers + t) % state.shape[0]
+            for c in range(columns):
+                tile = slice(c * LANES, (c + 1) * LANES)
+                base = ((t * rows + j) * columns + c) * high
+                for low, top in ((0, whole), (whole, levels)):
+                    total = terminal_ref[t, j, low:top, tile]
                     for bank in banks:
-                        piece = piece + bank[at : at + high, :]
-                    pieces.append(piece)
-                level = vertical(weight, jnp.concatenate(pieces, axis=1))
-                out_ref[t, j, :, half * 2 * LANES : (half + 1) * 2 * LANES] = level
-                done.append(level)
-            keep_ends(row, done[0][:, :LANES], done[-1][:, LANES:], west, east)
-    hand_out(odd_ref, out_ref, west, east, near_ref, far_ref, pair_ref, other_ref)
+                        total = total + bank[base + low : base + top, :]
+                    state[slot, low:top, tile] = total
+            for at in range(0, wide, 2 * LANES):
+                out_ref[t, j, :, at : at + 2 * LANES] = vertical(weight, state[slot, :, at : at + 2 * LANES])
+    hand_out(odd_ref, out_ref, range(rows), no_ends, near_ref, far_ref, pair_ref, other_ref)
 
 
 def shapes_of(tracers, rows, high, wide):
@@ -210,26 +249,26 @@
     return jax.ShapeDtypeStruct((tracers, rows, high, wide), f32), edge, edge, end, end
 
 
-def start(odd, got, base, weight, courant, tracers, rows, high, columns, devices):
+def start(odd, got, weight, terminal, high, devices):
     f32 = jnp.float32
-    places = tracers * rows * columns * high
+    tracers, rows, levels, wide = terminal.shape
+    places = tracers * rows * (wide // LANES) * high
     return pl.pallas_call(
-        functools.partial(start_kernel, (tracers, rows, high, columns, devices)),
-        out_shape=shapes_of(tracers, rows, high, columns * LANES),
-        in_specs=[SMEM, VMEM, HBM, HBM, VMEM],
+        functools.partial(start_kernel, devices),
+        out_shape=shapes_of(tracers, rows, high, wide),
+        in_specs=[SMEM, VMEM, HBM, HBM],
         out_specs=(VMEM,) * 5,
-        scratch_shapes=[pltpu.VMEM((places + 64, LANES), f32) for _ in range(BANKS)]
-        + [
+        scratch_shapes=[
+            pltpu.VMEM(terminal.shape, f32),
+            pltpu.VMEM(weight.shape, weight.dtype),
             pltpu.VMEM((devices, LANES), jnp.int32),
             pltpu.SMEM((devices, LANES), jnp.int32),
-            pltpu.VMEM(base.shape, f32),
-            pltpu.VMEM(weight.shape, weight.dtype),
-            pltpu.VMEM((high, LANES), f32),
-            pltpu.VMEM((high, LANES), f32),
+            pltpu.VMEM((2, high, wide), f32),
             pltpu.SemaphoreType.DMA((3,)),
-        ],
-        compiler_params=pltpu.CompilerParams(vmem_limit_bytes=40 * MIB),
-    )(odd, got, base, weight, courant)
+        ]
+        + [pltpu.VMEM((places + 64, LANES), f32) for _ in range(BANKS)],
+        compiler_params=pltpu.CompilerParams(vmem_limit_bytes=32 * MIB),
+    )(odd, got, weight, terminal)
 
 
 def ends_in_place(odd_ref, pair_ref, other_ref, west, east):
@@ -280,7 +319,7 @@
     return north, south
 
 
-def advance(rows_done, levels, lat, field, courant_ref, mask_ref, hw, he, weight_ref, out_ref, west, east, state):
+def advance(rows_done, levels, lat, field, courant_ref, mask_ref, hw, he, weight_ref, out_ref, state):
     tracers, rows, high, wide = field.shape
     for slot in range(state.shape[0]):
         state[slot, levels:high, :] = jnp.zeros((high - levels, wide), jnp.float32)
@@ -294,32 +333,29 @@
                 state[slot, strip, tile] = value
 
             transported(t, j, levels, field, courant_ref, mask, lat, hw, he, store)
-            done = []
             for at in range(0, wide, 2 * LANES):
                 level = vertical(weight, state[slot, :, at : at + 2 * LANES])
                 out_ref[t, j, :, at : at + 2 * LANES] = level
-                done.append(level)
-            keep_ends(t * rows + j, done[0][:, :LANES], done[-1][:, LANES:], west, east)
 
 
 def inner_kernel(levels, odd_ref, pair_ref, other_ref, field, courant_ref, mask_ref, weight_ref,
                  out_ref, west, east, hw, he, state):
     ends_in_place(odd_ref, pair_ref, other_ref, hw, he)
-    west[...] = jnp.zeros_like(west)
-    east[...] = jnp.zeros_like(east)
-    rows = field.shape[1]
-    advance(range(1, rows - 1), levels, None, field, courant_ref, mask_ref, hw, he, weight_ref, out_ref, west, east, state)
+    rows_done = range(1, field.shape[1] - 1)
+    advance(rows_done, levels, None, field, courant_ref, mask_ref, hw, he, weight_ref, out_ref, state)
+    for strip, first, last in collect_ends(rows_done, out_ref, no_ends):
+        west[strip, :] = first
+        east[strip, :] = last
 
 
 def edge_kernel(levels, odd_ref, pair_ref, other_ref, field, courant_ref, mask_ref, weight_ref, near_in, far_in,
-                part_ref, west_in, east_in, out_ref, near_ref, far_ref, pair_out, other_out, hw, he, west, east, state):
+                part_ref, west, east, out_ref, near_ref, far_ref, pair_out, other_out, hw, he, state):
     ends_in_place(odd_ref, pair_ref, other_ref, hw, he)
-    west[...] = west_in[...]
-    east[...] = east_in[...]
-    rows = field.shape[1]
+    rows_done = (0, field.shape[1] - 1)
     lat = by_side(odd_ref, near_in, far_in)
-    advance((0, rows - 1), levels, lat, field, courant_ref, mask_ref, hw, he, weight_ref, out_ref, west, east, state)
-    hand_out(odd_ref, out_ref, west, east, near_ref, far_ref, pair_out, other_out)
+    advance(rows_done, levels, lat, field, courant_ref, mask_ref, hw, he, weight_ref, out_ref, state)
+    before = lambda strip: (west[strip, :], east[strip, :])
+    hand_out(odd_ref, out_ref, rows_done, before, near_ref, far_ref, pair_out, other_out)
 
 
 def step(levels, odd, field, courant, mask, weight, halos):
@@ -329,8 +365,8 @@
     field_shape, edge, _, end, _ = shapes_of(tracers, rows, high, wide)
     ends = [pltpu.VMEM((high, LANES), f32)] * 2
     state = [pltpu.VMEM((2, high, wide), f32)]
-    params = pltpu.CompilerParams(vmem_limit_bytes=20 * MIB)
-    cost = lambda n: pl.CostEstimate(flops=n * 500_000_000, bytes_accessed=n * 1_000_000, transcendentals=0)
+    params = pltpu.CompilerParams(vmem_limit_bytes=24 * MIB)
+    cost = lambda n: pl.CostEstimate(flops=n * 5_000_000_000, bytes_accessed=n * 1_000_000, transcendentals=0)
     part, west, east = pl.pallas_call(
         functools.partial(inner_kernel, levels),
         out_shape=(field_shape, end, end),
@@ -345,7 +381,7 @@
         out_shape=(field_shape, edge, edge, end, end),
         in_specs=[SMEM] + [VMEM] * 11,
         out_specs=(VMEM,) * 5,
-        scratch_shapes=ends + ends + state,
+        scratch_shapes=ends + state,
         input_output_aliases={9: 0},
         compiler_params=params,
         cost_estimate=cost(2),
@@ -396,8 +432,8 @@
         pltpu.SemaphoreType.DMA((slots,)),
     ]
     shape = jax.ShapeDtypeStruct((tracers, levels, rows, wide), f32)
-    params = pltpu.CompilerParams(vmem_limit_bytes=20 * MIB)
-    cost = lambda n: pl.CostEstimate(flops=n * 500_000_000, bytes_accessed=n * 1_000_000, transcendentals=0)
+    params = pltpu.CompilerParams(vmem_limit_bytes=24 * MIB)
+    cost = lambda n: pl.CostEstimate(flops=n * 5_000_000_000, bytes_accessed=n * 1_000_000, transcendentals=0)
     part = pl.pallas_call(
         functools.partial(final_inner_kernel, levels),
         out_shape=shape,
@@ -445,15 +481,12 @@
     devices = lax.axis_size("lat") * lax.axis_size("lon")
     tracers, rows, levels, wide = terminal.shape
     high = padded_levels(levels)
-    columns = wide // LANES
     odd = jnp.stack([lax.axis_index("lat") % 2, lax.axis_index("lon") % 2]).astype(jnp.int32)
-    send = pack(obs_owner, obs_cell, obs_values, levels, high, columns, devices)
+    send = pack(obs_owner, obs_cell, obs_values, levels, high, wide // LANES, devices)
     got = lax.all_to_all(send, ("lat", "lon"), split_axis=0, concat_axis=0, tiled=True)
-    base = terminal.reshape(tracers * rows, levels, columns, LANES)
-    base = jnp.pad(jnp.swapaxes(base, 1, 2), ((0, 0), (0, 0), (0, high - levels), (0, 0)))
-    base = base.reshape(tracers * rows * columns * high, LANES)
+    terminal, courant = prepare(terminal, courant)
     weight = weights(inverse, high)
-    field, *edges = start(odd, got, base, weight, courant, tracers, rows, high, columns, devices)
+    field, *edges = start(odd, got, weight, terminal, high, devices)
     for _ in range(STEPS - 1):
         field, *edges = step(levels, odd, field, courant, land_mask, weight, exchange(*edges))
     out = last_step(levels, odd, field, courant, land_mask, exchange(*edges))

time: 103 us -> 367 us (3.56)
  Pallas kernels: 33.6 us -> 332 us
  local copies, waits for them, and re-layouts: 25.7 us -> 5.17 us
  waiting for transfers between devices: 17 us -> 2.73 us
    pallas_call x1 -> x2, Pallas kernels: 12.1 us -> 313 us  [the longest x1 299 us: prepare(): pl.pallas_call(prepare_kernel, out_shape=tuple((jax.ShapeDtypeStruct(x.sh...]
    unnamed x22 -> x9, local copies, waits for them, and re-layouts: 21.3 us -> 5.13 us
    all_to_all x1, waiting for transfers between devices: 8.24 us -> 0.01 us  [local(): lax.all_to_all(send, ('lat', 'lon'), split_axis=0, concat_axis=0, tiled=T...]
    ppermute x2, waiting for transfers between devices: 5.9 us -> 0.01 us  [exchange(): pair = lax.ppermute(pair, 'lon', [(i, i ^ 1) for i in range(lon)])]
  transfers between devices with their start and end apart: 9 -> 9, of which waited for: 5 -> 1; matrix products, arithmetic and copies ran while one was open for 21% -> 0% of each run, Pallas kernels for 9% -> 84%
where the time goes in v1:
time: 367 us; the launch traced here: 366 us
  Pallas kernels  332 us (90%)
  starting transfers between devices  25.4 us (7%)
  local copies, waits for them, and re-layouts  5.17 us (1%)
    pallas_call x1, Pallas kernels, prepare(): pl.pallas_call(prepare_kernel, out_shape=tuple((jax.ShapeDtypeStruct(x.sh...  299 us
    pallas_call x1, Pallas kernels, start(): pl.pallas_call(functools.partial(start_kernel, devices), out_shape=shapes...  13.5 us
    ppermute x2, starting transfers between devices, exchange(): far = lax.ppermute(far, 'lat', next_pair)  11 us
    all_to_all x1, starting transfers between devices, local(): lax.all_to_all(send, ('lat', 'lon'), split_axis=0, concat_axis=0, tiled=T...  10.5 us
    pallas_call x1, Pallas kernels, pack(): pl.pallas_call(functools.partial(pack_kernel, (levels, high, columns, dev...  8.13 us
  transfers between devices with their start and end apart: 9, of which 1 were waited for; matrix products, arithmetic and copies ran while one was open for 0% of the time, Pallas kernels for 84%

profile of v1, /device:TPU:8, one launch (start us, length us, event | category | flops | bytes accessed | tf_op | source)
XLA Modules:
  0.0 366.3 jit_solution(2362480385093243332)
XLA Ops:
  0.0 8.1 %shard_map.73 = f32[4224,1,128]{2,1,0:T(1,128)} custom-call(s32[16,128]{1,0:T(8,128)} %bitcast.14, s32[16,128]{1,0:T(8,128)} %bitcast.15, f32[2048,1,128]{2,1,0:T(1,128)} %bitcast.13), custom_call_target="tpu_custom_call" | custom-call | tf_op jit(solution)/shard_map/pallas_call | solution.py:96
  8.1 10.5 %all-to-all-start = ((f32[4224,1,128]{2,1,0:T(1,128)}), f32[4224,1,128]{2,1,0:T(1,128)S(1)}, u32[]{:S(2)}, u32[]{:S(2)}) async-start(f32[4224,1,128]{2,1,0:T(1,128)} %shard_map.73), calls=%async_computation | async-start | bytes 4325376 | tf_op jit(solution)/shard_map/all_to_all | solution.py:486
  18.6 0.2 copy.10
  18.9 299.3 %shard_map.74 = (f32[2,8,100,512]{3,2,1,0:T(8,128)}, f32[4,8,100,512]{3,2,1,0:T(8,128)}) custom-call(f32[2,100,8,512]{3,2,1,0:T(8,128)} %bitcast.12, f32[4,100,8,512]{3,2,1,0:T(8,128)} %bitcast.10), custom_call_target="tpu_custom_call" | custom-call | tf_op jit(solution)/shard_map/pallas_call | solution.py:177
  318.2 0.1 pad_add_fusion.odd_ref
  318.4 0.1 subtract_convert_fusion
  318.4 0.0 copy-start.2
  318.5 0.4 maximum_maximum_fusion.weight_hbm.weight_ref
  318.8 0.0 all-to-all-done.got_ref
  318.9 2.0 copy-done
  320.8 13.5 %shard_map.75 = (f32[2,8,104,512]{3,2,1,0:T(8,128)S(1)}, f32[2,104,512]{2,1,0:T(8,128)S(1)}, f32[2,104,512]{2,1,0:T(8,128)S(1)}, f32[104,128]{1,0:T(8,128)S(1)}, f32[104,128]{1,0:T(8,128)S(1)}) custom-call(s32[2]{0:T(128)S(1)} %pad_add_fusion.odd_ref, f32[4224,1,128]{2,1,0:T(1,128)S(1)} %all-to-all-done.got_ref, ...), custom_call_target="tpu_custom_call" | custom-call | tf_op jit(solution)/shard_map/pallas_call | solution.py:256
  334.3 0.5 collective-permute-start
  334.8 1.2 collective-permute-start.1
  336.1 0.0 collective-permute-start.2
  336.1 6.1 %collective-permute-start.3 = (f32[2,104,512]{2,1,0:T(8,128)S(1)}, f32[2,104,512]{2,1,0:T(8,128)S(1)}, u32[]{:S(2)}, u32[]{:S(2)}) collective-permute-start(f32[2,104,512]{2,1,0:T(8,128)S(1)} %get-tuple-element.26), channel_id=1, source_target_pairs={{4,8},{8,4},{12,16},{16,12},{20,24},{24,20},{28,32},{32,28},{36,40... | collective-permute-start | bytes 1277960 | tf_op jit(solution)/shard_map/ppermute | solution.py:475
  342.2 0.0 collective-permute-done.pair_ref
  342.2 0.0 collective-permute-done.1.other_ref
  342.2 2.9 copy-done.1
  345.1 3.3 shard_map.76
  348.5 0.0 collective-permute-done.2.near_in
  348.5 0.0 collective-permute-done.3.far_in
  348.5 1.7 shard_map.77
  350.2 0.7 collective-permute-start.4
  351.0 1.5 collective-permute-start.5
  352.4 0.0 collective-permute-start.6
  352.4 4.9 %collective-permute-start.7 = (f32[2,104,512]{2,1,0:T(8,128)S(1)}, f32[2,104,512]{2,1,0:T(8,128)S(1)}, u32[]{:S(2)}, u32[]{:S(2)}) collective-permute-start(f32[2,104,512]{2,1,0:T(8,128)S(1)} %get-tuple-element.34), channel_id=1, source_target_pairs={{4,8},{8,4},{12,16},{16,12},{20,24},{24,20},{28,32},{32,28},{36,40... | collective-permute-start | bytes 1277960 | tf_op jit(solution)/shard_map/ppermute | solution.py:475
  357.4 0.0 collective-permute-done.4.pair_ref
  357.4 0.0 collective-permute-done.5.other_ref
  357.4 3.9 %shard_map.78.part_ref = f32[2,100,8,512]{3,2,1,0:T(8,128)} custom-call(s32[2]{0:T(128)S(1)} %pad_add_fusion.odd_ref, f32[104,128]{1,0:T(8,128)S(1)} %collective-permute-done.4.pair_ref, f32[104,128]{1,0:T(8,128)S(1)} %collective-permute-done.5.other_ref, f32[2,8,104,512]{3,2,1,0:T(8,128)S(1)} %get-tuple-element.32.field, f32[4,8,100,512]{3,2,1,0:T(8,128)S(1)} %copy-done.1, ...), custom_call_target="tpu_custom_call" | custom-call | flops 30000001024 | bytes 6000000 | tf_op jit(solution)/shard_map/pallas_call | solution.py:437
  361.3 0.0 collective-permute-done.6.near_in
  361.3 2.7 collective-permute-done.7.far_in
  364.0 2.2 shard_map.79
  (7 shorter events, 0.1 us)
Async XLA Ops:
  0.0 18.6 %copy-start.3 = (f32[8,100,100]{2,0,1:T(8,128)S(1)}, f32[8,100,100]{2,0,1:T(8,128)}, u32[]{:S(2)}) copy-start(f32[8,100,100]{2,0,1:T(8,128)} %param.9) | copy-start | bytes 960004
  8.1 310.7 %all-to-all-start = ((f32[4224,1,128]{2,1,0:T(1,128)}), f32[4224,1,128]{2,1,0:T(1,128)S(1)}, u32[]{:S(2)}, u32[]{:S(2)}) async-start(f32[4224,1,128]{2,1,0:T(1,128)} %shard_map.73), calls=%async_computation | async-start | bytes 4325376 | tf_op jit(solution)/shard_map/all_to_all | solution.py:486
  318.4 23.7 %copy-start.2 = (s32[8,512]{1,0:T(8,128)S(1)}, s32[8,512]{1,0:T(8,128)}, u32[]{:S(2)}) copy-start(s32[8,512]{1,0:T(8,128)} %mask_ref.7) | copy-start | bytes 49156
  318.9 2.0 copy-start
  334.3 7.8 %collective-permute-start = (f32[104,128]{1,0:T(8,128)S(1)}, f32[104,128]{1,0:T(8,128)S(1)}, u32[]{:S(2)}, u32[]{:S(2)}) collective-permute-start(f32[104,128]{1,0:T(8,128)S(1)} %get-tuple-element.21), channel_id=1, source_target_pairs={{0,1},{1,0},{2,3},{3,2},{4,5},{5,4},{6,7},{7,6},{8,9},{9,8},{10,11... | collective-permute-start | bytes 159752 | tf_op jit(solution)/shard_map/ppermute | solution.py:474
  334.8 7.3 %collective-permute-start.1 = (f32[104,128]{1,0:T(8,128)S(1)}, f32[104,128]{1,0:T(8,128)S(1)}, u32[]{:S(2)}, u32[]{:S(2)}) collective-permute-start(f32[104,128]{1,0:T(8,128)S(1)} %get-tuple-element.22), channel_id=1, source_target_pairs={{0,3},{1,2},{2,1},{3,0},{4,7},{5,6},{6,5},{7,4},{8,11},{9,10},{10,... | collective-permute-start | bytes 159752 | tf_op jit(solution)/shard_map/ppermute | solution.py:473
  336.1 12.4 %collective-permute-start.2 = (f32[2,104,512]{2,1,0:T(8,128)S(1)}, f32[2,104,512]{2,1,0:T(8,128)S(1)}, u32[]{:S(2)}, u32[]{:S(2)}) collective-permute-start(f32[2,104,512]{2,1,0:T(8,128)S(1)} %get-tuple-element.25), channel_id=1, source_target_pairs={{0,4},{4,0},{8,12},{12,8},{16,20},{20,16},{24,28},{28,24},{32,36},... | collective-permute-start | bytes 1277960 | tf_op jit(solution)/shard_map/ppermute | solution.py:476
  336.1 12.4 %collective-permute-start.3 = (f32[2,104,512]{2,1,0:T(8,128)S(1)}, f32[2,104,512]{2,1,0:T(8,128)S(1)}, u32[]{:S(2)}, u32[]{:S(2)}) collective-permute-start(f32[2,104,512]{2,1,0:T(8,128)S(1)} %get-tuple-element.26), channel_id=1, source_target_pairs={{4,8},{8,4},{12,16},{16,12},{20,24},{24,20},{28,32},{32,28},{36,40... | collective-permute-start | bytes 1277960 | tf_op jit(solution)/shard_map/ppermute | solution.py:475
  342.2 2.9 copy-start.1
  350.2 7.1 %collective-permute-start.4 = (f32[104,128]{1,0:T(8,128)S(1)}, f32[104,128]{1,0:T(8,128)S(1)}, u32[]{:S(2)}, u32[]{:S(2)}) collective-permute-start(f32[104,128]{1,0:T(8,128)S(1)} %get-tuple-element.30), channel_id=1, source_target_pairs={{0,1},{1,0},{2,3},{3,2},{4,5},{5,4},{6,7},{7,6},{8,9},{9,8},{10,11... | collective-permute-start | bytes 159752 | tf_op jit(solution)/shard_map/ppermute | solution.py:474
  351.0 6.4 %collective-permute-start.5 = (f32[104,128]{1,0:T(8,128)S(1)}, f32[104,128]{1,0:T(8,128)S(1)}, u32[]{:S(2)}, u32[]{:S(2)}) collective-permute-start(f32[104,128]{1,0:T(8,128)S(1)} %get-tuple-element.31), channel_id=1, source_target_pairs={{0,3},{1,2},{2,1},{3,0},{4,7},{5,6},{6,5},{7,4},{8,11},{9,10},{10,... | collective-permute-start | bytes 159752 | tf_op jit(solution)/shard_map/ppermute | solution.py:473
  352.4 8.8 %collective-permute-start.6 = (f32[2,104,512]{2,1,0:T(8,128)S(1)}, f32[2,104,512]{2,1,0:T(8,128)S(1)}, u32[]{:S(2)}, u32[]{:S(2)}) collective-permute-start(f32[2,104,512]{2,1,0:T(8,128)S(1)} %get-tuple-element.33), channel_id=1, source_target_pairs={{0,4},{4,0},{8,12},{12,8},{16,20},{20,16},{24,28},{28,24},{32,36},... | collective-permute-start | bytes 1277960 | tf_op jit(solution)/shard_map/ppermute | solution.py:476
  352.4 11.5 %collective-permute-start.7 = (f32[2,104,512]{2,1,0:T(8,128)S(1)}, f32[2,104,512]{2,1,0:T(8,128)S(1)}, u32[]{:S(2)}, u32[]{:S(2)}) collective-permute-start(f32[2,104,512]{2,1,0:T(8,128)S(1)} %get-tuple-element.34), channel_id=1, source_target_pairs={{4,8},{8,4},{12,16},{16,12},{20,24},{24,20},{28,32},{32,28},{36,40... | collective-permute-start | bytes 1277960 | tf_op jit(solution)/shard_map/ppermute | solution.py:475

commit v2 on v1

--- a/solution.py
+++ b/solution.py
@@ -18,6 +18,8 @@
     return -(-levels // 8) * 8
 
 
+SPARE = 10
+LIMIT = 36
 VMEM = pl.BlockSpec(memory_space=pltpu.VMEM)
 SMEM = pl.BlockSpec(memory_space=pltpu.SMEM)
 HBM = pl.BlockSpec(memory_space=pltpu.HBM)
@@ -158,37 +160,57 @@
         far_ref[...] = field[:, last]
 
 
-def prepare_kernel(terminal_in, courant_in, terminal_out, courant_out, sems):
-    copies = []
-    for source, target in ((terminal_in, terminal_out), (courant_in, courant_out)):
-        parts, rows = target.shape[:2]
-        for part in range(parts):
-            for j in range(rows):
-                copies.append(
-                    pltpu.make_async_copy(source.at[part, :, j, :], target.at[part, j], sems.at[len(copies)])
-                )
-                copies[-1].start()
-    for copy in copies:
-        copy.wait()
+def prepare_kernel(terminal_in, courant_in, out, stage, sems):
+    moves = []
+    for source in (terminal_in, courant_in):
+        for part in range(source.shape[0]):
+            at = len(moves) // out.shape[1]
+            for j in range(out.shape[1]):
+                sem = sems.at[len(moves)]
+                load = pltpu.make_async_copy(source.at[part, :, j, :], stage.at[at, j], sem)
+                moves.append((load, pltpu.make_async_copy(stage.at[at, j], out.at[at, j], sem)))
+                load.start()
+    for load, save in moves:
+        load.wait()
+        save.start()
+    for load, save in moves:
+        save.wait()
 
 
 def prepare(terminal, courant):
-    rows = terminal.shape[1]
+    _, rows, levels, wide = terminal.shape
+    parts = terminal.shape[0] + courant.shape[0]
     return pl.pallas_call(
         prepare_kernel,
-        out_shape=tuple(jax.ShapeDtypeStruct(x.shape, x.dtype) for x in (terminal, courant)),
+        out_shape=jax.ShapeDtypeStruct((parts + SPARE, rows, levels, wide), terminal.dtype),
         in_specs=[HBM] * 2,
-        out_specs=(HBM,) * 2,
-        scratch_shapes=[pltpu.SemaphoreType.DMA(((terminal.shape[0] + courant.shape[0]) * rows,))],
+        out_specs=HBM,
+        scratch_shapes=[
+            pltpu.VMEM((parts, rows, levels, wide), terminal.dtype),
+            pltpu.SemaphoreType.DMA((parts * rows,)),
+        ],
         compiler_params=pltpu.CompilerParams(vmem_limit_bytes=60 * MIB),
     )(jnp.swapaxes(terminal, 1, 2), jnp.swapaxes(courant, 1, 2))
 
 
-def start_kernel(devices, odd_ref, got_ref, weight_hbm, terminal_hbm, out_ref, near_ref, far_ref, pair_ref, other_ref,
+def courant_copies(tracers, inputs_hbm, target, sems, rows_done, first=0, spots=None):
+    spots = spots or rows_done
+    return {
+        j: [
+            pltpu.make_async_copy(
+                inputs_hbm.at[tracers + part, j], target.at[part, spot], sems.at[first + n * target.shape[0] + part]
+            )
+            for part in range(target.shape[0])
+        ]
+        for n, (j, spot) in enumerate(zip(rows_done, spots))
+    }
+
+
+def start_kernel(devices, odd_ref, got_ref, weight_hbm, inputs_hbm, out_ref, near_ref, far_ref, pair_ref, other_ref,
                  terminal_ref, weight_ref, addr_v, addr_s, state, sems, *banks):
     tracers, rows, levels, wide = terminal_ref.shape
     columns = wide // LANES
-    get_terminal = pltpu.make_async_copy(terminal_hbm, terminal_ref, sems.at[1])
+    get_terminal = pltpu.make_async_copy(inputs_hbm.at[pl.ds(0, terminal_ref.shape[0])], terminal_ref, sems.at[1])
     get_weight = pltpu.make_async_copy(weight_hbm, weight_ref, sems.at[2])
     get_terminal.start()
     get_weight.start()
@@ -249,9 +271,9 @@
     return jax.ShapeDtypeStruct((tracers, rows, high, wide), f32), edge, edge, end, end
 
 
-def start(odd, got, weight, terminal, high, devices):
+def start(odd, got, weight, inputs, tracers, high, devices):
     f32 = jnp.float32
-    tracers, rows, levels, wide = terminal.shape
+    _, rows, levels, wide = inputs.shape
     places = tracers * rows * (wide // LANES) * high
     return pl.pallas_call(
         functools.partial(start_kernel, devices),
@@ -259,7 +281,7 @@
         in_specs=[SMEM, VMEM, HBM, HBM],
         out_specs=(VMEM,) * 5,
         scratch_shapes=[
-            pltpu.VMEM(terminal.shape, f32),
+            pltpu.VMEM((tracers, rows, levels, wide), f32),
             pltpu.VMEM(weight.shape, weight.dtype),
             pltpu.VMEM((devices, LANES), jnp.int32),
             pltpu.SMEM((devices, LANES), jnp.int32),
@@ -267,8 +289,8 @@
             pltpu.SemaphoreType.DMA((3,)),
         ]
         + [pltpu.VMEM((places + 64, LANES), f32) for _ in range(BANKS)],
-        compiler_params=pltpu.CompilerParams(vmem_limit_bytes=32 * MIB),
-    )(odd, got, weight, terminal)
+        compiler_params=pltpu.CompilerParams(vmem_limit_bytes=36 * MIB),
+    )(odd, got, weight, inputs)
 
 
 def ends_in_place(odd_ref, pair_ref, other_ref, west, east):
@@ -278,7 +300,7 @@
     east[...] = jnp.where(odd, other, pair)
 
 
-def transported(t, j, levels, field, courant_ref, mask, lat, west, east, store):
+def transported(t, j, levels, field, courant, mask, lat, west, east, store):
     rows, wide = field.shape[1], field.shape[3]
     row = t * rows + j
     tiles = [slice(c * LANES, (c + 1) * LANES) for c in range(wide // LANES)]
@@ -299,10 +321,10 @@
             s = lat[1](t, strip, tile) if j == 0 else field[t, j - 1, strip, tile]
             moved = (
                 v
-                + courant_ref[0, j, strip, tile] * (e - v)
-                + courant_ref[1, j, strip, tile] * (w - v)
-                + courant_ref[2, j, strip, tile] * (n - v)
-                + courant_ref[3, j, strip, tile] * (s - v)
+                + courant(0, j, strip, tile) * (e - v)
+                + courant(1, j, strip, tile) * (w - v)
+                + courant(2, j, strip, tile) * (n - v)
+                + courant(3, j, strip, tile) * (s - v)
             )
             store(strip, tile, mask[c] * moved)
 
@@ -319,11 +341,12 @@
     return north, south
 
 
-def advance(rows_done, levels, lat, field, courant_ref, mask_ref, hw, he, weight_ref, out_ref, state):
+def advance(rows_done, levels, lat, field, courant, ready, mask_ref, hw, he, weight_ref, out_ref, state):
     tracers, rows, high, wide = field.shape
     for slot in range(state.shape[0]):
         state[slot, levels:high, :] = jnp.zeros((high - levels, wide), jnp.float32)
     for j in rows_done:
+        ready(j)
         mask = mask_row(mask_ref, j)
         weight = weight_ref[j]
         for t in range(tracers):
@@ -332,20 +355,47 @@
             def store(strip, tile, value):
                 state[slot, strip, tile] = value
 
-            transported(t, j, levels, field, courant_ref, mask, lat, hw, he, store)
+            transported(t, j, levels, field, courant, mask, lat, hw, he, store)
             for at in range(0, wide, 2 * LANES):
                 level = vertical(weight, state[slot, :, at : at + 2 * LANES])
                 out_ref[t, j, :, at : at + 2 * LANES] = level
 
 
-def inner_kernel(levels, odd_ref, pair_ref, other_ref, field, courant_ref, mask_ref, weight_ref,
-                 out_ref, west, east, hw, he, state):
+def arriving(copies):
+    def ready(j):
+        for copy in copies[j]:
+            copy.wait()
+
+    return ready
+
+
+def inner_courant(courant_ref):
+    return lambda k, j, strip, tile: courant_ref[k, j - 1, strip, tile]
+
+
+def edge_courant(courant_ref):
+    return lambda k, j, strip, tile: courant_ref[k, min(j, 1), strip, tile]
+
+
+def inner_kernel(levels, odd_ref, pair_ref, other_ref, field, inputs_hbm, mask_ref, weight_ref,
+                 out_ref, west, east, edge_ref, hw, he, state, courant_ref, sems):
+    tracers, rows = field.shape[:2]
+    rows_done = range(1, rows - 1)
+    copies = courant_copies(tracers, inputs_hbm, courant_ref, sems, rows_done, 0, range(rows - 2))
+    edges = courant_copies(
+        tracers, inputs_hbm, edge_ref, sems, (0, rows - 1), (rows - 2) * courant_ref.shape[0], (0, 1)
+    )
+    for group in (*copies.values(), *edges.values()):
+        for copy in group:
+            copy.start()
     ends_in_place(odd_ref, pair_ref, other_ref, hw, he)
-    rows_done = range(1, field.shape[1] - 1)
-    advance(rows_done, levels, None, field, courant_ref, mask_ref, hw, he, weight_ref, out_ref, state)
+    courant = inner_courant(courant_ref)
+    advance(rows_done, levels, None, field, courant, arriving(copies), mask_ref, hw, he, weight_ref, out_ref, state)
     for strip, first, last in collect_ends(rows_done, out_ref, no_ends):
         west[strip, :] = first
         east[strip, :] = last
+    for j in edges:
+        arriving(edges)(j)
 
 
 def edge_kernel(levels, odd_ref, pair_ref, other_ref, field, courant_ref, mask_ref, weight_ref, near_in, far_in,
@@ -353,30 +403,36 @@
     ends_in_place(odd_ref, pair_ref, other_ref, hw, he)
     rows_done = (0, field.shape[1] - 1)
     lat = by_side(odd_ref, near_in, far_in)
-    advance(rows_done, levels, lat, field, courant_ref, mask_ref, hw, he, weight_ref, out_ref, state)
+    courant = edge_courant(courant_ref)
+    advance(rows_done, levels, lat, field, courant, lambda j: None, mask_ref, hw, he, weight_ref, out_ref, state)
     before = lambda strip: (west[strip, :], east[strip, :])
     hand_out(odd_ref, out_ref, rows_done, before, near_ref, far_ref, pair_out, other_out)
 
 
-def step(levels, odd, field, courant, mask, weight, halos):
+COST = pl.CostEstimate(flops=30_000_000_000, bytes_accessed=8_000_000, transcendentals=0)
+
+
+def step(levels, odd, field, inputs, mask, weight, halos):
     f32 = jnp.float32
     near, far, pair, other = halos
     tracers, rows, high, wide = field.shape
     field_shape, edge, _, end, _ = shapes_of(tracers, rows, high, wide)
+    parts = inputs.shape[0] - tracers - SPARE
     ends = [pltpu.VMEM((high, LANES), f32)] * 2
     state = [pltpu.VMEM((2, high, wide), f32)]
-    params = pltpu.CompilerParams(vmem_limit_bytes=24 * MIB)
-    cost = lambda n: pl.CostEstimate(flops=n * 5_000_000_000, bytes_accessed=n * 1_000_000, transcendentals=0)
-    part, west, east = pl.pallas_call(
+    params = pltpu.CompilerParams(vmem_limit_bytes=LIMIT * MIB)
+    part, west, east, edge_flow = pl.pallas_call(
         functools.partial(inner_kernel, levels),
-        out_shape=(field_shape, end, end),
-        in_specs=[SMEM] + [VMEM] * 6,
-        out_specs=(VMEM,) * 3,
-        scratch_shapes=ends + state,
+        out_shape=(field_shape, end, end, jax.ShapeDtypeStruct((parts, 2, levels, wide), f32)),
+        in_specs=[SMEM] + [VMEM] * 3 + [HBM] + [VMEM] * 2,
+        out_specs=(VMEM,) * 4,
+        scratch_shapes=ends
+        + state
+        + [pltpu.VMEM((parts, rows - 2, levels, wide), f32), pltpu.SemaphoreType.DMA((parts * rows,))],
         compiler_params=params,
-        cost_estimate=cost(rows - 2),
-    )(odd, pair, other, field, courant, mask, weight)
-    return pl.pallas_call(
+        cost_estimate=COST,
+    )(odd, pair, other, field, inputs, mask, weight)
+    return *pl.pallas_call(
         functools.partial(edge_kernel, levels),
         out_shape=(field_shape, edge, edge, end, end),
         in_specs=[SMEM] + [VMEM] * 11,
@@ -384,23 +440,24 @@
         scratch_shapes=ends + state,
         input_output_aliases={9: 0},
         compiler_params=params,
-        cost_estimate=cost(2),
-    )(odd, pair, other, field, courant, mask, weight, near, far, part, west, east)
-
-
-def finish(rows_done, levels, lat, field, courant_ref, mask_ref, hw, he, out_ref, state, sems):
+    )(odd, pair, other, field, edge_flow, mask, weight, near, far, part, west, east), edge_flow
+
+
+def finish(rows_done, levels, lat, field, courant, ready, mask_ref, hw, he, out_ref, state, sems):
     tracers = field.shape[0]
     slots = state.shape[0]
     flying = {}
     for k, (j, t) in enumerate((j, t) for j in rows_done for t in range(tracers)):
         slot = k % slots
+        if t == 0:
+            ready(j)
         if slot in flying:
             flying.pop(slot).wait()
 
         def store(strip, tile, value):
             state[slot, strip, tile] = value
 
-        transported(t, j, levels, field, courant_ref, mask_row(mask_ref, j), lat, hw, he, store)
+        transported(t, j, levels, field, courant, mask_row(mask_ref, j), lat, hw, he, store)
         copy = pltpu.make_async_copy(state.at[slot], out_ref.at[t, :, j, :], sems.at[slot])
         copy.start()
         flying[slot] = copy
@@ -408,10 +465,17 @@
         copy.wait()
 
 
-def final_inner_kernel(levels, odd_ref, pair_ref, other_ref, field, courant_ref, mask_ref, out_ref, hw, he, state, sems):
+def final_inner_kernel(levels, odd_ref, pair_ref, other_ref, field, inputs_hbm, mask_ref, out_ref, hw, he, state, sems,
+                       courant_ref, courant_sems):
+    tracers, rows = field.shape[:2]
+    rows_done = range(1, rows - 1)
+    copies = courant_copies(tracers, inputs_hbm, courant_ref, courant_sems, rows_done, 0, range(rows - 2))
+    for group in copies.values():
+        for copy in group:
+            copy.start()
     ends_in_place(odd_ref, pair_ref, other_ref, hw, he)
-    rows = field.shape[1]
-    finish(range(1, rows - 1), levels, None, field, courant_ref, mask_ref, hw, he, out_ref, state, sems)
+    courant = inner_courant(courant_ref)
+    finish(rows_done, levels, None, field, courant, arriving(copies), mask_ref, hw, he, out_ref, state, sems)
 
 
 def final_edge_kernel(levels, odd_ref, pair_ref, other_ref, field, courant_ref, mask_ref, near_in, far_in, part_ref,
@@ -419,30 +483,35 @@
     ends_in_place(odd_ref, pair_ref, other_ref, hw, he)
     rows = field.shape[1]
     lat = by_side(odd_ref, near_in, far_in)
-    finish((0, rows - 1), levels, lat, field, courant_ref, mask_ref, hw, he, out_ref, state, sems)
-
-
-def last_step(levels, odd, field, courant, mask, halos):
+    courant = edge_courant(courant_ref)
+    finish((0, rows - 1), levels, lat, field, courant, lambda j: None, mask_ref, hw, he, out_ref, state, sems)
+
+
+def last_step(levels, odd, field, inputs, edge_flow, mask, halos):
     f32 = jnp.float32
     near, far, pair, other = halos
     tracers, rows, high, wide = field.shape
+    parts = edge_flow.shape[0]
     slots = 4
     scratch = [pltpu.VMEM((high, LANES), f32)] * 2 + [
         pltpu.VMEM((slots, levels, wide), f32),
         pltpu.SemaphoreType.DMA((slots,)),
     ]
     shape = jax.ShapeDtypeStruct((tracers, levels, rows, wide), f32)
-    params = pltpu.CompilerParams(vmem_limit_bytes=24 * MIB)
-    cost = lambda n: pl.CostEstimate(flops=n * 5_000_000_000, bytes_accessed=n * 1_000_000, transcendentals=0)
+    params = pltpu.CompilerParams(vmem_limit_bytes=LIMIT * MIB)
     part = pl.pallas_call(
         functools.partial(final_inner_kernel, levels),
         out_shape=shape,
-        in_specs=[SMEM] + [VMEM] * 5,
+        in_specs=[SMEM] + [VMEM] * 3 + [HBM, VMEM],
         out_specs=HBM,
-        scratch_shapes=scratch,
+        scratch_shapes=scratch
+        + [
+            pltpu.VMEM((parts, rows - 2, levels, wide), f32),
+            pltpu.SemaphoreType.DMA((parts * (rows - 2),)),
+        ],
         compiler_params=params,
-        cost_estimate=cost(rows - 2),
-    )(odd, pair, other, field, courant, mask)
+        cost_estimate=COST,
+    )(odd, pair, other, field, inputs, mask)
     return pl.pallas_call(
         functools.partial(final_edge_kernel, levels),
         out_shape=shape,
@@ -451,8 +520,7 @@
         scratch_shapes=scratch,
         input_output_aliases={8: 0},
         compiler_params=params,
-        cost_estimate=cost(2),
-    )(odd, pair, other, field, courant, mask, near, far, part)
+    )(odd, pair, other, field, edge_flow, mask, near, far, part)
 
 
 def weights(inverse, high):
@@ -484,12 +552,12 @@
     odd = jnp.stack([lax.axis_index("lat") % 2, lax.axis_index("lon") % 2]).astype(jnp.int32)
     send = pack(obs_owner, obs_cell, obs_values, levels, high, wide // LANES, devices)
     got = lax.all_to_all(send, ("lat", "lon"), split_axis=0, concat_axis=0, tiled=True)
-    terminal, courant = prepare(terminal, courant)
+    inputs = prepare(terminal, courant)
     weight = weights(inverse, high)
-    field, *edges = start(odd, got, weight, terminal, high, devices)
+    field, *edges = start(odd, got, weight, inputs, tracers, high, devices)
     for _ in range(STEPS - 1):
-        field, *edges = step(levels, odd, field, courant, land_mask, weight, exchange(*edges))
-    out = last_step(levels, odd, field, courant, land_mask, exchange(*edges))
+        field, *edges, edge_flow = step(levels, odd, field, inputs, land_mask, weight, exchange(*edges))
+    out = last_step(levels, odd, field, inputs, edge_flow, land_mask, exchange(*edges))
     return jnp.swapaxes(out, 1, 2)
 
 

time: 367 us -> 93.8 us (0.26)
  Pallas kernels: 332 us -> 42.6 us
  waiting for transfers between devices: 2.73 us -> 23.5 us
  local copies, waits for them, and re-layouts: 5.17 us -> 0.29 us
    pallas_call x1, Pallas kernels: 299 us -> 9.01 us  [prepare(): pl.pallas_call(prepare_kernel, out_shape=jax.ShapeDtypeStruct((parts + SP...]
    all_to_all x1, waiting for transfers between devices: 0.01 us -> 20.3 us  [local(): lax.all_to_all(send, ('lat', 'lon'), split_axis=0, concat_axis=0, tiled=T...]
    unnamed x9 -> x5, local copies, waits for them, and re-layouts: 5.13 us -> 0.24 us
  transfers between devices with their start and end apart: 9 -> 9, of which waited for: 1 -> 4; matrix products, arithmetic and copies ran while one was open for 0% -> 1% of each run, Pallas kernels for 84% -> 22%
where the time goes in v2:
time: 93.8 us; the launch traced here: 92.9 us
  Pallas kernels  42.6 us (45%)
  starting transfers between devices  25.7 us (27%)
  waiting for transfers between devices  23.5 us (25%)
    all_to_all x1, waiting for transfers between devices, local(): lax.all_to_all(send, ('lat', 'lon'), split_axis=0, concat_axis=0, tiled=T...  20.3 us
    all_to_all x1, starting transfers between devices, local(): lax.all_to_all(send, ('lat', 'lon'), split_axis=0, concat_axis=0, tiled=T...  10.4 us
    pallas_call x1, Pallas kernels, start(): pl.pallas_call(functools.partial(start_kernel, devices), out_shape=shapes...  10.3 us
    pallas_call x1, Pallas kernels, prepare(): pl.pallas_call(prepare_kernel, out_shape=jax.ShapeDtypeStruct((parts + SP...  9.01 us
    ppermute x2, starting transfers between devices, exchange(): far = lax.ppermute(far, 'lat', next_pair)  8.56 us
    pallas_call x1, Pallas kernels, pack(): pl.pallas_call(functools.partial(pack_kernel, (levels, high, columns, dev...  8.08 us
    pallas_call x1, Pallas kernels, step(): pl.pallas_call(functools.partial(inner_kernel, levels), out_shape=(field_...  6 us
    pallas_call x1, Pallas kernels, last_step(): pl.pallas_call(functools.partial(final_inner_kernel, levels), out_shape=s...  5.34 us
  transfers between devices with their start and end apart: 9, of which 4 were waited for; matrix products, arithmetic and copies ran while one was open for 1% of the time, Pallas kernels for 22%

profile of v2, /device:TPU:8, one launch (start us, length us, event | category | flops | bytes accessed | tf_op | source)
XLA Modules:
  0.0 92.9 jit_solution(15710955996921169472)
XLA Ops:
  0.0 8.1 %shard_map.73 = f32[4224,1,128]{2,1,0:T(1,128)} custom-call(s32[16,128]{1,0:T(8,128)} %bitcast.14, s32[16,128]{1,0:T(8,128)} %bitcast.15, f32[2048,1,128]{2,1,0:T(1,128)} %bitcast.13), custom_call_target="tpu_custom_call" | custom-call | tf_op jit(solution)/shard_map/pallas_call | solution.py:98
  8.1 0.0 copy-start.1
  8.1 10.4 %all-to-all-start = ((f32[4224,1,128]{2,1,0:T(1,128)}), f32[4224,1,128]{2,1,0:T(1,128)S(1)}, u32[]{:S(2)}, u32[]{:S(2)}) async-start(f32[4224,1,128]{2,1,0:T(1,128)} %shard_map.73), calls=%async_computation | async-start | bytes 4325376 | tf_op jit(solution)/shard_map/all_to_all | solution.py:554
  18.6 0.0 copy-done.1
  18.6 0.2 copy.10
  18.8 9.0 %shard_map.74.inputs_hbm = f32[16,8,100,512]{3,2,1,0:T(8,128)} custom-call(f32[2,100,8,512]{3,2,1,0:T(8,128)} %bitcast.12, f32[4,100,8,512]{3,2,1,0:T(8,128)} %bitcast.10), custom_call_target="tpu_custom_call" | custom-call | tf_op jit(solution)/shard_map/pallas_call | solution.py:183
  27.8 0.1 pad_add_fusion.odd_ref
  28.0 0.1 subtract_convert_fusion
  28.1 0.4 maximum_maximum_fusion.weight_hbm.weight_ref
  28.5 0.0 copy-start
  28.5 20.3 %all-to-all-done.got_ref = f32[4224,1,128]{2,1,0:T(1,128)S(1)} async-done(((f32[4224,1,128]{2,1,0:T(1,128)}), f32[4224,1,128]{2,1,0:T(1,128)S(1)}, u32[]{:S(2)}, u32[]{:S(2)}) %all-to-all-start) | async-done | bytes 2162720 | tf_op jit(solution)/shard_map/all_to_all | solution.py:554
  48.8 10.3 %shard_map.75 = (f32[2,8,104,512]{3,2,1,0:T(8,128)S(1)}, f32[2,104,512]{2,1,0:T(8,128)S(1)}, f32[2,104,512]{2,1,0:T(8,128)S(1)}, f32[104,128]{1,0:T(8,128)S(1)}, f32[104,128]{1,0:T(8,128)S(1)}) custom-call(s32[2]{0:T(128)S(1)} %pad_add_fusion.odd_ref, f32[4224,1,128]{2,1,0:T(1,128)S(1)} %all-to-all-done.got_ref, ...), custom_call_target="tpu_custom_call" | custom-call | tf_op jit(solution)/shard_map/pallas_call | solution.py:278
  59.1 3.3 %collective-permute-start = (f32[104,128]{1,0:T(8,128)S(1)}, f32[104,128]{1,0:T(8,128)S(1)}, u32[]{:S(2)}, u32[]{:S(2)}) collective-permute-start(f32[104,128]{1,0:T(8,128)S(1)} %get-tuple-element.19), channel_id=1, source_target_pairs={{0,1},{1,0},{2,3},{3,2},{4,5},{5,4},{6,7},{7,6},{8,9},{9,8},{10,11... | collective-permute-start | bytes 159752 | tf_op jit(solution)/shard_map/ppermute | solution.py:542
  62.4 0.9 collective-permute-start.1
  63.3 0.0 collective-permute-start.2
  63.3 4.1 %collective-permute-start.3 = (f32[2,104,512]{2,1,0:T(8,128)S(1)}, f32[2,104,512]{2,1,0:T(8,128)S(1)}, u32[]{:S(2)}, u32[]{:S(2)}) collective-permute-start(f32[2,104,512]{2,1,0:T(8,128)S(1)} %get-tuple-element.24), channel_id=1, source_target_pairs={{4,8},{8,4},{12,16},{16,12},{20,24},{24,20},{28,32},{32,28},{36,40... | collective-permute-start | bytes 1277960 | tf_op jit(solution)/shard_map/ppermute | solution.py:543
  67.4 0.0 collective-permute-done.pair_ref
  67.4 0.4 collective-permute-done.1.other_ref
  67.8 6.0 %shard_map.76 = (f32[2,8,104,512]{3,2,1,0:T(8,128)S(1)}, f32[104,128]{1,0:T(8,128)S(1)}, f32[104,128]{1,0:T(8,128)S(1)}, f32[4,2,100,512]{3,2,1,0:T(8,128)S(1)}) custom-call(s32[2]{0:T(128)S(1)} %pad_add_fusion.odd_ref, f32[104,128]{1,0:T(8,128)S(1)} %collective-permute-done.pair_ref, f32[104,128]{1,0:T(8,128)S(1)} %collective-permute-done.1.other_ref, ...), custom_call_target="tpu_custom_call" | custom-call | flops 30000001024 | bytes 8000000 | tf_op jit(solution)/shard_map/pallas_call | solution.py:424
  73.8 0.0 collective-permute-done.2.near_in
  73.8 1.1 %collective-permute-done.3.far_in = f32[2,104,512]{2,1,0:T(8,128)S(1)} collective-permute-done((f32[2,104,512]{2,1,0:T(8,128)S(1)}, f32[2,104,512]{2,1,0:T(8,128)S(1)}, u32[]{:S(2)}, u32[]{:S(2)}) %collective-permute-start.3) | collective-permute-done | bytes 426016 | tf_op jit(solution)/shard_map/ppermute | solution.py:543
  74.8 1.7 %shard_map.77 = (f32[2,8,104,512]{3,2,1,0:T(8,128)S(1)}, f32[2,104,512]{2,1,0:T(8,128)S(1)}, f32[2,104,512]{2,1,0:T(8,128)S(1)}, f32[104,128]{1,0:T(8,128)S(1)}, f32[104,128]{1,0:T(8,128)S(1)}) custom-call(s32[2]{0:T(128)S(1)} %pad_add_fusion.odd_ref, f32[104,128]{1,0:T(8,128)S(1)} %collective-permute-done.pair_ref, ...), custom_call_target="tpu_custom_call", output_to_operand_aliasing={{0}: (9, {})} | custom-call | tf_op jit(solution)/shard_map/pallas_call | solution.py:435
  76.6 1.4 %collective-permute-start.4 = (f32[104,128]{1,0:T(8,128)S(1)}, f32[104,128]{1,0:T(8,128)S(1)}, u32[]{:S(2)}, u32[]{:S(2)}) collective-permute-start(f32[104,128]{1,0:T(8,128)S(1)} %get-tuple-element.28), channel_id=1, source_target_pairs={{0,1},{1,0},{2,3},{3,2},{4,5},{5,4},{6,7},{7,6},{8,9},{9,8},{10,11... | collective-permute-start | bytes 159752 | tf_op jit(solution)/shard_map/ppermute | solution.py:542
  78.0 1.1 %collective-permute-start.5 = (f32[104,128]{1,0:T(8,128)S(1)}, f32[104,128]{1,0:T(8,128)S(1)}, u32[]{:S(2)}, u32[]{:S(2)}) collective-permute-start(f32[104,128]{1,0:T(8,128)S(1)} %get-tuple-element.29), channel_id=1, source_target_pairs={{0,3},{1,2},{2,1},{3,0},{4,7},{5,6},{6,5},{7,4},{8,11},{9,10},{10,... | collective-permute-start | bytes 159752 | tf_op jit(solution)/shard_map/ppermute | solution.py:541
  79.1 0.0 collective-permute-start.6
  79.1 4.5 %collective-permute-start.7 = (f32[2,104,512]{2,1,0:T(8,128)S(1)}, f32[2,104,512]{2,1,0:T(8,128)S(1)}, u32[]{:S(2)}, u32[]{:S(2)}) collective-permute-start(f32[2,104,512]{2,1,0:T(8,128)S(1)} %get-tuple-element.32), channel_id=1, source_target_pairs={{4,8},{8,4},{12,16},{16,12},{20,24},{24,20},{28,32},{32,28},{36,40... | collective-permute-start | bytes 1277960 | tf_op jit(solution)/shard_map/ppermute | solution.py:543
  83.6 0.0 collective-permute-done.4.pair_ref
  83.6 0.0 collective-permute-done.5.other_ref
  83.6 5.3 %shard_map.78.part_ref = f32[2,100,8,512]{3,2,1,0:T(8,128)} custom-call(s32[2]{0:T(128)S(1)} %pad_add_fusion.odd_ref, f32[104,128]{1,0:T(8,128)S(1)} %collective-permute-done.4.pair_ref, f32[104,128]{1,0:T(8,128)S(1)} %collective-permute-done.5.other_ref, f32[2,8,104,512]{3,2,1,0:T(8,128)S(1)} %get-tuple-element.30.field, ...), custom_call_target="tpu_custom_call" | custom-call | flops 30000001024 | bytes 8000000 | tf_op jit(solution)/shard_map/pallas_call | solution.py:502
  89.0 0.0 collective-permute-done.6.near_in
  89.0 1.7 %collective-permute-done.7.far_in = f32[2,104,512]{2,1,0:T(8,128)S(1)} collective-permute-done((f32[2,104,512]{2,1,0:T(8,128)S(1)}, f32[2,104,512]{2,1,0:T(8,128)S(1)}, u32[]{:S(2)}, u32[]{:S(2)}) %collective-permute-start.7) | collective-permute-done | bytes 426016 | tf_op jit(solution)/shard_map/ppermute | solution.py:543
  90.7 2.1 %shard_map.79 = f32[2,100,8,512]{3,2,1,0:T(8,128)} custom-call(s32[2]{0:T(128)S(1)} %pad_add_fusion.odd_ref, f32[104,128]{1,0:T(8,128)S(1)} %collective-permute-done.4.pair_ref, f32[104,128]{1,0:T(8,128)S(1)} %collective-permute-done.5.other_ref, f32[2,8,104,512]{3,2,1,0:T(8,128)S(1)} %get-tuple-element.30.field, ...), custom_call_target="tpu_custom_call", output_to_operand_aliasing={{}: (8, {})} | custom-call | tf_op jit(solution)/shard_map/pallas_call | solution.py:515
  (3 shorter events, 0.1 us)
Async XLA Ops:
  8.1 10.5 %copy-start.1 = (f32[8,100,100]{2,0,1:T(8,128)S(1)}, f32[8,100,100]{2,0,1:T(8,128)}, u32[]{:S(2)}) copy-start(f32[8,100,100]{2,0,1:T(8,128)} %param.9) | copy-start | bytes 960004
  8.1 40.7 %all-to-all-start = ((f32[4224,1,128]{2,1,0:T(1,128)}), f32[4224,1,128]{2,1,0:T(1,128)S(1)}, u32[]{:S(2)}, u32[]{:S(2)}) async-start(f32[4224,1,128]{2,1,0:T(1,128)} %shard_map.73), calls=%async_computation | async-start | bytes 4325376 | tf_op jit(solution)/shard_map/all_to_all | solution.py:554
  28.5 39.3 %copy-start = (s32[8,512]{1,0:T(8,128)S(1)}, s32[8,512]{1,0:T(8,128)}, u32[]{:S(2)}) copy-start(s32[8,512]{1,0:T(8,128)} %mask_ref.7) | copy-start | bytes 49156
  59.1 8.3 %collective-permute-start = (f32[104,128]{1,0:T(8,128)S(1)}, f32[104,128]{1,0:T(8,128)S(1)}, u32[]{:S(2)}, u32[]{:S(2)}) collective-permute-start(f32[104,128]{1,0:T(8,128)S(1)} %get-tuple-element.19), channel_id=1, source_target_pairs={{0,1},{1,0},{2,3},{3,2},{4,5},{5,4},{6,7},{7,6},{8,9},{9,8},{10,11... | collective-permute-start | bytes 159752 | tf_op jit(solution)/shard_map/ppermute | solution.py:542
  62.4 5.3 %collective-permute-start.1 = (f32[104,128]{1,0:T(8,128)S(1)}, f32[104,128]{1,0:T(8,128)S(1)}, u32[]{:S(2)}, u32[]{:S(2)}) collective-permute-start(f32[104,128]{1,0:T(8,128)S(1)} %get-tuple-element.20), channel_id=1, source_target_pairs={{0,3},{1,2},{2,1},{3,0},{4,7},{5,6},{6,5},{7,4},{8,11},{9,10},{10,... | collective-permute-start | bytes 159752 | tf_op jit(solution)/shard_map/ppermute | solution.py:541
  63.3 10.5 %collective-permute-start.2 = (f32[2,104,512]{2,1,0:T(8,128)S(1)}, f32[2,104,512]{2,1,0:T(8,128)S(1)}, u32[]{:S(2)}, u32[]{:S(2)}) collective-permute-start(f32[2,104,512]{2,1,0:T(8,128)S(1)} %get-tuple-element.23), channel_id=1, source_target_pairs={{0,4},{4,0},{8,12},{12,8},{16,20},{20,16},{24,28},{28,24},{32,36},... | collective-permute-start | bytes 1277960 | tf_op jit(solution)/shard_map/ppermute | solution.py:544
  63.3 11.5 %collective-permute-start.3 = (f32[2,104,512]{2,1,0:T(8,128)S(1)}, f32[2,104,512]{2,1,0:T(8,128)S(1)}, u32[]{:S(2)}, u32[]{:S(2)}) collective-permute-start(f32[2,104,512]{2,1,0:T(8,128)S(1)} %get-tuple-element.24), channel_id=1, source_target_pairs={{4,8},{8,4},{12,16},{16,12},{20,24},{24,20},{28,32},{32,28},{36,40... | collective-permute-start | bytes 1277960 | tf_op jit(solution)/shard_map/ppermute | solution.py:543
  76.6 7.0 %collective-permute-start.4 = (f32[104,128]{1,0:T(8,128)S(1)}, f32[104,128]{1,0:T(8,128)S(1)}, u32[]{:S(2)}, u32[]{:S(2)}) collective-permute-start(f32[104,128]{1,0:T(8,128)S(1)} %get-tuple-element.28), channel_id=1, source_target_pairs={{0,1},{1,0},{2,3},{3,2},{4,5},{5,4},{6,7},{7,6},{8,9},{9,8},{10,11... | collective-permute-start | bytes 159752 | tf_op jit(solution)/shard_map/ppermute | solution.py:542
  78.0 5.6 %collective-permute-start.5 = (f32[104,128]{1,0:T(8,128)S(1)}, f32[104,128]{1,0:T(8,128)S(1)}, u32[]{:S(2)}, u32[]{:S(2)}) collective-permute-start(f32[104,128]{1,0:T(8,128)S(1)} %get-tuple-element.29), channel_id=1, source_target_pairs={{0,3},{1,2},{2,1},{3,0},{4,7},{5,6},{6,5},{7,4},{8,11},{9,10},{10,... | collective-permute-start | bytes 159752 | tf_op jit(solution)/shard_map/ppermute | solution.py:541
  79.1 9.9 %collective-permute-start.6 = (f32[2,104,512]{2,1,0:T(8,128)S(1)}, f32[2,104,512]{2,1,0:T(8,128)S(1)}, u32[]{:S(2)}, u32[]{:S(2)}) collective-permute-start(f32[2,104,512]{2,1,0:T(8,128)S(1)} %get-tuple-element.31), channel_id=1, source_target_pairs={{0,4},{4,0},{8,12},{12,8},{16,20},{20,16},{24,28},{28,24},{32,36},... | collective-permute-start | bytes 1277960 | tf_op jit(solution)/shard_map/ppermute | solution.py:544
  79.1 11.5 %collective-permute-start.7 = (f32[2,104,512]{2,1,0:T(8,128)S(1)}, f32[2,104,512]{2,1,0:T(8,128)S(1)}, u32[]{:S(2)}, u32[]{:S(2)}) collective-permute-start(f32[2,104,512]{2,1,0:T(8,128)S(1)} %get-tuple-element.32), channel_id=1, source_target_pairs={{4,8},{8,4},{12,16},{16,12},{20,24},{24,20},{28,32},{32,28},{36,40... | collective-permute-start | bytes 1277960 | tf_op jit(solution)/shard_map/ppermute | solution.py:543

commit v3 on v1

--- a/solution.py
+++ b/solution.py
@@ -18,6 +18,8 @@
     return -(-levels // 8) * 8
 
 
+SPARE = 10
+LIMIT = 24
 VMEM = pl.BlockSpec(memory_space=pltpu.VMEM)
 SMEM = pl.BlockSpec(memory_space=pltpu.SMEM)
 HBM = pl.BlockSpec(memory_space=pltpu.HBM)
@@ -158,40 +160,50 @@
         far_ref[...] = field[:, last]
 
 
-def prepare_kernel(terminal_in, courant_in, terminal_out, courant_out, sems):
-    copies = []
-    for source, target in ((terminal_in, terminal_out), (courant_in, courant_out)):
-        parts, rows = target.shape[:2]
-        for part in range(parts):
-            for j in range(rows):
-                copies.append(
-                    pltpu.make_async_copy(source.at[part, :, j, :], target.at[part, j], sems.at[len(copies)])
-                )
-                copies[-1].start()
-    for copy in copies:
-        copy.wait()
+def prepare_kernel(terminal_in, courant_in, out, stage, sems):
+    moves = []
+    for source in (terminal_in, courant_in):
+        for part in range(source.shape[0]):
+            at = len(moves) // out.shape[1]
+            for j in range(out.shape[1]):
+                sem = sems.at[len(moves)]
+                load = pltpu.make_async_copy(source.at[part, :, j, :], stage.at[at, j], sem)
+                moves.append((load, pltpu.make_async_copy(stage.at[at, j], out.at[at, j], sem)))
+                load.start()
+    for load, save in moves:
+        load.wait()
+        save.start()
+    for load, save in moves:
+        save.wait()
 
 
 def prepare(terminal, courant):
-    rows = terminal.shape[1]
+    _, rows, levels, wide = terminal.shape
+    parts = terminal.shape[0] + courant.shape[0]
     return pl.pallas_call(
         prepare_kernel,
-        out_shape=tuple(jax.ShapeDtypeStruct(x.shape, x.dtype) for x in (terminal, courant)),
+        out_shape=jax.ShapeDtypeStruct((parts + SPARE, rows, levels, wide), terminal.dtype),
         in_specs=[HBM] * 2,
-        out_specs=(HBM,) * 2,
-        scratch_shapes=[pltpu.SemaphoreType.DMA(((terminal.shape[0] + courant.shape[0]) * rows,))],
+        out_specs=HBM,
+        scratch_shapes=[
+            pltpu.VMEM((parts, rows, levels, wide), terminal.dtype),
+            pltpu.SemaphoreType.DMA((parts * rows,)),
+        ],
         compiler_params=pltpu.CompilerParams(vmem_limit_bytes=60 * MIB),
     )(jnp.swapaxes(terminal, 1, 2), jnp.swapaxes(courant, 1, 2))
 
 
-def start_kernel(devices, odd_ref, got_ref, weight_hbm, terminal_hbm, out_ref, near_ref, far_ref, pair_ref, other_ref,
+def start_kernel(devices, odd_ref, got_ref, weight_hbm, inputs_hbm, out_ref, near_ref, far_ref, pair_ref, other_ref, courant_ref,
                  terminal_ref, weight_ref, addr_v, addr_s, state, sems, *banks):
     tracers, rows, levels, wide = terminal_ref.shape
     columns = wide // LANES
-    get_terminal = pltpu.make_async_copy(terminal_hbm, terminal_ref, sems.at[1])
+    get_terminal = pltpu.make_async_copy(inputs_hbm.at[pl.ds(0, terminal_ref.shape[0])], terminal_ref, sems.at[1])
     get_weight = pltpu.make_async_copy(weight_hbm, weight_ref, sems.at[2])
+    tracers, parts = terminal_ref.shape[0], courant_ref.shape[0]
+    get_courant = pltpu.make_async_copy(inputs_hbm.at[pl.ds(tracers, parts)], courant_ref, sems.at[3])
     get_terminal.start()
     get_weight.start()
+    get_courant.start()
     high = state.shape[1]
     whole = levels // 8 * 8
     for o in range(devices):
@@ -214,12 +226,12 @@
         for b in range(1, BANKS):
             most = jnp.maximum(most, addr_s[first + b, 32])
 
-        @pl.loop(0, (most + 3) // 4)
+        @pl.loop(0, (most + 7) // 8)
         def _(c):
-            for u in range(4):
+            for u in range(8):
                 for b, bank in enumerate(banks):
-                    place = addr_s[first + b, c * 4 + u]
-                    bank[pl.ds(place, 1), :] += got_ref[(first + b) * SLOTS + c * 4 + u]
+                    place = addr_s[first + b, c * 8 + u]
+                    bank[pl.ds(place, 1), :] += got_ref[(first + b) * SLOTS + c * 8 + u]
 
     for slot in range(state.shape[0]):
         state[slot, levels:high, :] = jnp.zeros((high - levels, wide), jnp.float32)
@@ -240,6 +252,7 @@
             for at in range(0, wide, 2 * LANES):
                 out_ref[t, j, :, at : at + 2 * LANES] = vertical(weight, state[slot, :, at : at + 2 * LANES])
     hand_out(odd_ref, out_ref, range(rows), no_ends, near_ref, far_ref, pair_ref, other_ref)
+    get_courant.wait()
 
 
 def shapes_of(tracers, rows, high, wide):
@@ -249,26 +262,27 @@
     return jax.ShapeDtypeStruct((tracers, rows, high, wide), f32), edge, edge, end, end
 
 
-def start(odd, got, weight, terminal, high, devices):
+def start(odd, got, weight, inputs, tracers, high, devices):
     f32 = jnp.float32
-    tracers, rows, levels, wide = terminal.shape
+    parts, rows, levels, wide = inputs.shape
     places = tracers * rows * (wide // LANES) * high
     return pl.pallas_call(
         functools.partial(start_kernel, devices),
-        out_shape=shapes_of(tracers, rows, high, wide),
+        out_shape=shapes_of(tracers, rows, high, wide)
+        + (jax.ShapeDtypeStruct((parts - SPARE - tracers, rows, levels, wide), f32),),
         in_specs=[SMEM, VMEM, HBM, HBM],
-        out_specs=(VMEM,) * 5,
+        out_specs=(VMEM,) * 6,
         scratch_shapes=[
-            pltpu.VMEM(terminal.shape, f32),
+            pltpu.VMEM((tracers, rows, levels, wide), f32),
             pltpu.VMEM(weight.shape, weight.dtype),
             pltpu.VMEM((devices, LANES), jnp.int32),
             pltpu.SMEM((devices, LANES), jnp.int32),
             pltpu.VMEM((2, high, wide), f32),
-            pltpu.SemaphoreType.DMA((3,)),
+            pltpu.SemaphoreType.DMA((4,)),
         ]
         + [pltpu.VMEM((places + 64, LANES), f32) for _ in range(BANKS)],
-        compiler_params=pltpu.CompilerParams(vmem_limit_bytes=32 * MIB),
-    )(odd, got, weight, terminal)
+        compiler_params=pltpu.CompilerParams(vmem_limit_bytes=36 * MIB),
+    )(odd, got, weight, inputs)
 
 
 def ends_in_place(odd_ref, pair_ref, other_ref, west, east):
@@ -358,33 +372,33 @@
     hand_out(odd_ref, out_ref, rows_done, before, near_ref, far_ref, pair_out, other_out)
 
 
+COST = pl.CostEstimate(flops=30_000_000_000, bytes_accessed=8_000_000, transcendentals=0)
+
+
 def step(levels, odd, field, courant, mask, weight, halos):
     f32 = jnp.float32
     near, far, pair, other = halos
     tracers, rows, high, wide = field.shape
     field_shape, edge, _, end, _ = shapes_of(tracers, rows, high, wide)
-    ends = [pltpu.VMEM((high, LANES), f32)] * 2
-    state = [pltpu.VMEM((2, high, wide), f32)]
-    params = pltpu.CompilerParams(vmem_limit_bytes=24 * MIB)
-    cost = lambda n: pl.CostEstimate(flops=n * 5_000_000_000, bytes_accessed=n * 1_000_000, transcendentals=0)
+    scratch = [pltpu.VMEM((high, LANES), f32)] * 2 + [pltpu.VMEM((2, high, wide), f32)]
+    params = pltpu.CompilerParams(vmem_limit_bytes=LIMIT * MIB)
     part, west, east = pl.pallas_call(
         functools.partial(inner_kernel, levels),
         out_shape=(field_shape, end, end),
         in_specs=[SMEM] + [VMEM] * 6,
         out_specs=(VMEM,) * 3,
-        scratch_shapes=ends + state,
+        scratch_shapes=scratch,
         compiler_params=params,
-        cost_estimate=cost(rows - 2),
+        cost_estimate=COST,
     )(odd, pair, other, field, courant, mask, weight)
     return pl.pallas_call(
         functools.partial(edge_kernel, levels),
         out_shape=(field_shape, edge, edge, end, end),
         in_specs=[SMEM] + [VMEM] * 11,
         out_specs=(VMEM,) * 5,
-        scratch_shapes=ends + state,
+        scratch_shapes=scratch,
         input_output_aliases={9: 0},
         compiler_params=params,
-        cost_estimate=cost(2),
     )(odd, pair, other, field, courant, mask, weight, near, far, part, west, east)
 
 
@@ -410,30 +424,28 @@
 
 def final_inner_kernel(levels, odd_ref, pair_ref, other_ref, field, courant_ref, mask_ref, out_ref, hw, he, state, sems):
     ends_in_place(odd_ref, pair_ref, other_ref, hw, he)
-    rows = field.shape[1]
-    finish(range(1, rows - 1), levels, None, field, courant_ref, mask_ref, hw, he, out_ref, state, sems)
+    rows_done = range(1, field.shape[1] - 1)
+    finish(rows_done, levels, None, field, courant_ref, mask_ref, hw, he, out_ref, state, sems)
 
 
 def final_edge_kernel(levels, odd_ref, pair_ref, other_ref, field, courant_ref, mask_ref, near_in, far_in, part_ref,
                       out_ref, hw, he, state, sems):
     ends_in_place(odd_ref, pair_ref, other_ref, hw, he)
-    rows = field.shape[1]
     lat = by_side(odd_ref, near_in, far_in)
-    finish((0, rows - 1), levels, lat, field, courant_ref, mask_ref, hw, he, out_ref, state, sems)
+    finish((0, field.shape[1] - 1), levels, lat, field, courant_ref, mask_ref, hw, he, out_ref, state, sems)
 
 
 def last_step(levels, odd, field, courant, mask, halos):
     f32 = jnp.float32
     near, far, pair, other = halos
     tracers, rows, high, wide = field.shape
-    slots = 4
+    slots = 12
     scratch = [pltpu.VMEM((high, LANES), f32)] * 2 + [
         pltpu.VMEM((slots, levels, wide), f32),
         pltpu.SemaphoreType.DMA((slots,)),
     ]
     shape = jax.ShapeDtypeStruct((tracers, levels, rows, wide), f32)
-    params = pltpu.CompilerParams(vmem_limit_bytes=24 * MIB)
-    cost = lambda n: pl.CostEstimate(flops=n * 5_000_000_000, bytes_accessed=n * 1_000_000, transcendentals=0)
+    params = pltpu.CompilerParams(vmem_limit_bytes=LIMIT * MIB)
     part = pl.pallas_call(
         functools.partial(final_inner_kernel, levels),
         out_shape=shape,
@@ -441,7 +453,7 @@
         out_specs=HBM,
         scratch_shapes=scratch,
         compiler_params=params,
-        cost_estimate=cost(rows - 2),
+        cost_estimate=COST,
     )(odd, pair, other, field, courant, mask)
     return pl.pallas_call(
         functools.partial(final_edge_kernel, levels),
@@ -451,7 +463,6 @@
         scratch_shapes=scratch,
         input_output_aliases={8: 0},
         compiler_params=params,
-        cost_estimate=cost(2),
     )(odd, pair, other, field, courant, mask, near, far, part)
 
 
@@ -484,9 +495,9 @@
     odd = jnp.stack([lax.axis_index("lat") % 2, lax.axis_index("lon") % 2]).astype(jnp.int32)
     send = pack(obs_owner, obs_cell, obs_values, levels, high, wide // LANES, devices)
     got = lax.all_to_all(send, ("lat", "lon"), split_axis=0, concat_axis=0, tiled=True)
-    terminal, courant = prepare(terminal, courant)
+    inputs = prepare(terminal, courant)
     weight = weights(inverse, high)
-    field, *edges = start(odd, got, weight, terminal, high, devices)
+    field, *edges, courant = start(odd, got, weight, inputs, tracers, high, devices)
     for _ in range(STEPS - 1):
         field, *edges = step(levels, odd, field, courant, land_mask, weight, exchange(*edges))
     out = last_step(levels, odd, field, courant, land_mask, exchange(*edges))

time: 367 us -> 93.2 us (0.25)
  Pallas kernels: 332 us -> 37.8 us
  waiting for transfers between devices: 2.73 us -> 29.3 us
  local copies, waits for them, and re-layouts: 5.17 us -> 0.28 us
    pallas_call x1, Pallas kernels: 299 us -> 9.01 us  [prepare(): pl.pallas_call(prepare_kernel, out_shape=jax.ShapeDtypeStruct((parts + SP...]
    all_to_all x1, waiting for transfers between devices: 0.01 us -> 20.3 us  [local(): lax.all_to_all(send, ('lat', 'lon'), split_axis=0, concat_axis=0, tiled=T...]
    ppermute x2, waiting for transfers between devices: 2.71 us -> 8.17 us  [exchange(): far = lax.ppermute(far, 'lat', next_pair)]
    unnamed x9 -> x5, local copies, waits for them, and re-layouts: 5.13 us -> 0.24 us
    ppermute x2, starting transfers between devices: 11 us -> 6.88 us  [exchange(): far = lax.ppermute(far, 'lat', next_pair)]
    pallas_call x1, Pallas kernels: 13.5 us -> 9.49 us  [start(): pl.pallas_call(functools.partial(start_kernel, devices), out_shape=shapes...]
  transfers between devices with their start and end apart: 9 -> 9, of which waited for: 1 -> 4; matrix products, arithmetic and copies ran while one was open for 0% -> 1% of each run, Pallas kernels for 84% -> 17%
where the time goes in v3:
time: 93.2 us
  Pallas kernels  37.8 us (41%)
  waiting for transfers between devices  29.3 us (31%)
  starting transfers between devices  25 us (27%)
    all_to_all x1, waiting for transfers between devices, local(): lax.all_to_all(send, ('lat', 'lon'), split_axis=0, concat_axis=0, tiled=T...  20.3 us
    all_to_all x1, starting transfers between devices, local(): lax.all_to_all(send, ('lat', 'lon'), split_axis=0, concat_axis=0, tiled=T...  10.5 us
    pallas_call x1, Pallas kernels, start(): pl.pallas_call(functools.partial(start_kernel, devices), out_shape=shapes...  9.49 us
    pallas_call x1, Pallas kernels, prepare(): pl.pallas_call(prepare_kernel, out_shape=jax.ShapeDtypeStruct((parts + SP...  9.01 us
    ppermute x2, waiting for transfers between devices, exchange(): far = lax.ppermute(far, 'lat', next_pair)  8.17 us
    pallas_call x1, Pallas kernels, pack(): pl.pallas_call(functools.partial(pack_kernel, (levels, high, columns, dev...  8.13 us
    ppermute x2, starting transfers between devices, exchange(): far = lax.ppermute(far, 'lat', next_pair)  6.88 us
    ppermute x2, starting transfers between devices, exchange(): pair = lax.ppermute(pair, 'lon', [(i, i ^ 1) for i in range(lon)])  4.31 us
  transfers between devices with their start and end apart: 9, of which 4 were waited for; matrix products, arithmetic and copies ran while one was open for 1% of the time, Pallas kernels for 17%

profile of v3, /device:TPU:8, one launch (start us, length us, event | category | flops | bytes accessed | tf_op | source)
XLA Modules:
  0.0 93.2 jit_solution(14690927531548799066)
XLA Ops:
  0.0 8.1 %shard_map.73 = f32[4224,1,128]{2,1,0:T(1,128)} custom-call(s32[16,128]{1,0:T(8,128)} %bitcast.14, s32[16,128]{1,0:T(8,128)} %bitcast.15, f32[2048,1,128]{2,1,0:T(1,128)} %bitcast.13), custom_call_target="tpu_custom_call" | custom-call | tf_op jit(solution)/shard_map/pallas_call | solution.py:98
  8.1 10.5 %all-to-all-start = ((f32[4224,1,128]{2,1,0:T(1,128)}), f32[4224,1,128]{2,1,0:T(1,128)S(1)}, u32[]{:S(2)}, u32[]{:S(2)}) async-start(f32[4224,1,128]{2,1,0:T(1,128)} %shard_map.73), calls=%async_computation | async-start | bytes 4325376 | tf_op jit(solution)/shard_map/all_to_all | solution.py:497
  18.6 0.0 copy-done.1
  18.6 0.2 copy.10
  18.9 9.0 %shard_map.74.inputs_hbm = f32[16,8,100,512]{3,2,1,0:T(8,128)} custom-call(f32[2,100,8,512]{3,2,1,0:T(8,128)} %bitcast.12, f32[4,100,8,512]{3,2,1,0:T(8,128)} %bitcast.10), custom_call_target="tpu_custom_call" | custom-call | tf_op jit(solution)/shard_map/pallas_call | solution.py:183
  27.9 0.1 pad_add_fusion.odd_ref
  28.0 0.1 subtract_convert_fusion
  28.1 0.4 maximum_maximum_fusion.weight_hbm.weight_ref
  28.5 0.0 copy-start
  28.5 20.3 %all-to-all-done.got_ref = f32[4224,1,128]{2,1,0:T(1,128)S(1)} async-done(((f32[4224,1,128]{2,1,0:T(1,128)}), f32[4224,1,128]{2,1,0:T(1,128)S(1)}, u32[]{:S(2)}, u32[]{:S(2)}) %all-to-all-start) | async-done | bytes 2162720 | tf_op jit(solution)/shard_map/all_to_all | solution.py:497
  48.9 9.5 %shard_map.75 = (f32[2,8,104,512]{3,2,1,0:T(8,128)S(1)}, f32[2,104,512]{2,1,0:T(8,128)S(1)}, f32[2,104,512]{2,1,0:T(8,128)S(1)}, f32[104,128]{1,0:T(8,128)S(1)},...) custom-call(s32[2]{0:T(128)S(1)} %pad_add_fusion.odd_ref, f32[4224,1,128]{2,1,0:T(1,128)S(1)} %all-to-all-done.got_ref, ...), custom_call_target="tpu_custom_call" | custom-call | tf_op jit(solution)/shard_map/pallas_call | solution.py:269
  58.4 4.0 %collective-permute-start = (f32[104,128]{1,0:T(8,128)S(1)}, f32[104,128]{1,0:T(8,128)S(1)}, u32[]{:S(2)}, u32[]{:S(2)}) collective-permute-start(f32[104,128]{1,0:T(8,128)S(1)} %get-tuple-element.19), channel_id=1, source_target_pairs={{0,1},{1,0},{2,3},{3,2},{4,5},{5,4},{6,7},{7,6},{8,9},{9,8},{10,11... | collective-permute-start | bytes 159752 | tf_op jit(solution)/shard_map/ppermute | solution.py:485
  62.4 0.3 collective-permute-start.1
  62.7 0.0 collective-permute-start.2
  62.7 4.3 %collective-permute-start.3 = (f32[2,104,512]{2,1,0:T(8,128)S(1)}, f32[2,104,512]{2,1,0:T(8,128)S(1)}, u32[]{:S(2)}, u32[]{:S(2)}) collective-permute-start(f32[2,104,512]{2,1,0:T(8,128)S(1)} %get-tuple-element.24), channel_id=1, source_target_pairs={{4,8},{8,4},{12,16},{16,12},{20,24},{24,20},{28,32},{32,28},{36,40... | collective-permute-start | bytes 1277960 | tf_op jit(solution)/shard_map/ppermute | solution.py:486
  67.0 0.0 collective-permute-done.pair_ref
  67.0 0.8 collective-permute-done.1.other_ref
  67.7 0.0 copy-done
  67.8 3.3 %shard_map.76 = (f32[2,8,104,512]{3,2,1,0:T(8,128)S(1)}, f32[104,128]{1,0:T(8,128)S(1)}, f32[104,128]{1,0:T(8,128)S(1)}) custom-call(s32[2]{0:T(128)S(1)} %pad_add_fusion.odd_ref, f32[104,128]{1,0:T(8,128)S(1)} %collective-permute-done.pair_ref, f32[104,128]{1,0:T(8,128)S(1)} %collective-permute-done.1.other_ref, ...), custom_call_target="tpu_custom_call" | custom-call | flops 30000001024 | bytes 8000000 | tf_op jit(solution)/shard_map/pallas_call | solution.py:385
  71.1 0.0 collective-permute-done.2.near_in
  71.1 3.2 %collective-permute-done.3.far_in = f32[2,104,512]{2,1,0:T(8,128)S(1)} collective-permute-done((f32[2,104,512]{2,1,0:T(8,128)S(1)}, f32[2,104,512]{2,1,0:T(8,128)S(1)}, u32[]{:S(2)}, u32[]{:S(2)}) %collective-permute-start.3) | collective-permute-done | bytes 426016 | tf_op jit(solution)/shard_map/ppermute | solution.py:486
  74.2 1.7 %shard_map.77 = (f32[2,8,104,512]{3,2,1,0:T(8,128)S(1)}, f32[2,104,512]{2,1,0:T(8,128)S(1)}, f32[2,104,512]{2,1,0:T(8,128)S(1)}, f32[104,128]{1,0:T(8,128)S(1)}, f32[104,128]{1,0:T(8,128)S(1)}) custom-call(s32[2]{0:T(128)S(1)} %pad_add_fusion.odd_ref, f32[104,128]{1,0:T(8,128)S(1)} %collective-permute-done.pair_ref, ...), custom_call_target="tpu_custom_call", output_to_operand_aliasing={{0}: (9, {})} | custom-call | tf_op jit(solution)/shard_map/pallas_call | solution.py:394
  76.0 0.3 collective-permute-start.4
  76.2 3.0 %collective-permute-start.5 = (f32[104,128]{1,0:T(8,128)S(1)}, f32[104,128]{1,0:T(8,128)S(1)}, u32[]{:S(2)}, u32[]{:S(2)}) collective-permute-start(f32[104,128]{1,0:T(8,128)S(1)} %get-tuple-element.29), channel_id=1, source_target_pairs={{0,3},{1,2},{2,1},{3,0},{4,7},{5,6},{6,5},{7,4},{8,11},{9,10},{10,... | collective-permute-start | bytes 159752 | tf_op jit(solution)/shard_map/ppermute | solution.py:484
  79.3 0.0 collective-permute-start.6
  79.3 2.6 %collective-permute-start.7 = (f32[2,104,512]{2,1,0:T(8,128)S(1)}, f32[2,104,512]{2,1,0:T(8,128)S(1)}, u32[]{:S(2)}, u32[]{:S(2)}) collective-permute-start(f32[2,104,512]{2,1,0:T(8,128)S(1)} %get-tuple-element.32), channel_id=1, source_target_pairs={{4,8},{8,4},{12,16},{16,12},{20,24},{24,20},{28,32},{32,28},{36,40... | collective-permute-start | bytes 1277960 | tf_op jit(solution)/shard_map/ppermute | solution.py:486
  81.9 0.0 collective-permute-done.4.pair_ref
  81.9 0.0 collective-permute-done.5.other_ref
  81.9 3.9 %shard_map.78.part_ref = f32[2,100,8,512]{3,2,1,0:T(8,128)} custom-call(s32[2]{0:T(128)S(1)} %pad_add_fusion.odd_ref, f32[104,128]{1,0:T(8,128)S(1)} %collective-permute-done.4.pair_ref, f32[104,128]{1,0:T(8,128)S(1)} %collective-permute-done.5.other_ref, f32[2,8,104,512]{3,2,1,0:T(8,128)S(1)} %get-tuple-element.30.field, ...), custom_call_target="tpu_custom_call" | custom-call | flops 30000001024 | bytes 8000000 | tf_op jit(solution)/shard_map/pallas_call | solution.py:449
  85.8 0.0 collective-permute-done.6.near_in
  85.8 5.0 %collective-permute-done.7.far_in = f32[2,104,512]{2,1,0:T(8,128)S(1)} collective-permute-done((f32[2,104,512]{2,1,0:T(8,128)S(1)}, f32[2,104,512]{2,1,0:T(8,128)S(1)}, u32[]{:S(2)}, u32[]{:S(2)}) %collective-permute-start.7) | collective-permute-done | bytes 426016 | tf_op jit(solution)/shard_map/ppermute | solution.py:486
  90.8 2.2 %shard_map.79 = f32[2,100,8,512]{3,2,1,0:T(8,128)} custom-call(s32[2]{0:T(128)S(1)} %pad_add_fusion.odd_ref, f32[104,128]{1,0:T(8,128)S(1)} %collective-permute-done.4.pair_ref, f32[104,128]{1,0:T(8,128)S(1)} %collective-permute-done.5.other_ref, f32[2,8,104,512]{3,2,1,0:T(8,128)S(1)} %get-tuple-element.30.field, ...), custom_call_target="tpu_custom_call", output_to_operand_aliasing={{}: (8, {})} | custom-call | tf_op jit(solution)/shard_map/pallas_call | solution.py:458
  (3 shorter events, 0.1 us)
Async XLA Ops:
  0.0 18.6 %copy-start.1 = (f32[8,100,100]{2,0,1:T(8,128)S(1)}, f32[8,100,100]{2,0,1:T(8,128)}, u32[]{:S(2)}) copy-start(f32[8,100,100]{2,0,1:T(8,128)} %param.9) | copy-start | bytes 960004
  8.1 40.7 %all-to-all-start = ((f32[4224,1,128]{2,1,0:T(1,128)}), f32[4224,1,128]{2,1,0:T(1,128)S(1)}, u32[]{:S(2)}, u32[]{:S(2)}) async-start(f32[4224,1,128]{2,1,0:T(1,128)} %shard_map.73), calls=%async_computation | async-start | bytes 4325376 | tf_op jit(solution)/shard_map/all_to_all | solution.py:497
  28.5 39.3 %copy-start = (s32[8,512]{1,0:T(8,128)S(1)}, s32[8,512]{1,0:T(8,128)}, u32[]{:S(2)}) copy-start(s32[8,512]{1,0:T(8,128)} %mask_ref.7) | copy-start | bytes 49156
  58.4 8.6 %collective-permute-start = (f32[104,128]{1,0:T(8,128)S(1)}, f32[104,128]{1,0:T(8,128)S(1)}, u32[]{:S(2)}, u32[]{:S(2)}) collective-permute-start(f32[104,128]{1,0:T(8,128)S(1)} %get-tuple-element.19), channel_id=1, source_target_pairs={{0,1},{1,0},{2,3},{3,2},{4,5},{5,4},{6,7},{7,6},{8,9},{9,8},{10,11... | collective-permute-start | bytes 159752 | tf_op jit(solution)/shard_map/ppermute | solution.py:485
  62.4 5.3 %collective-permute-start.1 = (f32[104,128]{1,0:T(8,128)S(1)}, f32[104,128]{1,0:T(8,128)S(1)}, u32[]{:S(2)}, u32[]{:S(2)}) collective-permute-start(f32[104,128]{1,0:T(8,128)S(1)} %get-tuple-element.20), channel_id=1, source_target_pairs={{0,3},{1,2},{2,1},{3,0},{4,7},{5,6},{6,5},{7,4},{8,11},{9,10},{10,... | collective-permute-start | bytes 159752 | tf_op jit(solution)/shard_map/ppermute | solution.py:484
  62.7 8.4 %collective-permute-start.2 = (f32[2,104,512]{2,1,0:T(8,128)S(1)}, f32[2,104,512]{2,1,0:T(8,128)S(1)}, u32[]{:S(2)}, u32[]{:S(2)}) collective-permute-start(f32[2,104,512]{2,1,0:T(8,128)S(1)} %get-tuple-element.23), channel_id=1, source_target_pairs={{0,4},{4,0},{8,12},{12,8},{16,20},{20,16},{24,28},{28,24},{32,36},... | collective-permute-start | bytes 1277960 | tf_op jit(solution)/shard_map/ppermute | solution.py:487
  62.7 11.5 %collective-permute-start.3 = (f32[2,104,512]{2,1,0:T(8,128)S(1)}, f32[2,104,512]{2,1,0:T(8,128)S(1)}, u32[]{:S(2)}, u32[]{:S(2)}) collective-permute-start(f32[2,104,512]{2,1,0:T(8,128)S(1)} %get-tuple-element.24), channel_id=1, source_target_pairs={{4,8},{8,4},{12,16},{16,12},{20,24},{24,20},{28,32},{32,28},{36,40... | collective-permute-start | bytes 1277960 | tf_op jit(solution)/shard_map/ppermute | solution.py:486
  76.0 5.9 %collective-permute-start.4 = (f32[104,128]{1,0:T(8,128)S(1)}, f32[104,128]{1,0:T(8,128)S(1)}, u32[]{:S(2)}, u32[]{:S(2)}) collective-permute-start(f32[104,128]{1,0:T(8,128)S(1)} %get-tuple-element.28), channel_id=1, source_target_pairs={{0,1},{1,0},{2,3},{3,2},{4,5},{5,4},{6,7},{7,6},{8,9},{9,8},{10,11... | collective-permute-start | bytes 159752 | tf_op jit(solution)/shard_map/ppermute | solution.py:485
  76.2 5.7 %collective-permute-start.5 = (f32[104,128]{1,0:T(8,128)S(1)}, f32[104,128]{1,0:T(8,128)S(1)}, u32[]{:S(2)}, u32[]{:S(2)}) collective-permute-start(f32[104,128]{1,0:T(8,128)S(1)} %get-tuple-element.29), channel_id=1, source_target_pairs={{0,3},{1,2},{2,1},{3,0},{4,7},{5,6},{6,5},{7,4},{8,11},{9,10},{10,... | collective-permute-start | bytes 159752 | tf_op jit(solution)/shard_map/ppermute | solution.py:484
  79.3 6.5 %collective-permute-start.6 = (f32[2,104,512]{2,1,0:T(8,128)S(1)}, f32[2,104,512]{2,1,0:T(8,128)S(1)}, u32[]{:S(2)}, u32[]{:S(2)}) collective-permute-start(f32[2,104,512]{2,1,0:T(8,128)S(1)} %get-tuple-element.31), channel_id=1, source_target_pairs={{0,4},{4,0},{8,12},{12,8},{16,20},{20,16},{24,28},{28,24},{32,36},... | collective-permute-start | bytes 1277960 | tf_op jit(solution)/shard_map/ppermute | solution.py:487
  79.3 11.5 %collective-permute-start.7 = (f32[2,104,512]{2,1,0:T(8,128)S(1)}, f32[2,104,512]{2,1,0:T(8,128)S(1)}, u32[]{:S(2)}, u32[]{:S(2)}) collective-permute-start(f32[2,104,512]{2,1,0:T(8,128)S(1)} %get-tuple-element.32), channel_id=1, source_target_pairs={{4,8},{8,4},{12,16},{16,12},{20,24},{24,20},{28,32},{32,28},{36,40... | collective-permute-start | bytes 1277960 | tf_op jit(solution)/shard_map/ppermute | solution.py:486

commit v4 on v3

--- a/solution.py
+++ b/solution.py
@@ -362,7 +362,7 @@
         east[strip, :] = last
 
 
-def edge_kernel(levels, odd_ref, pair_ref, other_ref, field, courant_ref, mask_ref, weight_ref, near_in, far_in,
+def edge_kernel(levels, odd_ref, pair_ref, other_ref, field, courant_ref, mask_ref, weight_ref, far_in, near_in,
                 part_ref, west, east, out_ref, near_ref, far_ref, pair_out, other_out, hw, he, state):
     ends_in_place(odd_ref, pair_ref, other_ref, hw, he)
     rows_done = (0, field.shape[1] - 1)
@@ -399,7 +399,7 @@
         scratch_shapes=scratch,
         input_output_aliases={9: 0},
         compiler_params=params,
-    )(odd, pair, other, field, courant, mask, weight, near, far, part, west, east)
+    )(odd, pair, other, field, courant, mask, weight, far, near, part, west, east)
 
 
 def finish(rows_done, levels, lat, field, courant_ref, mask_ref, hw, he, out_ref, state, sems):
@@ -428,7 +428,7 @@
     finish(rows_done, levels, None, field, courant_ref, mask_ref, hw, he, out_ref, state, sems)
 
 
-def final_edge_kernel(levels, odd_ref, pair_ref, other_ref, field, courant_ref, mask_ref, near_in, far_in, part_ref,
+def final_edge_kernel(levels, odd_ref, pair_ref, other_ref, field, courant_ref, mask_ref, far_in, near_in, part_ref,
                       out_ref, hw, he, state, sems):
     ends_in_place(odd_ref, pair_ref, other_ref, hw, he)
     lat = by_side(odd_ref, near_in, far_in)
@@ -463,7 +463,7 @@
         scratch_shapes=scratch,
         input_output_aliases={8: 0},
         compiler_params=params,
-    )(odd, pair, other, field, courant, mask, near, far, part)
+    )(odd, pair, other, field, courant, mask, far, near, part)
 
 
 def weights(inverse, high):

time: 93.2 us -> 93.4 us (level)
  waiting for transfers between devices: 29.3 us -> 31.2 us
  starting transfers between devices: 25 us -> 23.6 us
    ppermute x2, waiting for transfers between devices: 0.78 us -> 3.58 us  [exchange(): lax.ppermute(other, 'lon', [(i, (i + 1 if i % 2 else i - 1) % lon) for i...]
    ppermute x2, starting transfers between devices: 6.88 us -> 4.87 us  [exchange(): far = lax.ppermute(far, 'lat', next_pair)]
    ppermute x2, starting transfers between devices: 4.31 us -> 6.14 us  [exchange(): pair = lax.ppermute(pair, 'lon', [(i, i ^ 1) for i in range(lon)])]
    ppermute x2, starting transfers between devices: 3.31 us -> 2.01 us  [exchange(): lax.ppermute(other, 'lon', [(i, (i + 1 if i % 2 else i - 1) % lon) for i...]
    ppermute x2, waiting for transfers between devices: 8.17 us -> 7.22 us  [exchange(): far = lax.ppermute(far, 'lat', next_pair)]
  transfers between devices with their start and end apart: 9 -> 9, of which waited for: 4 -> 5; matrix products, arithmetic and copies ran while one was open for 1% -> 1% of each run, Pallas kernels for 17% -> 17%
where the time goes in v4:
time: 93.4 us; the launch traced here: 93.2 us
  Pallas kernels  37.3 us (40%)
  waiting for transfers between devices  31.2 us (33%)
  starting transfers between devices  23.6 us (25%)
    all_to_all x1, waiting for transfers between devices, local(): lax.all_to_all(send, ('lat', 'lon'), split_axis=0, concat_axis=0, tiled=T...  20.3 us
    all_to_all x1, starting transfers between devices, local(): lax.all_to_all(send, ('lat', 'lon'), split_axis=0, concat_axis=0, tiled=T...  10.5 us
    pallas_call x1, Pallas kernels, prepare(): pl.pallas_call(prepare_kernel, out_shape=jax.ShapeDtypeStruct((parts + SP...  9.01 us
    pallas_call x1, Pallas kernels, start(): pl.pallas_call(functools.partial(start_kernel, devices), out_shape=shapes...  8.99 us
    pallas_call x1, Pallas kernels, pack(): pl.pallas_call(functools.partial(pack_kernel, (levels, high, columns, dev...  8.13 us
    ppermute x2, waiting for transfers between devices, exchange(): far = lax.ppermute(far, 'lat', next_pair)  7.22 us
    ppermute x2, starting transfers between devices, exchange(): pair = lax.ppermute(pair, 'lon', [(i, i ^ 1) for i in range(lon)])  6.14 us
    ppermute x2, starting transfers between devices, exchange(): far = lax.ppermute(far, 'lat', next_pair)  4.87 us
  transfers between devices with their start and end apart: 9, of which 5 were waited for; matrix products, arithmetic and copies ran while one was open for 1% of the time, Pallas kernels for 17%

profile of v4, /device:TPU:8, one launch (start us, length us, event | category | flops | bytes accessed | tf_op | source)
XLA Modules:
  0.0 93.2 jit_solution(13640234789722879749)
XLA Ops:
  0.0 8.1 %shard_map.73 = f32[4224,1,128]{2,1,0:T(1,128)} custom-call(s32[16,128]{1,0:T(8,128)} %bitcast.14, s32[16,128]{1,0:T(8,128)} %bitcast.15, f32[2048,1,128]{2,1,0:T(1,128)} %bitcast.13), custom_call_target="tpu_custom_call" | custom-call | tf_op jit(solution)/shard_map/pallas_call | solution.py:98
  8.1 10.5 %all-to-all-start = ((f32[4224,1,128]{2,1,0:T(1,128)}), f32[4224,1,128]{2,1,0:T(1,128)S(1)}, u32[]{:S(2)}, u32[]{:S(2)}) async-start(f32[4224,1,128]{2,1,0:T(1,128)} %shard_map.73), calls=%async_computation | async-start | bytes 4325376 | tf_op jit(solution)/shard_map/all_to_all | solution.py:497
  18.6 0.0 copy-done.1
  18.6 0.2 copy.10
  18.9 9.0 %shard_map.74.inputs_hbm = f32[16,8,100,512]{3,2,1,0:T(8,128)} custom-call(f32[2,100,8,512]{3,2,1,0:T(8,128)} %bitcast.12, f32[4,100,8,512]{3,2,1,0:T(8,128)} %bitcast.10), custom_call_target="tpu_custom_call" | custom-call | tf_op jit(solution)/shard_map/pallas_call | solution.py:183
  27.9 0.1 pad_add_fusion.odd_ref
  28.0 0.1 subtract_convert_fusion
  28.1 0.4 maximum_maximum_fusion.weight_hbm.weight_ref
  28.5 0.0 copy-start
  28.5 20.3 %all-to-all-done.got_ref = f32[4224,1,128]{2,1,0:T(1,128)S(1)} async-done(((f32[4224,1,128]{2,1,0:T(1,128)}), f32[4224,1,128]{2,1,0:T(1,128)S(1)}, u32[]{:S(2)}, u32[]{:S(2)}) %all-to-all-start) | async-done | bytes 2162720 | tf_op jit(solution)/shard_map/all_to_all | solution.py:497
  48.9 9.0 %shard_map.75 = (f32[2,8,104,512]{3,2,1,0:T(8,128)S(1)}, f32[2,104,512]{2,1,0:T(8,128)S(1)}, f32[2,104,512]{2,1,0:T(8,128)S(1)}, f32[104,128]{1,0:T(8,128)S(1)},...) custom-call(s32[2]{0:T(128)S(1)} %pad_add_fusion.odd_ref, f32[4224,1,128]{2,1,0:T(1,128)S(1)} %all-to-all-done.got_ref, ...), custom_call_target="tpu_custom_call" | custom-call | tf_op jit(solution)/shard_map/pallas_call | solution.py:269
  57.9 4.6 %collective-permute-start = (f32[104,128]{1,0:T(8,128)S(1)}, f32[104,128]{1,0:T(8,128)S(1)}, u32[]{:S(2)}, u32[]{:S(2)}) collective-permute-start(f32[104,128]{1,0:T(8,128)S(1)} %get-tuple-element.19), channel_id=1, source_target_pairs={{0,1},{1,0},{2,3},{3,2},{4,5},{5,4},{6,7},{7,6},{8,9},{9,8},{10,11... | collective-permute-start | bytes 159752 | tf_op jit(solution)/shard_map/ppermute | solution.py:485
  62.4 0.3 collective-permute-start.1
  62.7 3.0 %collective-permute-start.2 = (f32[2,104,512]{2,1,0:T(8,128)S(1)}, f32[2,104,512]{2,1,0:T(8,128)S(1)}, u32[]{:S(2)}, u32[]{:S(2)}) collective-permute-start(f32[2,104,512]{2,1,0:T(8,128)S(1)} %get-tuple-element.23), channel_id=1, source_target_pairs={{4,8},{8,4},{12,16},{16,12},{20,24},{24,20},{28,32},{32,28},{36,40... | collective-permute-start | bytes 1277960 | tf_op jit(solution)/shard_map/ppermute | solution.py:486
  65.7 0.1 collective-permute-start.3
  65.8 0.0 collective-permute-done.pair_ref
  65.8 2.0 %collective-permute-done.1.other_ref = f32[104,128]{1,0:T(8,128)S(1)} collective-permute-done((f32[104,128]{1,0:T(8,128)S(1)}, f32[104,128]{1,0:T(8,128)S(1)}, u32[]{:S(2)}, u32[]{:S(2)}) %collective-permute-start.1) | collective-permute-done | bytes 53280 | tf_op jit(solution)/shard_map/ppermute | solution.py:484
  67.8 0.0 copy-done
  67.8 3.3 %shard_map.76 = (f32[2,8,104,512]{3,2,1,0:T(8,128)S(1)}, f32[104,128]{1,0:T(8,128)S(1)}, f32[104,128]{1,0:T(8,128)S(1)}) custom-call(s32[2]{0:T(128)S(1)} %pad_add_fusion.odd_ref, f32[104,128]{1,0:T(8,128)S(1)} %collective-permute-done.pair_ref, f32[104,128]{1,0:T(8,128)S(1)} %collective-permute-done.1.other_ref, ...), custom_call_target="tpu_custom_call" | custom-call | flops 30000001024 | bytes 8000000 | tf_op jit(solution)/shard_map/pallas_call | solution.py:385
  71.1 3.2 %collective-permute-done.2.far_in = f32[2,104,512]{2,1,0:T(8,128)S(1)} collective-permute-done((f32[2,104,512]{2,1,0:T(8,128)S(1)}, f32[2,104,512]{2,1,0:T(8,128)S(1)}, u32[]{:S(2)}, u32[]{:S(2)}) %collective-permute-start.2) | collective-permute-done | bytes 426016 | tf_op jit(solution)/shard_map/ppermute | solution.py:486
  74.2 0.0 collective-permute-done.3.near_in
  74.2 1.7 %shard_map.77 = (f32[2,8,104,512]{3,2,1,0:T(8,128)S(1)}, f32[2,104,512]{2,1,0:T(8,128)S(1)}, f32[2,104,512]{2,1,0:T(8,128)S(1)}, f32[104,128]{1,0:T(8,128)S(1)}, f32[104,128]{1,0:T(8,128)S(1)}) custom-call(s32[2]{0:T(128)S(1)} %pad_add_fusion.odd_ref, f32[104,128]{1,0:T(8,128)S(1)} %collective-permute-done.pair_ref, ...), custom_call_target="tpu_custom_call", output_to_operand_aliasing={{0}: (9, {})} | custom-call | tf_op jit(solution)/shard_map/pallas_call | solution.py:394
  76.0 1.6 %collective-permute-start.4 = (f32[104,128]{1,0:T(8,128)S(1)}, f32[104,128]{1,0:T(8,128)S(1)}, u32[]{:S(2)}, u32[]{:S(2)}) collective-permute-start(f32[104,128]{1,0:T(8,128)S(1)} %get-tuple-element.28), channel_id=1, source_target_pairs={{0,1},{1,0},{2,3},{3,2},{4,5},{5,4},{6,7},{7,6},{8,9},{9,8},{10,11... | collective-permute-start | bytes 159752 | tf_op jit(solution)/shard_map/ppermute | solution.py:485
  77.5 1.7 %collective-permute-start.5 = (f32[104,128]{1,0:T(8,128)S(1)}, f32[104,128]{1,0:T(8,128)S(1)}, u32[]{:S(2)}, u32[]{:S(2)}) collective-permute-start(f32[104,128]{1,0:T(8,128)S(1)} %get-tuple-element.29), channel_id=1, source_target_pairs={{0,3},{1,2},{2,1},{3,0},{4,7},{5,6},{6,5},{7,4},{8,11},{9,10},{10,... | collective-permute-start | bytes 159752 | tf_op jit(solution)/shard_map/ppermute | solution.py:484
  79.3 1.9 %collective-permute-start.6 = (f32[2,104,512]{2,1,0:T(8,128)S(1)}, f32[2,104,512]{2,1,0:T(8,128)S(1)}, u32[]{:S(2)}, u32[]{:S(2)}) collective-permute-start(f32[2,104,512]{2,1,0:T(8,128)S(1)} %get-tuple-element.31), channel_id=1, source_target_pairs={{4,8},{8,4},{12,16},{16,12},{20,24},{24,20},{28,32},{32,28},{36,40... | collective-permute-start | bytes 1277960 | tf_op jit(solution)/shard_map/ppermute | solution.py:486
  81.2 0.1 collective-permute-start.7
  81.3 0.0 collective-permute-done.4.pair_ref
  81.3 1.6 %collective-permute-done.5.other_ref = f32[104,128]{1,0:T(8,128)S(1)} collective-permute-done((f32[104,128]{1,0:T(8,128)S(1)}, f32[104,128]{1,0:T(8,128)S(1)}, u32[]{:S(2)}, u32[]{:S(2)}) %collective-permute-start.5) | collective-permute-done | bytes 53280 | tf_op jit(solution)/shard_map/ppermute | solution.py:484
  82.9 3.9 %shard_map.78.part_ref = f32[2,100,8,512]{3,2,1,0:T(8,128)} custom-call(s32[2]{0:T(128)S(1)} %pad_add_fusion.odd_ref, f32[104,128]{1,0:T(8,128)S(1)} %collective-permute-done.4.pair_ref, f32[104,128]{1,0:T(8,128)S(1)} %collective-permute-done.5.other_ref, f32[2,8,104,512]{3,2,1,0:T(8,128)S(1)} %get-tuple-element.30.field, ...), custom_call_target="tpu_custom_call" | custom-call | flops 30000001024 | bytes 8000000 | tf_op jit(solution)/shard_map/pallas_call | solution.py:449
  86.8 4.1 %collective-permute-done.6.far_in = f32[2,104,512]{2,1,0:T(8,128)S(1)} collective-permute-done((f32[2,104,512]{2,1,0:T(8,128)S(1)}, f32[2,104,512]{2,1,0:T(8,128)S(1)}, u32[]{:S(2)}, u32[]{:S(2)}) %collective-permute-start.6) | collective-permute-done | bytes 426016 | tf_op jit(solution)/shard_map/ppermute | solution.py:486
  90.8 0.0 collective-permute-done.7.near_in
  90.8 2.2 %shard_map.79 = f32[2,100,8,512]{3,2,1,0:T(8,128)} custom-call(s32[2]{0:T(128)S(1)} %pad_add_fusion.odd_ref, f32[104,128]{1,0:T(8,128)S(1)} %collective-permute-done.4.pair_ref, f32[104,128]{1,0:T(8,128)S(1)} %collective-permute-done.5.other_ref, f32[2,8,104,512]{3,2,1,0:T(8,128)S(1)} %get-tuple-element.30.field, ...), custom_call_target="tpu_custom_call", output_to_operand_aliasing={{}: (8, {})} | custom-call | tf_op jit(solution)/shard_map/pallas_call | solution.py:458
  (3 shorter events, 0.1 us)
Async XLA Ops:
  0.0 18.6 %copy-start.1 = (f32[8,100,100]{2,0,1:T(8,128)S(1)}, f32[8,100,100]{2,0,1:T(8,128)}, u32[]{:S(2)}) copy-start(f32[8,100,100]{2,0,1:T(8,128)} %param.9) | copy-start | bytes 960004
  8.1 40.7 %all-to-all-start = ((f32[4224,1,128]{2,1,0:T(1,128)}), f32[4224,1,128]{2,1,0:T(1,128)S(1)}, u32[]{:S(2)}, u32[]{:S(2)}) async-start(f32[4224,1,128]{2,1,0:T(1,128)} %shard_map.73), calls=%async_computation | async-start | bytes 4325376 | tf_op jit(solution)/shard_map/all_to_all | solution.py:497
  28.5 39.3 %copy-start = (s32[8,512]{1,0:T(8,128)S(1)}, s32[8,512]{1,0:T(8,128)}, u32[]{:S(2)}) copy-start(s32[8,512]{1,0:T(8,128)} %mask_ref.7) | copy-start | bytes 49156
  57.9 7.9 %collective-permute-start = (f32[104,128]{1,0:T(8,128)S(1)}, f32[104,128]{1,0:T(8,128)S(1)}, u32[]{:S(2)}, u32[]{:S(2)}) collective-permute-start(f32[104,128]{1,0:T(8,128)S(1)} %get-tuple-element.19), channel_id=1, source_target_pairs={{0,1},{1,0},{2,3},{3,2},{4,5},{5,4},{6,7},{7,6},{8,9},{9,8},{10,11... | collective-permute-start | bytes 159752 | tf_op jit(solution)/shard_map/ppermute | solution.py:485
  62.4 5.3 %collective-permute-start.1 = (f32[104,128]{1,0:T(8,128)S(1)}, f32[104,128]{1,0:T(8,128)S(1)}, u32[]{:S(2)}, u32[]{:S(2)}) collective-permute-start(f32[104,128]{1,0:T(8,128)S(1)} %get-tuple-element.20), channel_id=1, source_target_pairs={{0,3},{1,2},{2,1},{3,0},{4,7},{5,6},{6,5},{7,4},{8,11},{9,10},{10,... | collective-permute-start | bytes 159752 | tf_op jit(solution)/shard_map/ppermute | solution.py:484
  62.7 11.5 %collective-permute-start.2 = (f32[2,104,512]{2,1,0:T(8,128)S(1)}, f32[2,104,512]{2,1,0:T(8,128)S(1)}, u32[]{:S(2)}, u32[]{:S(2)}) collective-permute-start(f32[2,104,512]{2,1,0:T(8,128)S(1)} %get-tuple-element.23), channel_id=1, source_target_pairs={{4,8},{8,4},{12,16},{16,12},{20,24},{24,20},{28,32},{32,28},{36,40... | collective-permute-start | bytes 1277960 | tf_op jit(solution)/shard_map/ppermute | solution.py:486
  65.7 8.6 %collective-permute-start.3 = (f32[2,104,512]{2,1,0:T(8,128)S(1)}, f32[2,104,512]{2,1,0:T(8,128)S(1)}, u32[]{:S(2)}, u32[]{:S(2)}) collective-permute-start(f32[2,104,512]{2,1,0:T(8,128)S(1)} %get-tuple-element.24), channel_id=1, source_target_pairs={{0,4},{4,0},{8,12},{12,8},{16,20},{20,16},{24,28},{28,24},{32,36},... | collective-permute-start | bytes 1277960 | tf_op jit(solution)/shard_map/ppermute | solution.py:487
  76.0 5.3 %collective-permute-start.4 = (f32[104,128]{1,0:T(8,128)S(1)}, f32[104,128]{1,0:T(8,128)S(1)}, u32[]{:S(2)}, u32[]{:S(2)}) collective-permute-start(f32[104,128]{1,0:T(8,128)S(1)} %get-tuple-element.28), channel_id=1, source_target_pairs={{0,1},{1,0},{2,3},{3,2},{4,5},{5,4},{6,7},{7,6},{8,9},{9,8},{10,11... | collective-permute-start | bytes 159752 | tf_op jit(solution)/shard_map/ppermute | solution.py:485
  77.5 5.3 %collective-permute-start.5 = (f32[104,128]{1,0:T(8,128)S(1)}, f32[104,128]{1,0:T(8,128)S(1)}, u32[]{:S(2)}, u32[]{:S(2)}) collective-permute-start(f32[104,128]{1,0:T(8,128)S(1)} %get-tuple-element.29), channel_id=1, source_target_pairs={{0,3},{1,2},{2,1},{3,0},{4,7},{5,6},{6,5},{7,4},{8,11},{9,10},{10,... | collective-permute-start | bytes 159752 | tf_op jit(solution)/shard_map/ppermute | solution.py:484
  79.3 11.5 %collective-permute-start.6 = (f32[2,104,512]{2,1,0:T(8,128)S(1)}, f32[2,104,512]{2,1,0:T(8,128)S(1)}, u32[]{:S(2)}, u32[]{:S(2)}) collective-permute-start(f32[2,104,512]{2,1,0:T(8,128)S(1)} %get-tuple-element.31), channel_id=1, source_target_pairs={{4,8},{8,4},{12,16},{16,12},{20,24},{24,20},{28,32},{32,28},{36,40... | collective-permute-start | bytes 1277960 | tf_op jit(solution)/shard_map/ppermute | solution.py:486
  81.2 9.6 %collective-permute-start.7 = (f32[2,104,512]{2,1,0:T(8,128)S(1)}, f32[2,104,512]{2,1,0:T(8,128)S(1)}, u32[]{:S(2)}, u32[]{:S(2)}) collective-permute-start(f32[2,104,512]{2,1,0:T(8,128)S(1)} %get-tuple-element.32), channel_id=1, source_target_pairs={{0,4},{4,0},{8,12},{12,8},{16,20},{20,16},{24,28},{28,24},{32,36},... | collective-permute-start | bytes 1277960 | tf_op jit(solution)/shard_map/ppermute | solution.py:487

commit v5 on v4

--- a/solution.py
+++ b/solution.py
@@ -326,18 +326,25 @@
     return [mask_ref[j : j + 1, c : c + LANES].astype(jnp.float32) for c in range(0, wide, LANES)]
 
 
-def by_side(odd_ref, near_ref, far_ref):
-    odd = odd_ref[0] != 0
-    north = lambda t, strip, tile: jnp.where(odd, far_ref[t, strip, tile], near_ref[t, strip, tile])
-    south = lambda t, strip, tile: jnp.where(odd, near_ref[t, strip, tile], far_ref[t, strip, tile])
-    return north, south
-
-
-def advance(rows_done, levels, lat, field, courant_ref, mask_ref, hw, he, weight_ref, out_ref, state):
+def beyond(halo_ref):
+    read = lambda t, strip, tile: halo_ref[t, strip, tile]
+    return read, read
+
+
+def each_row(odd_ref, rows, inner, near, do):
+    if inner:
+        for j in range(1, rows - 1):
+            do(j)
+    for j in (0, rows - 1):
+        pl.when((odd_ref[0] != 0) == ((j == 0) == near))(functools.partial(do, j))
+
+
+def advance(levels, lat, field, courant_ref, mask_ref, hw, he, weight_ref, out_ref, state):
     tracers, rows, high, wide = field.shape
     for slot in range(state.shape[0]):
         state[slot, levels:high, :] = jnp.zeros((high - levels, wide), jnp.float32)
-    for j in rows_done:
+
+    def do(j):
         mask = mask_row(mask_ref, j)
         weight = weight_ref[j]
         for t in range(tracers):
@@ -348,31 +355,33 @@
 
             transported(t, j, levels, field, courant_ref, mask, lat, hw, he, store)
             for at in range(0, wide, 2 * LANES):
-                level = vertical(weight, state[slot, :, at : at + 2 * LANES])
-                out_ref[t, j, :, at : at + 2 * LANES] = level
-
-
-def inner_kernel(levels, odd_ref, pair_ref, other_ref, field, courant_ref, mask_ref, weight_ref,
+                out_ref[t, j, :, at : at + 2 * LANES] = vertical(weight, state[slot, :, at : at + 2 * LANES])
+
+    return do
+
+
+def inner_kernel(levels, odd_ref, pair_ref, other_ref, field, courant_ref, mask_ref, weight_ref, near_in,
                  out_ref, west, east, hw, he, state):
     ends_in_place(odd_ref, pair_ref, other_ref, hw, he)
-    rows_done = range(1, field.shape[1] - 1)
-    advance(rows_done, levels, None, field, courant_ref, mask_ref, hw, he, weight_ref, out_ref, state)
-    for strip, first, last in collect_ends(rows_done, out_ref, no_ends):
+    rows = field.shape[1]
+    do = advance(levels, beyond(near_in), field, courant_ref, mask_ref, hw, he, weight_ref, out_ref, state)
+    each_row(odd_ref, rows, True, True, do)
+    for strip, first, last in collect_ends(range(1, rows - 1), out_ref, no_ends):
         west[strip, :] = first
         east[strip, :] = last
 
 
-def edge_kernel(levels, odd_ref, pair_ref, other_ref, field, courant_ref, mask_ref, weight_ref, far_in, near_in,
+def edge_kernel(levels, odd_ref, pair_ref, other_ref, field, courant_ref, mask_ref, weight_ref, far_in,
                 part_ref, west, east, out_ref, near_ref, far_ref, pair_out, other_out, hw, he, state):
     ends_in_place(odd_ref, pair_ref, other_ref, hw, he)
-    rows_done = (0, field.shape[1] - 1)
-    lat = by_side(odd_ref, near_in, far_in)
-    advance(rows_done, levels, lat, field, courant_ref, mask_ref, hw, he, weight_ref, out_ref, state)
+    rows = field.shape[1]
+    do = advance(levels, beyond(far_in), field, courant_ref, mask_ref, hw, he, weight_ref, out_ref, state)
+    each_row(odd_ref, rows, False, False, do)
     before = lambda strip: (west[strip, :], east[strip, :])
-    hand_out(odd_ref, out_ref, rows_done, before, near_ref, far_ref, pair_out, other_out)
-
-
-COST = pl.CostEstimate(flops=30_000_000_000, bytes_accessed=8_000_000, transcendentals=0)
+    hand_out(odd_ref, out_ref, (0, rows - 1), before, near_ref, far_ref, pair_out, other_out)
+
+
+COST = pl.CostEstimate(flops=3_000_000_000, bytes_accessed=8_000_000, transcendentals=0)
 
 
 def step(levels, odd, field, courant, mask, weight, halos):
@@ -385,61 +394,70 @@
     part, west, east = pl.pallas_call(
         functools.partial(inner_kernel, levels),
         out_shape=(field_shape, end, end),
-        in_specs=[SMEM] + [VMEM] * 6,
+        in_specs=[SMEM] + [VMEM] * 7,
         out_specs=(VMEM,) * 3,
         scratch_shapes=scratch,
         compiler_params=params,
         cost_estimate=COST,
-    )(odd, pair, other, field, courant, mask, weight)
+    )(odd, pair, other, field, courant, mask, weight, near)
     return pl.pallas_call(
         functools.partial(edge_kernel, levels),
         out_shape=(field_shape, edge, edge, end, end),
-        in_specs=[SMEM] + [VMEM] * 11,
+        in_specs=[SMEM] + [VMEM] * 10,
         out_specs=(VMEM,) * 5,
         scratch_shapes=scratch,
-        input_output_aliases={9: 0},
+        input_output_aliases={8: 0},
         compiler_params=params,
-    )(odd, pair, other, field, courant, mask, weight, far, near, part, west, east)
-
-
-def finish(rows_done, levels, lat, field, courant_ref, mask_ref, hw, he, out_ref, state, sems):
-    tracers = field.shape[0]
+    )(odd, pair, other, field, courant, mask, weight, far, part, west, east)
+
+
+def finish(levels, lat, field, courant_ref, mask_ref, hw, he, out_ref, state, sems, flying=None):
+    tracers, rows = field.shape[:2]
     slots = state.shape[0]
-    flying = {}
-    for k, (j, t) in enumerate((j, t) for j in rows_done for t in range(tracers)):
-        slot = k % slots
-        if slot in flying:
-            flying.pop(slot).wait()
-
-        def store(strip, tile, value):
-            state[slot, strip, tile] = value
-
-        transported(t, j, levels, field, courant_ref, mask_row(mask_ref, j), lat, hw, he, store)
-        copy = pltpu.make_async_copy(state.at[slot], out_ref.at[t, :, j, :], sems.at[slot])
-        copy.start()
-        flying[slot] = copy
-    for copy in flying.values():
+
+    def do(j):
+        started = []
+        for t in range(tracers):
+            slot = (j * tracers + t) % slots
+
+            def store(strip, tile, value):
+                state[slot, strip, tile] = value
+
+            transported(t, j, levels, field, courant_ref, mask_row(mask_ref, j), lat, hw, he, store)
+            copy = pltpu.make_async_copy(state.at[slot], out_ref.at[t, :, j, :], sems.at[slot])
+            copy.start()
+            started.append(copy)
+        if flying is not None and 0 < j < rows - 1:
+            flying.extend(started)
+        else:
+            for copy in started:
+                copy.wait()
+
+    return do
+
+
+def final_inner_kernel(levels, odd_ref, pair_ref, other_ref, field, courant_ref, mask_ref, near_in, out_ref, hw, he, state,
+                       sems):
+    ends_in_place(odd_ref, pair_ref, other_ref, hw, he)
+    flying = []
+    do = finish(levels, beyond(near_in), field, courant_ref, mask_ref, hw, he, out_ref, state, sems, flying)
+    each_row(odd_ref, field.shape[1], True, True, do)
+    for copy in flying:
         copy.wait()
 
 
-def final_inner_kernel(levels, odd_ref, pair_ref, other_ref, field, courant_ref, mask_ref, out_ref, hw, he, state, sems):
-    ends_in_place(odd_ref, pair_ref, other_ref, hw, he)
-    rows_done = range(1, field.shape[1] - 1)
-    finish(rows_done, levels, None, field, courant_ref, mask_ref, hw, he, out_ref, state, sems)
-
-
-def final_edge_kernel(levels, odd_ref, pair_ref, other_ref, field, courant_ref, mask_ref, far_in, near_in, part_ref,
+def final_edge_kernel(levels, odd_ref, pair_ref, other_ref, field, courant_ref, mask_ref, far_in, part_ref,
                       out_ref, hw, he, state, sems):
     ends_in_place(odd_ref, pair_ref, other_ref, hw, he)
-    lat = by_side(odd_ref, near_in, far_in)
-    finish((0, field.shape[1] - 1), levels, lat, field, courant_ref, mask_ref, hw, he, out_ref, state, sems)
+    do = finish(levels, beyond(far_in), field, courant_ref, mask_ref, hw, he, out_ref, state, sems)
+    each_row(odd_ref, field.shape[1], False, False, do)
 
 
 def last_step(levels, odd, field, courant, mask, halos):
     f32 = jnp.float32
     near, far, pair, other = halos
     tracers, rows, high, wide = field.shape
-    slots = 12
+    slots = tracers * rows
     scratch = [pltpu.VMEM((high, LANES), f32)] * 2 + [
         pltpu.VMEM((slots, levels, wide), f32),
         pltpu.SemaphoreType.DMA((slots,)),
@@ -449,21 +467,21 @@
     part = pl.pallas_call(
         functools.partial(final_inner_kernel, levels),
         out_shape=shape,
-        in_specs=[SMEM] + [VMEM] * 5,
+        in_specs=[SMEM] + [VMEM] * 6,
         out_specs=HBM,
         scratch_shapes=scratch,
         compiler_params=params,
         cost_estimate=COST,
-    )(odd, pair, other, field, courant, mask)
+    )(odd, pair, other, field, courant, mask, near)
     return pl.pallas_call(
         functools.partial(final_edge_kernel, levels),
         out_shape=shape,
-        in_specs=[SMEM] + [VMEM] * 7 + [HBM],
+        in_specs=[SMEM] + [VMEM] * 6 + [HBM],
         out_specs=HBM,
         scratch_shapes=scratch,
-        input_output_aliases={8: 0},
+        input_output_aliases={7: 0},
         compiler_params=params,
-    )(odd, pair, other, field, courant, mask, far, near, part)
+    )(odd, pair, other, field, courant, mask, far, part)
 
 
 def weights(inverse, high):

time: 93.4 us -> 92 us (0.985)
  waiting for transfers between devices: 31.2 us -> 29.9 us
  starting transfers between devices: 23.6 us -> 22.4 us
    ppermute x2, waiting for transfers between devices: 7.22 us -> 0.01 us  [exchange(): far = lax.ppermute(far, 'lat', next_pair)]
    ppermute x2, waiting for transfers between devices: 0.01 us -> 4.98 us  [exchange(): pair = lax.ppermute(pair, 'lon', [(i, i ^ 1) for i in range(lon)])]
    ppermute x2, starting transfers between devices: 6.14 us -> 3.61 us  [exchange(): pair = lax.ppermute(pair, 'lon', [(i, i ^ 1) for i in range(lon)])]
    ppermute x2, starting transfers between devices: 4.87 us -> 6.96 us  [exchange(): far = lax.ppermute(far, 'lat', next_pair)]
    ppermute x2, waiting for transfers between devices: 3.58 us -> 4.53 us  [exchange(): lax.ppermute(other, 'lon', [(i, (i + 1 if i % 2 else i - 1) % lon) for i...]
  transfers between devices with their start and end apart: 9 -> 9, of which waited for: 5 -> 5; matrix products, arithmetic and copies ran while one was open for 1% -> 1% of each run, Pallas kernels for 17% -> 19%
where the time goes in v5:
time: 92 us; the launch traced here: 91.6 us
  Pallas kernels  38.1 us (41%)
  waiting for transfers between devices  29.9 us (32%)
  starting transfers between devices  22.4 us (24%)
    all_to_all x1, waiting for transfers between devices, local(): lax.all_to_all(send, ('lat', 'lon'), split_axis=0, concat_axis=0, tiled=T...  20.3 us
    all_to_all x1, starting transfers between devices, local(): lax.all_to_all(send, ('lat', 'lon'), split_axis=0, concat_axis=0, tiled=T...  10.5 us
    pallas_call x1, Pallas kernels, start(): pl.pallas_call(functools.partial(start_kernel, devices), out_shape=shapes...  9.32 us
    pallas_call x1, Pallas kernels, prepare(): pl.pallas_call(prepare_kernel, out_shape=jax.ShapeDtypeStruct((parts + SP...  9.01 us
    pallas_call x1, Pallas kernels, pack(): pl.pallas_call(functools.partial(pack_kernel, (levels, high, columns, dev...  8.13 us
    ppermute x2, starting transfers between devices, exchange(): far = lax.ppermute(far, 'lat', next_pair)  6.96 us
    ppermute x2, waiting for transfers between devices, exchange(): pair = lax.ppermute(pair, 'lon', [(i, i ^ 1) for i in range(lon)])  4.98 us
    ppermute x2, waiting for transfers between devices, exchange(): lax.ppermute(other, 'lon', [(i, (i + 1 if i % 2 else i - 1) % lon) for i...  4.53 us
  transfers between devices with their start and end apart: 9, of which 5 were waited for; matrix products, arithmetic and copies ran while one was open for 1% of the time, Pallas kernels for 19%

profile of v5, /device:TPU:8, one launch (start us, length us, event | category | flops | bytes accessed | tf_op | source)
XLA Modules:
  0.0 91.6 jit_solution(6243605615655251493)
XLA Ops:
  0.0 8.1 %shard_map.73 = f32[4224,1,128]{2,1,0:T(1,128)} custom-call(s32[16,128]{1,0:T(8,128)} %bitcast.14, s32[16,128]{1,0:T(8,128)} %bitcast.15, f32[2048,1,128]{2,1,0:T(1,128)} %bitcast.13), custom_call_target="tpu_custom_call" | custom-call | tf_op jit(solution)/shard_map/pallas_call | solution.py:98
  8.1 10.5 %all-to-all-start = ((f32[4224,1,128]{2,1,0:T(1,128)}), f32[4224,1,128]{2,1,0:T(1,128)S(1)}, u32[]{:S(2)}, u32[]{:S(2)}) async-start(f32[4224,1,128]{2,1,0:T(1,128)} %shard_map.73), calls=%async_computation | async-start | bytes 4325376 | tf_op jit(solution)/shard_map/all_to_all | solution.py:515
  18.6 0.0 copy-done.1
  18.6 0.2 copy.10
  18.9 9.0 %shard_map.74.inputs_hbm = f32[16,8,100,512]{3,2,1,0:T(8,128)} custom-call(f32[2,100,8,512]{3,2,1,0:T(8,128)} %bitcast.12, f32[4,100,8,512]{3,2,1,0:T(8,128)} %bitcast.10), custom_call_target="tpu_custom_call" | custom-call | tf_op jit(solution)/shard_map/pallas_call | solution.py:183
  27.9 0.1 pad_add_fusion.odd_ref
  28.0 0.1 subtract_convert_fusion
  28.1 0.4 maximum_maximum_fusion.weight_hbm.weight_ref
  28.5 0.0 copy-start
  28.5 20.3 %all-to-all-done.got_ref = f32[4224,1,128]{2,1,0:T(1,128)S(1)} async-done(((f32[4224,1,128]{2,1,0:T(1,128)}), f32[4224,1,128]{2,1,0:T(1,128)S(1)}, u32[]{:S(2)}, u32[]{:S(2)}) %all-to-all-start) | async-done | bytes 2162720 | tf_op jit(solution)/shard_map/all_to_all | solution.py:515
  48.9 9.3 %shard_map.75 = (f32[2,8,104,512]{3,2,1,0:T(8,128)S(1)}, f32[2,104,512]{2,1,0:T(8,128)S(1)}, f32[2,104,512]{2,1,0:T(8,128)S(1)}, f32[104,128]{1,0:T(8,128)S(1)},...) custom-call(s32[2]{0:T(128)S(1)} %pad_add_fusion.odd_ref, f32[4224,1,128]{2,1,0:T(1,128)S(1)} %all-to-all-done.got_ref, ...), custom_call_target="tpu_custom_call" | custom-call | tf_op jit(solution)/shard_map/pallas_call | solution.py:269
  58.2 0.1 collective-permute-start.3
  58.3 4.3 %collective-permute-start.2 = (f32[2,104,512]{2,1,0:T(8,128)S(1)}, f32[2,104,512]{2,1,0:T(8,128)S(1)}, u32[]{:S(2)}, u32[]{:S(2)}) collective-permute-start(f32[2,104,512]{2,1,0:T(8,128)S(1)} %get-tuple-element.23), channel_id=1, source_target_pairs={{4,8},{8,4},{12,16},{16,12},{20,24},{24,20},{28,32},{32,28},{36,40... | collective-permute-start | bytes 1277960 | tf_op jit(solution)/shard_map/ppermute | solution.py:504
  62.5 3.5 %collective-permute-start = (f32[104,128]{1,0:T(8,128)S(1)}, f32[104,128]{1,0:T(8,128)S(1)}, u32[]{:S(2)}, u32[]{:S(2)}) collective-permute-start(f32[104,128]{1,0:T(8,128)S(1)} %get-tuple-element.19), channel_id=1, source_target_pairs={{0,1},{1,0},{2,3},{3,2},{4,5},{5,4},{6,7},{7,6},{8,9},{9,8},{10,11... | collective-permute-start | bytes 159752 | tf_op jit(solution)/shard_map/ppermute | solution.py:503
  66.1 0.0 collective-permute-start.1
  66.1 2.1 %collective-permute-done.pair_ref = f32[104,128]{1,0:T(8,128)S(1)} collective-permute-done((f32[104,128]{1,0:T(8,128)S(1)}, f32[104,128]{1,0:T(8,128)S(1)}, u32[]{:S(2)}, u32[]{:S(2)}) %collective-permute-start) | collective-permute-done | bytes 53280 | tf_op jit(solution)/shard_map/ppermute | solution.py:503
  68.2 3.2 %collective-permute-done.1.other_ref = f32[104,128]{1,0:T(8,128)S(1)} collective-permute-done((f32[104,128]{1,0:T(8,128)S(1)}, f32[104,128]{1,0:T(8,128)S(1)}, u32[]{:S(2)}, u32[]{:S(2)}) %collective-permute-start.1) | collective-permute-done | bytes 53280 | tf_op jit(solution)/shard_map/ppermute | solution.py:502
  71.4 0.0 collective-permute-done.3.near_in
  71.4 0.0 copy-done
  71.4 4.0 %shard_map.76 = (f32[2,8,104,512]{3,2,1,0:T(8,128)S(1)}, f32[104,128]{1,0:T(8,128)S(1)}, f32[104,128]{1,0:T(8,128)S(1)}) custom-call(s32[2]{0:T(128)S(1)} %pad_add_fusion.odd_ref, f32[104,128]{1,0:T(8,128)S(1)} %collective-permute-done.pair_ref, f32[104,128]{1,0:T(8,128)S(1)} %collective-permute-done.1.other_ref, ...), custom_call_target="tpu_custom_call" | custom-call | flops 3000000000 | bytes 8000000 | tf_op jit(solution)/shard_map/pallas_call | solution.py:394
  75.4 0.0 collective-permute-done.2.far_in
  75.4 1.5 %shard_map.77 = (f32[2,8,104,512]{3,2,1,0:T(8,128)S(1)}, f32[2,104,512]{2,1,0:T(8,128)S(1)}, f32[2,104,512]{2,1,0:T(8,128)S(1)}, f32[104,128]{1,0:T(8,128)S(1)}, f32[104,128]{1,0:T(8,128)S(1)}) custom-call(s32[2]{0:T(128)S(1)} %pad_add_fusion.odd_ref, f32[104,128]{1,0:T(8,128)S(1)} %collective-permute-done.pair_ref, ...), custom_call_target="tpu_custom_call", output_to_operand_aliasing={{0}: (8, {})} | custom-call | tf_op jit(solution)/shard_map/pallas_call | solution.py:403
  76.9 0.1 collective-permute-start.7
  77.0 2.7 %collective-permute-start.6 = (f32[2,104,512]{2,1,0:T(8,128)S(1)}, f32[2,104,512]{2,1,0:T(8,128)S(1)}, u32[]{:S(2)}, u32[]{:S(2)}) collective-permute-start(f32[2,104,512]{2,1,0:T(8,128)S(1)} %get-tuple-element.31), channel_id=1, source_target_pairs={{4,8},{8,4},{12,16},{16,12},{20,24},{24,20},{28,32},{32,28},{36,40... | collective-permute-start | bytes 1277960 | tf_op jit(solution)/shard_map/ppermute | solution.py:504
  79.7 0.1 collective-permute-start.4
  79.8 1.2 %collective-permute-start.5 = (f32[104,128]{1,0:T(8,128)S(1)}, f32[104,128]{1,0:T(8,128)S(1)}, u32[]{:S(2)}, u32[]{:S(2)}) collective-permute-start(f32[104,128]{1,0:T(8,128)S(1)} %get-tuple-element.29), channel_id=1, source_target_pairs={{0,3},{1,2},{2,1},{3,0},{4,7},{5,6},{6,5},{7,4},{8,11},{9,10},{10,... | collective-permute-start | bytes 159752 | tf_op jit(solution)/shard_map/ppermute | solution.py:502
  81.1 2.9 %collective-permute-done.4.pair_ref = f32[104,128]{1,0:T(8,128)S(1)} collective-permute-done((f32[104,128]{1,0:T(8,128)S(1)}, f32[104,128]{1,0:T(8,128)S(1)}, u32[]{:S(2)}, u32[]{:S(2)}) %collective-permute-start.4) | collective-permute-done | bytes 53280 | tf_op jit(solution)/shard_map/ppermute | solution.py:503
  83.9 1.3 %collective-permute-done.5.other_ref = f32[104,128]{1,0:T(8,128)S(1)} collective-permute-done((f32[104,128]{1,0:T(8,128)S(1)}, f32[104,128]{1,0:T(8,128)S(1)}, u32[]{:S(2)}, u32[]{:S(2)}) %collective-permute-start.5) | collective-permute-done | bytes 53280 | tf_op jit(solution)/shard_map/ppermute | solution.py:502
  85.2 0.0 collective-permute-done.7.near_in
  85.3 4.4 %shard_map.78.part_ref = f32[2,100,8,512]{3,2,1,0:T(8,128)} custom-call(s32[2]{0:T(128)S(1)} %pad_add_fusion.odd_ref, f32[104,128]{1,0:T(8,128)S(1)} %collective-permute-done.4.pair_ref, f32[104,128]{1,0:T(8,128)S(1)} %collective-permute-done.5.other_ref, f32[2,8,104,512]{3,2,1,0:T(8,128)S(1)} %get-tuple-element.30.field, ...), custom_call_target="tpu_custom_call" | custom-call | flops 3000000000 | bytes 8000000 | tf_op jit(solution)/shard_map/pallas_call | solution.py:467
  89.6 0.0 collective-permute-done.6.far_in
  89.6 1.8 %shard_map.79 = f32[2,100,8,512]{3,2,1,0:T(8,128)} custom-call(s32[2]{0:T(128)S(1)} %pad_add_fusion.odd_ref, f32[104,128]{1,0:T(8,128)S(1)} %collective-permute-done.4.pair_ref, f32[104,128]{1,0:T(8,128)S(1)} %collective-permute-done.5.other_ref, f32[2,8,104,512]{3,2,1,0:T(8,128)S(1)} %get-tuple-element.30.field, ...), custom_call_target="tpu_custom_call", output_to_operand_aliasing={{}: (7, {})} | custom-call | tf_op jit(solution)/shard_map/pallas_call | solution.py:476
  (3 shorter events, 0.1 us)
Async XLA Ops:
  0.0 18.6 %copy-start.1 = (f32[8,100,100]{2,0,1:T(8,128)S(1)}, f32[8,100,100]{2,0,1:T(8,128)}, u32[]{:S(2)}) copy-start(f32[8,100,100]{2,0,1:T(8,128)} %param.9) | copy-start | bytes 960004
  8.1 40.7 %all-to-all-start = ((f32[4224,1,128]{2,1,0:T(1,128)}), f32[4224,1,128]{2,1,0:T(1,128)S(1)}, u32[]{:S(2)}, u32[]{:S(2)}) async-start(f32[4224,1,128]{2,1,0:T(1,128)} %shard_map.73), calls=%async_computation | async-start | bytes 4325376 | tf_op jit(solution)/shard_map/all_to_all | solution.py:515
  28.5 42.9 %copy-start = (s32[8,512]{1,0:T(8,128)S(1)}, s32[8,512]{1,0:T(8,128)}, u32[]{:S(2)}) copy-start(s32[8,512]{1,0:T(8,128)} %mask_ref.7) | copy-start | bytes 49156
  58.2 13.2 %collective-permute-start.3 = (f32[2,104,512]{2,1,0:T(8,128)S(1)}, f32[2,104,512]{2,1,0:T(8,128)S(1)}, u32[]{:S(2)}, u32[]{:S(2)}) collective-permute-start(f32[2,104,512]{2,1,0:T(8,128)S(1)} %get-tuple-element.24), channel_id=1, source_target_pairs={{0,4},{4,0},{8,12},{12,8},{16,20},{20,16},{24,28},{28,24},{32,36},... | collective-permute-start | bytes 1277960 | tf_op jit(solution)/shard_map/ppermute | solution.py:505
  58.3 17.1 %collective-permute-start.2 = (f32[2,104,512]{2,1,0:T(8,128)S(1)}, f32[2,104,512]{2,1,0:T(8,128)S(1)}, u32[]{:S(2)}, u32[]{:S(2)}) collective-permute-start(f32[2,104,512]{2,1,0:T(8,128)S(1)} %get-tuple-element.23), channel_id=1, source_target_pairs={{4,8},{8,4},{12,16},{16,12},{20,24},{24,20},{28,32},{32,28},{36,40... | collective-permute-start | bytes 1277960 | tf_op jit(solution)/shard_map/ppermute | solution.py:504
  62.5 5.6 %collective-permute-start = (f32[104,128]{1,0:T(8,128)S(1)}, f32[104,128]{1,0:T(8,128)S(1)}, u32[]{:S(2)}, u32[]{:S(2)}) collective-permute-start(f32[104,128]{1,0:T(8,128)S(1)} %get-tuple-element.19), channel_id=1, source_target_pairs={{0,1},{1,0},{2,3},{3,2},{4,5},{5,4},{6,7},{7,6},{8,9},{9,8},{10,11... | collective-permute-start | bytes 159752 | tf_op jit(solution)/shard_map/ppermute | solution.py:503
  66.1 5.3 %collective-permute-start.1 = (f32[104,128]{1,0:T(8,128)S(1)}, f32[104,128]{1,0:T(8,128)S(1)}, u32[]{:S(2)}, u32[]{:S(2)}) collective-permute-start(f32[104,128]{1,0:T(8,128)S(1)} %get-tuple-element.20), channel_id=1, source_target_pairs={{0,3},{1,2},{2,1},{3,0},{4,7},{5,6},{6,5},{7,4},{8,11},{9,10},{10,... | collective-permute-start | bytes 159752 | tf_op jit(solution)/shard_map/ppermute | solution.py:502
  76.9 8.3 %collective-permute-start.7 = (f32[2,104,512]{2,1,0:T(8,128)S(1)}, f32[2,104,512]{2,1,0:T(8,128)S(1)}, u32[]{:S(2)}, u32[]{:S(2)}) collective-permute-start(f32[2,104,512]{2,1,0:T(8,128)S(1)} %get-tuple-element.32), channel_id=1, source_target_pairs={{0,4},{4,0},{8,12},{12,8},{16,20},{20,16},{24,28},{28,24},{32,36},... | collective-permute-start | bytes 1277960 | tf_op jit(solution)/shard_map/ppermute | solution.py:505
  77.0 12.6 %collective-permute-start.6 = (f32[2,104,512]{2,1,0:T(8,128)S(1)}, f32[2,104,512]{2,1,0:T(8,128)S(1)}, u32[]{:S(2)}, u32[]{:S(2)}) collective-permute-start(f32[2,104,512]{2,1,0:T(8,128)S(1)} %get-tuple-element.31), channel_id=1, source_target_pairs={{4,8},{8,4},{12,16},{16,12},{20,24},{24,20},{28,32},{32,28},{36,40... | collective-permute-start | bytes 1277960 | tf_op jit(solution)/shard_map/ppermute | solution.py:504
  79.7 4.2 %collective-permute-start.4 = (f32[104,128]{1,0:T(8,128)S(1)}, f32[104,128]{1,0:T(8,128)S(1)}, u32[]{:S(2)}, u32[]{:S(2)}) collective-permute-start(f32[104,128]{1,0:T(8,128)S(1)} %get-tuple-element.28), channel_id=1, source_target_pairs={{0,1},{1,0},{2,3},{3,2},{4,5},{5,4},{6,7},{7,6},{8,9},{9,8},{10,11... | collective-permute-start | bytes 159752 | tf_op jit(solution)/shard_map/ppermute | solution.py:503
  79.8 5.4 %collective-permute-start.5 = (f32[104,128]{1,0:T(8,128)S(1)}, f32[104,128]{1,0:T(8,128)S(1)}, u32[]{:S(2)}, u32[]{:S(2)}) collective-permute-start(f32[104,128]{1,0:T(8,128)S(1)} %get-tuple-element.29), channel_id=1, source_target_pairs={{0,3},{1,2},{2,1},{3,0},{4,7},{5,6},{6,5},{7,4},{8,11},{9,10},{10,... | collective-permute-start | bytes 159752 | tf_op jit(solution)/shard_map/ppermute | solution.py:502

commit v6 on v5

--- a/solution.py
+++ b/solution.py
@@ -19,7 +19,7 @@
 
 
 SPARE = 10
-LIMIT = 24
+LIMIT = 26
 VMEM = pl.BlockSpec(memory_space=pltpu.VMEM)
 SMEM = pl.BlockSpec(memory_space=pltpu.SMEM)
 HBM = pl.BlockSpec(memory_space=pltpu.HBM)
@@ -360,12 +360,64 @@
     return do
 
 
-def inner_kernel(levels, odd_ref, pair_ref, other_ref, field, courant_ref, mask_ref, weight_ref, near_in,
+def body_kernel(levels, field, courant_ref, mask_ref, out_ref, none):
+    none[...] = jnp.zeros_like(none)
+    tracers, rows = field.shape[:2]
+    for j in range(1, rows - 1):
+        mask = mask_row(mask_ref, j)
+        for t in range(tracers):
+
+            def store(strip, tile, value):
+                out_ref[t, j, strip, tile] = value
+
+            transported(t, j, levels, field, courant_ref, mask, None, none, none, store)
+
+
+def body(levels, field, courant, mask):
+    tracers, rows, high, wide = field.shape
+    return pl.pallas_call(
+        functools.partial(body_kernel, levels),
+        out_shape=jax.ShapeDtypeStruct((tracers, rows, levels, wide), jnp.float32),
+        in_specs=[VMEM] * 3,
+        out_specs=VMEM,
+        scratch_shapes=[pltpu.VMEM((high, LANES), jnp.float32)],
+        compiler_params=pltpu.CompilerParams(vmem_limit_bytes=LIMIT * MIB),
+        cost_estimate=COST,
+    )(field, courant, mask)
+
+
+def patched(t, j, levels, body_ref, courant_ref, mask, hw, he, rows, store):
+    wide = body_ref.shape[3]
+    row = t * rows + j
+    first, last = slice(0, LANES), slice(wide - LANES, wide)
+    for at in range(0, levels, 8):
+        count = min(8, levels - at)
+        strip = slice(at, at + count)
+        lane = lax.broadcasted_iota(jnp.int32, (count, LANES), 1)
+        w = jnp.where(lane == 0, pltpu.roll(hw[strip, :], (LANES - row) % LANES, 1), 0.0)
+        e = jnp.where(lane == LANES - 1, pltpu.roll(he[strip, :], LANES - 1 - row, 1), 0.0)
+        store(strip, 0, body_ref[t, j, strip, first] + mask[0] * (courant_ref[1, j, strip, first] * w))
+        store(strip, 1, body_ref[t, j, strip, last] + mask[-1] * (courant_ref[0, j, strip, last] * e))
+
+
+def inner_kernel(levels, odd_ref, pair_ref, other_ref, field, courant_ref, mask_ref, weight_ref, near_in, body_ref,
                  out_ref, west, east, hw, he, state):
     ends_in_place(odd_ref, pair_ref, other_ref, hw, he)
-    rows = field.shape[1]
+    tracers, rows, high, wide = field.shape
     do = advance(levels, beyond(near_in), field, courant_ref, mask_ref, hw, he, weight_ref, out_ref, state)
-    each_row(odd_ref, rows, True, True, do)
+    for j in range(1, rows - 1):
+        mask = mask_row(mask_ref, j)
+        for t in range(tracers):
+            slot = (j * tracers + t) % state.shape[0]
+
+            def store(strip, side, value):
+                state[slot, strip, side * (wide - LANES) : side * (wide - LANES) + LANES] = value
+
+            patched(t, j, levels, body_ref, courant_ref, mask, hw, he, rows, store)
+            state[slot, :levels, LANES : wide - LANES] = body_ref[t, j, :, LANES : wide - LANES]
+            for at in range(0, wide, 2 * LANES):
+                out_ref[t, j, :, at : at + 2 * LANES] = vertical(weight_ref[j], state[slot, :, at : at + 2 * LANES])
+    each_row(odd_ref, rows, False, True, do)
     for strip, first, last in collect_ends(range(1, rows - 1), out_ref, no_ends):
         west[strip, :] = first
         east[strip, :] = last
@@ -381,7 +433,7 @@
     hand_out(odd_ref, out_ref, (0, rows - 1), before, near_ref, far_ref, pair_out, other_out)
 
 
-COST = pl.CostEstimate(flops=3_000_000_000, bytes_accessed=8_000_000, transcendentals=0)
+COST = pl.CostEstimate(flops=1_000_000_000, bytes_accessed=8_000_000, transcendentals=0)
 
 
 def step(levels, odd, field, courant, mask, weight, halos):
@@ -394,12 +446,12 @@
     part, west, east = pl.pallas_call(
         functools.partial(inner_kernel, levels),
         out_shape=(field_shape, end, end),
-        in_specs=[SMEM] + [VMEM] * 7,
+        in_specs=[SMEM] + [VMEM] * 8,
         out_specs=(VMEM,) * 3,
         scratch_shapes=scratch,
         compiler_params=params,
         cost_estimate=COST,
-    )(odd, pair, other, field, courant, mask, weight, near)
+    )(odd, pair, other, field, courant, mask, weight, near, body(levels, field, courant, mask))
     return pl.pallas_call(
         functools.partial(edge_kernel, levels),
         out_shape=(field_shape, edge, edge, end, end),
@@ -436,12 +488,36 @@
     return do
 
 
-def final_inner_kernel(levels, odd_ref, pair_ref, other_ref, field, courant_ref, mask_ref, near_in, out_ref, hw, he, state,
-                       sems):
+def final_inner_kernel(levels, odd_ref, pair_ref, other_ref, field, courant_ref, mask_ref, near_in, body_ref, out_ref,
+                       hw, he, state, sems, sides, side_sems):
+    tracers, rows, _, wide = field.shape
+    middle = pl.ds(LANES, wide - 2 * LANES)
+    flying = []
+    for j in range(1, rows - 1):
+        for t in range(tracers):
+            flying.append(pltpu.make_async_copy(
+                body_ref.at[t, j, :, middle], out_ref.at[t, :, j, middle], sems.at[j * tracers + t]
+            ))
+            flying[-1].start()
     ends_in_place(odd_ref, pair_ref, other_ref, hw, he)
-    flying = []
-    do = finish(levels, beyond(near_in), field, courant_ref, mask_ref, hw, he, out_ref, state, sems, flying)
-    each_row(odd_ref, field.shape[1], True, True, do)
+    for j in range(1, rows - 1):
+        mask = mask_row(mask_ref, j)
+        for t in range(tracers):
+            slot = j * tracers + t
+
+            def store(strip, side, value):
+                sides[slot, side, strip, :] = value
+
+            patched(t, j, levels, body_ref, courant_ref, mask, hw, he, rows, store)
+            for side in (0, 1):
+                flying.append(pltpu.make_async_copy(
+                    sides.at[slot, side],
+                    out_ref.at[t, :, j, pl.ds(side * (wide - LANES), LANES)],
+                    side_sems.at[slot * 2 + side],
+                ))
+                flying[-1].start()
+    do = finish(levels, beyond(near_in), field, courant_ref, mask_ref, hw, he, out_ref, state, sems)
+    each_row(odd_ref, rows, False, True, do)
     for copy in flying:
         copy.wait()
 
@@ -467,12 +543,13 @@
     part = pl.pallas_call(
         functools.partial(final_inner_kernel, levels),
         out_shape=shape,
-        in_specs=[SMEM] + [VMEM] * 6,
+        in_specs=[SMEM] + [VMEM] * 7,
         out_specs=HBM,
-        scratch_shapes=scratch,
+        scratch_shapes=scratch
+        + [pltpu.VMEM((slots, 2, levels, LANES), f32), pltpu.SemaphoreType.DMA((2 * slots,))],
         compiler_params=params,
         cost_estimate=COST,
-    )(odd, pair, other, field, courant, mask, near)
+    )(odd, pair, other, field, courant, mask, near, body(levels, field, courant, mask))
     return pl.pallas_call(
         functools.partial(final_edge_kernel, levels),
         out_shape=shape,

time: 92 us -> 89.5 us (0.973)
  waiting for transfers between devices: 29.9 us -> 26.3 us
  Pallas kernels: 38.1 us -> 39.7 us
    ppermute x2, waiting for transfers between devices: 4.98 us -> 1.11 us  [exchange(): pair = lax.ppermute(pair, 'lon', [(i, i ^ 1) for i in range(lon)])]
    pallas_call x0 -> x2, Pallas kernels: none -> 3.12 us  [body(): pl.pallas_call(functools.partial(body_kernel, levels), out_shape=jax.Shap...]
    pallas_call x1, Pallas kernels: 4.35 us -> 2.67 us  [last_step(): pl.pallas_call(functools.partial(final_inner_kernel, levels), out_shape=s...]
    pallas_call x1, Pallas kernels: 9.32 us -> 10.8 us  [start(): pl.pallas_call(functools.partial(start_kernel, devices), out_shape=shapes...]
    ppermute x2, starting transfers between devices: 3.61 us -> 2.45 us  [exchange(): pair = lax.ppermute(pair, 'lon', [(i, i ^ 1) for i in range(lon)])]
    pallas_call x1, Pallas kernels: 3.98 us -> 2.86 us  [step(): pl.pallas_call(functools.partial(inner_kernel, levels), out_shape=(field_...]
  transfers between devices with their start and end apart: 9 -> 9, of which waited for: 5 -> 5; matrix products, arithmetic and copies ran while one was open for 1% -> 1% of each run, Pallas kernels for 19% -> 20%
where the time goes in v6:
time: 89.5 us; the launch traced here: 89.8 us
  Pallas kernels  39.7 us (44%)
  waiting for transfers between devices  26.3 us (29%)
  starting transfers between devices  22.7 us (25%)
    all_to_all x1, waiting for transfers between devices, local(): lax.all_to_all(send, ('lat', 'lon'), split_axis=0, concat_axis=0, tiled=T...  20.3 us
    pallas_call x1, Pallas kernels, start(): pl.pallas_call(functools.partial(start_kernel, devices), out_shape=shapes...  10.8 us
    all_to_all x1, starting transfers between devices, local(): lax.all_to_all(send, ('lat', 'lon'), split_axis=0, concat_axis=0, tiled=T...  10.5 us
    pallas_call x1, Pallas kernels, prepare(): pl.pallas_call(prepare_kernel, out_shape=jax.ShapeDtypeStruct((parts + SP...  9.01 us
    pallas_call x1, Pallas kernels, pack(): pl.pallas_call(functools.partial(pack_kernel, (levels, high, columns, dev...  8.13 us
    ppermute x2, starting transfers between devices, exchange(): far = lax.ppermute(far, 'lat', next_pair)  7.04 us
    ppermute x2, waiting for transfers between devices, exchange(): lax.ppermute(other, 'lon', [(i, (i + 1 if i % 2 else i - 1) % lon) for i...  4.66 us
    pallas_call x2, Pallas kernels, body(): pl.pallas_call(functools.partial(body_kernel, levels), out_shape=jax.Shap...  3.12 us
  transfers between devices with their start and end apart: 9, of which 5 were waited for; matrix products, arithmetic and copies ran while one was open for 1% of the time, Pallas kernels for 20%

profile of v6, /device:TPU:8, one launch (start us, length us, event | category | flops | bytes accessed | tf_op | source)
XLA Modules:
  0.0 89.8 jit_solution(5284685590018347479)
XLA Ops:
  0.0 8.1 %shard_map.73 = f32[4224,1,128]{2,1,0:T(1,128)} custom-call(s32[16,128]{1,0:T(8,128)} %bitcast.14, s32[16,128]{1,0:T(8,128)} %bitcast.15, f32[2048,1,128]{2,1,0:T(1,128)} %bitcast.13), custom_call_target="tpu_custom_call" | custom-call | tf_op jit(solution)/shard_map/pallas_call | solution.py:98
  8.1 10.5 %all-to-all-start = ((f32[4224,1,128]{2,1,0:T(1,128)}), f32[4224,1,128]{2,1,0:T(1,128)S(1)}, u32[]{:S(2)}, u32[]{:S(2)}) async-start(f32[4224,1,128]{2,1,0:T(1,128)} %shard_map.73), calls=%async_computation | async-start | bytes 4325376 | tf_op jit(solution)/shard_map/all_to_all | solution.py:592
  18.6 0.2 copy.10
  18.9 9.0 %shard_map.74.inputs_hbm = f32[16,8,100,512]{3,2,1,0:T(8,128)} custom-call(f32[2,100,8,512]{3,2,1,0:T(8,128)} %bitcast.12, f32[4,100,8,512]{3,2,1,0:T(8,128)} %bitcast.10), custom_call_target="tpu_custom_call" | custom-call | tf_op jit(solution)/shard_map/pallas_call | solution.py:183
  27.9 0.1 pad_add_fusion.odd_ref
  28.0 0.1 subtract_convert_fusion
  28.1 0.4 maximum_maximum_fusion.weight_hbm.weight_ref
  28.5 0.0 copy-start
  28.5 20.3 %all-to-all-done.got_ref = f32[4224,1,128]{2,1,0:T(1,128)S(1)} async-done(((f32[4224,1,128]{2,1,0:T(1,128)}), f32[4224,1,128]{2,1,0:T(1,128)S(1)}, u32[]{:S(2)}, u32[]{:S(2)}) %all-to-all-start) | async-done | bytes 2162720 | tf_op jit(solution)/shard_map/all_to_all | solution.py:592
  48.9 10.8 %shard_map.75 = (f32[2,8,104,512]{3,2,1,0:T(8,128)S(1)}, f32[2,104,512]{2,1,0:T(8,128)S(1)}, f32[2,104,512]{2,1,0:T(8,128)S(1)}, f32[104,128]{1,0:T(8,128)S(1)},...) custom-call(s32[2]{0:T(128)S(1)} %pad_add_fusion.odd_ref, f32[4224,1,128]{2,1,0:T(1,128)S(1)} %all-to-all-done.got_ref, ...), custom_call_target="tpu_custom_call" | custom-call | tf_op jit(solution)/shard_map/pallas_call | solution.py:269
  59.6 0.9 collective-permute-start.3
  60.5 4.3 %collective-permute-start.2 = (f32[2,104,512]{2,1,0:T(8,128)S(1)}, f32[2,104,512]{2,1,0:T(8,128)S(1)}, u32[]{:S(2)}, u32[]{:S(2)}) collective-permute-start(f32[2,104,512]{2,1,0:T(8,128)S(1)} %get-tuple-element.23), channel_id=1, source_target_pairs={{4,8},{8,4},{12,16},{16,12},{20,24},{24,20},{28,32},{32,28},{36,40... | collective-permute-start | bytes 1277960 | tf_op jit(solution)/shard_map/ppermute | solution.py:581
  64.9 1.8 %collective-permute-start = (f32[104,128]{1,0:T(8,128)S(1)}, f32[104,128]{1,0:T(8,128)S(1)}, u32[]{:S(2)}, u32[]{:S(2)}) collective-permute-start(f32[104,128]{1,0:T(8,128)S(1)} %get-tuple-element.19), channel_id=1, source_target_pairs={{0,1},{1,0},{2,3},{3,2},{4,5},{5,4},{6,7},{7,6},{8,9},{9,8},{10,11... | collective-permute-start | bytes 159752 | tf_op jit(solution)/shard_map/ppermute | solution.py:580
  66.7 0.9 collective-permute-start.1
  67.5 1.6 %shard_map.76.body_ref = f32[2,8,100,512]{3,2,1,0:T(8,128)S(1)} custom-call(f32[2,8,104,512]{3,2,1,0:T(8,128)S(1)} %get-tuple-element.21.field, f32[4,8,100,512]{3,2,1,0:T(8,128)S(1)} %get-tuple-element.22.courant_ref, s32[8,512]{1,0:T(8,128)S(1)} %copy-done), custom_call_target="tpu_custom_call" | custom-call | flops 1000000000 | bytes 8000000 | tf_op jit(solution)/shard_map/pallas_call | solution.py:378
  69.1 0.0 collective-permute-done.pair_ref
  69.1 2.9 %collective-permute-done.1.other_ref = f32[104,128]{1,0:T(8,128)S(1)} collective-permute-done((f32[104,128]{1,0:T(8,128)S(1)}, f32[104,128]{1,0:T(8,128)S(1)}, u32[]{:S(2)}, u32[]{:S(2)}) %collective-permute-start.1) | collective-permute-done | bytes 53280 | tf_op jit(solution)/shard_map/ppermute | solution.py:579
  72.0 0.0 collective-permute-done.3.near_in
  72.0 2.9 %shard_map.77 = (f32[2,8,104,512]{3,2,1,0:T(8,128)S(1)}, f32[104,128]{1,0:T(8,128)S(1)}, f32[104,128]{1,0:T(8,128)S(1)}) custom-call(s32[2]{0:T(128)S(1)} %pad_add_fusion.odd_ref, f32[104,128]{1,0:T(8,128)S(1)} %collective-permute-done.pair_ref, f32[104,128]{1,0:T(8,128)S(1)} %collective-permute-done.1.other_ref, ...), custom_call_target="tpu_custom_call" | custom-call | flops 1000000000 | bytes 8000000 | tf_op jit(solution)/shard_map/pallas_call | solution.py:446
  74.9 0.0 collective-permute-done.2.far_in
  74.9 1.3 %shard_map.78 = (f32[2,8,104,512]{3,2,1,0:T(8,128)S(1)}, f32[2,104,512]{2,1,0:T(8,128)S(1)}, f32[2,104,512]{2,1,0:T(8,128)S(1)}, f32[104,128]{1,0:T(8,128)S(1)}, f32[104,128]{1,0:T(8,128)S(1)}) custom-call(s32[2]{0:T(128)S(1)} %pad_add_fusion.odd_ref, f32[104,128]{1,0:T(8,128)S(1)} %collective-permute-done.pair_ref, ...), custom_call_target="tpu_custom_call", output_to_operand_aliasing={{0}: (8, {})} | custom-call | tf_op jit(solution)/shard_map/pallas_call | solution.py:455
  76.2 0.1 collective-permute-start.7
  76.3 2.7 %collective-permute-start.6 = (f32[2,104,512]{2,1,0:T(8,128)S(1)}, f32[2,104,512]{2,1,0:T(8,128)S(1)}, u32[]{:S(2)}, u32[]{:S(2)}) collective-permute-start(f32[2,104,512]{2,1,0:T(8,128)S(1)} %get-tuple-element.31), channel_id=1, source_target_pairs={{4,8},{8,4},{12,16},{16,12},{20,24},{24,20},{28,32},{32,28},{36,40... | collective-permute-start | bytes 1277960 | tf_op jit(solution)/shard_map/ppermute | solution.py:581
  79.0 0.7 collective-permute-start.4
  79.7 0.9 collective-permute-start.5
  80.6 1.6 %shard_map.79.body_ref = f32[2,8,100,512]{3,2,1,0:T(8,128)S(1)} custom-call(f32[2,8,104,512]{3,2,1,0:T(8,128)S(1)} %get-tuple-element.30.field, f32[4,8,100,512]{3,2,1,0:T(8,128)S(1)} %get-tuple-element.22.courant_ref, s32[8,512]{1,0:T(8,128)S(1)} %copy-done), custom_call_target="tpu_custom_call" | custom-call | flops 1000000000 | bytes 8000000 | tf_op jit(solution)/shard_map/pallas_call | solution.py:378
  82.1 1.1 %collective-permute-done.4.pair_ref = f32[104,128]{1,0:T(8,128)S(1)} collective-permute-done((f32[104,128]{1,0:T(8,128)S(1)}, f32[104,128]{1,0:T(8,128)S(1)}, u32[]{:S(2)}, u32[]{:S(2)}) %collective-permute-start.4) | collective-permute-done | bytes 53280 | tf_op jit(solution)/shard_map/ppermute | solution.py:580
  83.3 1.8 %collective-permute-done.5.other_ref = f32[104,128]{1,0:T(8,128)S(1)} collective-permute-done((f32[104,128]{1,0:T(8,128)S(1)}, f32[104,128]{1,0:T(8,128)S(1)}, u32[]{:S(2)}, u32[]{:S(2)}) %collective-permute-start.5) | collective-permute-done | bytes 53280 | tf_op jit(solution)/shard_map/ppermute | solution.py:579
  85.0 0.0 collective-permute-done.7.near_in
  85.0 2.7 %shard_map.80.part_ref = f32[2,100,8,512]{3,2,1,0:T(8,128)} custom-call(s32[2]{0:T(128)S(1)} %pad_add_fusion.odd_ref, f32[104,128]{1,0:T(8,128)S(1)} %collective-permute-done.4.pair_ref, f32[104,128]{1,0:T(8,128)S(1)} %collective-permute-done.5.other_ref, f32[2,8,104,512]{3,2,1,0:T(8,128)S(1)} %get-tuple-element.30.field, ...), custom_call_target="tpu_custom_call" | custom-call | flops 1000000000 | bytes 8000000 | tf_op jit(solution)/shard_map/pallas_call | solution.py:543
  87.7 0.2 collective-permute-done.6.far_in
  87.9 1.8 %shard_map.81 = f32[2,100,8,512]{3,2,1,0:T(8,128)} custom-call(s32[2]{0:T(128)S(1)} %pad_add_fusion.odd_ref, f32[104,128]{1,0:T(8,128)S(1)} %collective-permute-done.4.pair_ref, f32[104,128]{1,0:T(8,128)S(1)} %collective-permute-done.5.other_ref, f32[2,8,104,512]{3,2,1,0:T(8,128)S(1)} %get-tuple-element.30.field, ...), custom_call_target="tpu_custom_call", output_to_operand_aliasing={{}: (7, {})} | custom-call | tf_op jit(solution)/shard_map/pallas_call | solution.py:553
  (5 shorter events, 0.1 us)
Async XLA Ops:
  0.0 18.6 %copy-start.1 = (f32[8,100,100]{2,0,1:T(8,128)S(1)}, f32[8,100,100]{2,0,1:T(8,128)}, u32[]{:S(2)}) copy-start(f32[8,100,100]{2,0,1:T(8,128)} %param.9) | copy-start | bytes 960004
  8.1 40.7 %all-to-all-start = ((f32[4224,1,128]{2,1,0:T(1,128)}), f32[4224,1,128]{2,1,0:T(1,128)S(1)}, u32[]{:S(2)}, u32[]{:S(2)}) async-start(f32[4224,1,128]{2,1,0:T(1,128)} %shard_map.73), calls=%async_computation | async-start | bytes 4325376 | tf_op jit(solution)/shard_map/all_to_all | solution.py:592
  28.5 39.0 %copy-start = (s32[8,512]{1,0:T(8,128)S(1)}, s32[8,512]{1,0:T(8,128)}, u32[]{:S(2)}) copy-start(s32[8,512]{1,0:T(8,128)} %mask_ref.11) | copy-start | bytes 49156
  59.6 12.4 %collective-permute-start.3 = (f32[2,104,512]{2,1,0:T(8,128)S(1)}, f32[2,104,512]{2,1,0:T(8,128)S(1)}, u32[]{:S(2)}, u32[]{:S(2)}) collective-permute-start(f32[2,104,512]{2,1,0:T(8,128)S(1)} %get-tuple-element.24), channel_id=1, source_target_pairs={{0,4},{4,0},{8,12},{12,8},{16,20},{20,16},{24,28},{28,24},{32,36},... | collective-permute-start | bytes 1277960 | tf_op jit(solution)/shard_map/ppermute | solution.py:582
  60.5 14.3 %collective-permute-start.2 = (f32[2,104,512]{2,1,0:T(8,128)S(1)}, f32[2,104,512]{2,1,0:T(8,128)S(1)}, u32[]{:S(2)}, u32[]{:S(2)}) collective-permute-start(f32[2,104,512]{2,1,0:T(8,128)S(1)} %get-tuple-element.23), channel_id=1, source_target_pairs={{4,8},{8,4},{12,16},{16,12},{20,24},{24,20},{28,32},{32,28},{36,40... | collective-permute-start | bytes 1277960 | tf_op jit(solution)/shard_map/ppermute | solution.py:581
  64.9 4.3 %collective-permute-start = (f32[104,128]{1,0:T(8,128)S(1)}, f32[104,128]{1,0:T(8,128)S(1)}, u32[]{:S(2)}, u32[]{:S(2)}) collective-permute-start(f32[104,128]{1,0:T(8,128)S(1)} %get-tuple-element.19), channel_id=1, source_target_pairs={{0,1},{1,0},{2,3},{3,2},{4,5},{5,4},{6,7},{7,6},{8,9},{9,8},{10,11... | collective-permute-start | bytes 159752 | tf_op jit(solution)/shard_map/ppermute | solution.py:580
  66.7 5.3 %collective-permute-start.1 = (f32[104,128]{1,0:T(8,128)S(1)}, f32[104,128]{1,0:T(8,128)S(1)}, u32[]{:S(2)}, u32[]{:S(2)}) collective-permute-start(f32[104,128]{1,0:T(8,128)S(1)} %get-tuple-element.20), channel_id=1, source_target_pairs={{0,3},{1,2},{2,1},{3,0},{4,7},{5,6},{6,5},{7,4},{8,11},{9,10},{10,... | collective-permute-start | bytes 159752 | tf_op jit(solution)/shard_map/ppermute | solution.py:579
  76.2 8.8 %collective-permute-start.7 = (f32[2,104,512]{2,1,0:T(8,128)S(1)}, f32[2,104,512]{2,1,0:T(8,128)S(1)}, u32[]{:S(2)}, u32[]{:S(2)}) collective-permute-start(f32[2,104,512]{2,1,0:T(8,128)S(1)} %get-tuple-element.32), channel_id=1, source_target_pairs={{0,4},{4,0},{8,12},{12,8},{16,20},{20,16},{24,28},{28,24},{32,36},... | collective-permute-start | bytes 1277960 | tf_op jit(solution)/shard_map/ppermute | solution.py:582
  76.3 11.6 %collective-permute-start.6 = (f32[2,104,512]{2,1,0:T(8,128)S(1)}, f32[2,104,512]{2,1,0:T(8,128)S(1)}, u32[]{:S(2)}, u32[]{:S(2)}) collective-permute-start(f32[2,104,512]{2,1,0:T(8,128)S(1)} %get-tuple-element.31), channel_id=1, source_target_pairs={{4,8},{8,4},{12,16},{16,12},{20,24},{24,20},{28,32},{32,28},{36,40... | collective-permute-start | bytes 1277960 | tf_op jit(solution)/shard_map/ppermute | solution.py:581
  79.0 4.2 %collective-permute-start.4 = (f32[104,128]{1,0:T(8,128)S(1)}, f32[104,128]{1,0:T(8,128)S(1)}, u32[]{:S(2)}, u32[]{:S(2)}) collective-permute-start(f32[104,128]{1,0:T(8,128)S(1)} %get-tuple-element.28), channel_id=1, source_target_pairs={{0,1},{1,0},{2,3},{3,2},{4,5},{5,4},{6,7},{7,6},{8,9},{9,8},{10,11... | collective-permute-start | bytes 159752 | tf_op jit(solution)/shard_map/ppermute | solution.py:580
  79.7 5.3 %collective-permute-start.5 = (f32[104,128]{1,0:T(8,128)S(1)}, f32[104,128]{1,0:T(8,128)S(1)}, u32[]{:S(2)}, u32[]{:S(2)}) collective-permute-start(f32[104,128]{1,0:T(8,128)S(1)} %get-tuple-element.29), channel_id=1, source_target_pairs={{0,3},{1,2},{2,1},{3,0},{4,7},{5,6},{6,5},{7,4},{8,11},{9,10},{10,... | collective-permute-start | bytes 159752 | tf_op jit(solution)/shard_map/ppermute | solution.py:579

commit v7 on v6

--- a/solution.py
+++ b/solution.py
@@ -433,7 +433,7 @@
     hand_out(odd_ref, out_ref, (0, rows - 1), before, near_ref, far_ref, pair_out, other_out)
 
 
-COST = pl.CostEstimate(flops=1_000_000_000, bytes_accessed=8_000_000, transcendentals=0)
+COST = pl.CostEstimate(flops=3_000_000_000, bytes_accessed=8_000_000, transcendentals=0)
 
 
 def step(levels, odd, field, courant, mask, weight, halos):

time: 89.5 us -> 92.3 us (1.031)
  starting transfers between devices: 22.7 us -> 26.4 us
  Pallas kernels: 39.7 us -> 38 us
    ppermute x2, waiting for transfers between devices: 0.15 us -> 6.39 us  [exchange(): far = lax.ppermute(far, 'lat', next_pair)]
    ppermute x2, waiting for transfers between devices: 4.66 us -> 0.01 us  [exchange(): lax.ppermute(other, 'lon', [(i, (i + 1 if i % 2 else i - 1) % lon) for i...]
    pallas_call x1, Pallas kernels: 10.8 us -> 9.1 us  [start(): pl.pallas_call(functools.partial(start_kernel, devices), out_shape=shapes...]
    ppermute x2, starting transfers between devices: 1.77 us -> 3.21 us  [exchange(): lax.ppermute(other, 'lon', [(i, (i + 1 if i % 2 else i - 1) % lon) for i...]
    ppermute x2, waiting for transfers between devices: 1.11 us -> 0.01 us  [exchange(): pair = lax.ppermute(pair, 'lon', [(i, i ^ 1) for i in range(lon)])]
  transfers between devices with their start and end apart: 9 -> 9, of which waited for: 5 -> 3; matrix products, arithmetic and copies ran while one was open for 1% -> 1% of each run, Pallas kernels for 20% -> 19%
where the time goes in v7:
time: 92.3 us; the launch traced here: 92.4 us
  Pallas kernels  38 us (41%)
  waiting for transfers between devices  26.7 us (29%)
  starting transfers between devices  26.4 us (29%)
    all_to_all x1, waiting for transfers between devices, local(): lax.all_to_all(send, ('lat', 'lon'), split_axis=0, concat_axis=0, tiled=T...  20.3 us
    all_to_all x1, starting transfers between devices, local(): lax.all_to_all(send, ('lat', 'lon'), split_axis=0, concat_axis=0, tiled=T...  10.5 us
    pallas_call x1, Pallas kernels, start(): pl.pallas_call(functools.partial(start_kernel, devices), out_shape=shapes...  9.1 us
    pallas_call x1, Pallas kernels, prepare(): pl.pallas_call(prepare_kernel, out_shape=jax.ShapeDtypeStruct((parts + SP...  9.01 us
    pallas_call x1, Pallas kernels, pack(): pl.pallas_call(functools.partial(pack_kernel, (levels, high, columns, dev...  8.13 us
    ppermute x2, starting transfers between devices, exchange(): far = lax.ppermute(far, 'lat', next_pair)  7.92 us
    ppermute x2, waiting for transfers between devices, exchange(): far = lax.ppermute(far, 'lat', next_pair)  6.39 us
    ppermute x2, starting transfers between devices, exchange(): pair = lax.ppermute(pair, 'lon', [(i, i ^ 1) for i in range(lon)])  3.37 us
  transfers between devices with their start and end apart: 9, of which 3 were waited for; matrix products, arithmetic and copies ran while one was open for 1% of the time, Pallas kernels for 19%

profile of v7, /device:TPU:8, one launch (start us, length us, event | category | flops | bytes accessed | tf_op | source)
XLA Modules:
  0.0 92.4 jit_solution(14119064992819214868)
XLA Ops:
  0.0 8.1 %shard_map.73 = f32[4224,1,128]{2,1,0:T(1,128)} custom-call(s32[16,128]{1,0:T(8,128)} %bitcast.14, s32[16,128]{1,0:T(8,128)} %bitcast.15, f32[2048,1,128]{2,1,0:T(1,128)} %bitcast.13), custom_call_target="tpu_custom_call" | custom-call | tf_op jit(solution)/shard_map/pallas_call | solution.py:98
  8.1 10.5 %all-to-all-start = ((f32[4224,1,128]{2,1,0:T(1,128)}), f32[4224,1,128]{2,1,0:T(1,128)S(1)}, u32[]{:S(2)}, u32[]{:S(2)}) async-start(f32[4224,1,128]{2,1,0:T(1,128)} %shard_map.73), calls=%async_computation | async-start | bytes 4325376 | tf_op jit(solution)/shard_map/all_to_all | solution.py:592
  18.6 0.2 copy.10
  18.9 9.0 %shard_map.74.inputs_hbm = f32[16,8,100,512]{3,2,1,0:T(8,128)} custom-call(f32[2,100,8,512]{3,2,1,0:T(8,128)} %bitcast.12, f32[4,100,8,512]{3,2,1,0:T(8,128)} %bitcast.10), custom_call_target="tpu_custom_call" | custom-call | tf_op jit(solution)/shard_map/pallas_call | solution.py:183
  27.9 0.1 pad_add_fusion.odd_ref
  28.0 0.1 subtract_convert_fusion
  28.1 0.4 maximum_maximum_fusion.weight_hbm.weight_ref
  28.5 0.0 copy-start
  28.5 20.3 %all-to-all-done.got_ref = f32[4224,1,128]{2,1,0:T(1,128)S(1)} async-done(((f32[4224,1,128]{2,1,0:T(1,128)}), f32[4224,1,128]{2,1,0:T(1,128)S(1)}, u32[]{:S(2)}, u32[]{:S(2)}) %all-to-all-start) | async-done | bytes 2162720 | tf_op jit(solution)/shard_map/all_to_all | solution.py:592
  48.9 9.1 %shard_map.75 = (f32[2,8,104,512]{3,2,1,0:T(8,128)S(1)}, f32[2,104,512]{2,1,0:T(8,128)S(1)}, f32[2,104,512]{2,1,0:T(8,128)S(1)}, f32[104,128]{1,0:T(8,128)S(1)},...) custom-call(s32[2]{0:T(128)S(1)} %pad_add_fusion.odd_ref, f32[4224,1,128]{2,1,0:T(1,128)S(1)} %all-to-all-done.got_ref, ...), custom_call_target="tpu_custom_call" | custom-call | tf_op jit(solution)/shard_map/pallas_call | solution.py:269
  58.0 1.4 %collective-permute-start.3 = (f32[2,104,512]{2,1,0:T(8,128)S(1)}, f32[2,104,512]{2,1,0:T(8,128)S(1)}, u32[]{:S(2)}, u32[]{:S(2)}) collective-permute-start(f32[2,104,512]{2,1,0:T(8,128)S(1)} %get-tuple-element.24), channel_id=1, source_target_pairs={{0,4},{4,0},{8,12},{12,8},{16,20},{20,16},{24,28},{28,24},{32,36},... | collective-permute-start | bytes 1277960 | tf_op jit(solution)/shard_map/ppermute | solution.py:582
  59.3 3.2 %collective-permute-start = (f32[104,128]{1,0:T(8,128)S(1)}, f32[104,128]{1,0:T(8,128)S(1)}, u32[]{:S(2)}, u32[]{:S(2)}) collective-permute-start(f32[104,128]{1,0:T(8,128)S(1)} %get-tuple-element.19), channel_id=1, source_target_pairs={{0,1},{1,0},{2,3},{3,2},{4,5},{5,4},{6,7},{7,6},{8,9},{9,8},{10,11... | collective-permute-start | bytes 159752 | tf_op jit(solution)/shard_map/ppermute | solution.py:580
  62.5 0.0 collective-permute-start.1
  62.5 4.4 %collective-permute-start.2 = (f32[2,104,512]{2,1,0:T(8,128)S(1)}, f32[2,104,512]{2,1,0:T(8,128)S(1)}, u32[]{:S(2)}, u32[]{:S(2)}) collective-permute-start(f32[2,104,512]{2,1,0:T(8,128)S(1)} %get-tuple-element.23), channel_id=1, source_target_pairs={{4,8},{8,4},{12,16},{16,12},{20,24},{24,20},{28,32},{32,28},{36,40... | collective-permute-start | bytes 1277960 | tf_op jit(solution)/shard_map/ppermute | solution.py:581
  66.9 1.6 %shard_map.76.body_ref = f32[2,8,100,512]{3,2,1,0:T(8,128)S(1)} custom-call(f32[2,8,104,512]{3,2,1,0:T(8,128)S(1)} %get-tuple-element.21.field, f32[4,8,100,512]{3,2,1,0:T(8,128)S(1)} %get-tuple-element.22.courant_ref, s32[8,512]{1,0:T(8,128)S(1)} %copy-done), custom_call_target="tpu_custom_call" | custom-call | flops 3000000000 | bytes 8000000 | tf_op jit(solution)/shard_map/pallas_call | solution.py:378
  68.5 0.0 collective-permute-done.pair_ref
  68.5 0.0 collective-permute-done.1.other_ref
  68.5 0.0 collective-permute-done.3.near_in
  68.5 2.9 %shard_map.77 = (f32[2,8,104,512]{3,2,1,0:T(8,128)S(1)}, f32[104,128]{1,0:T(8,128)S(1)}, f32[104,128]{1,0:T(8,128)S(1)}) custom-call(s32[2]{0:T(128)S(1)} %pad_add_fusion.odd_ref, f32[104,128]{1,0:T(8,128)S(1)} %collective-permute-done.pair_ref, f32[104,128]{1,0:T(8,128)S(1)} %collective-permute-done.1.other_ref, ...), custom_call_target="tpu_custom_call" | custom-call | flops 3000000000 | bytes 8000000 | tf_op jit(solution)/shard_map/pallas_call | solution.py:446
  71.4 2.7 %collective-permute-done.2.far_in = f32[2,104,512]{2,1,0:T(8,128)S(1)} collective-permute-done((f32[2,104,512]{2,1,0:T(8,128)S(1)}, f32[2,104,512]{2,1,0:T(8,128)S(1)}, u32[]{:S(2)}, u32[]{:S(2)}) %collective-permute-start.2) | collective-permute-done | bytes 426016 | tf_op jit(solution)/shard_map/ppermute | solution.py:581
  74.0 1.3 %shard_map.78 = (f32[2,8,104,512]{3,2,1,0:T(8,128)S(1)}, f32[2,104,512]{2,1,0:T(8,128)S(1)}, f32[2,104,512]{2,1,0:T(8,128)S(1)}, f32[104,128]{1,0:T(8,128)S(1)}, f32[104,128]{1,0:T(8,128)S(1)}) custom-call(s32[2]{0:T(128)S(1)} %pad_add_fusion.odd_ref, f32[104,128]{1,0:T(8,128)S(1)} %collective-permute-done.pair_ref, ...), custom_call_target="tpu_custom_call", output_to_operand_aliasing={{0}: (8, {})} | custom-call | tf_op jit(solution)/shard_map/pallas_call | solution.py:455
  75.4 0.1 collective-permute-start.7
  75.5 0.2 collective-permute-start.4
  75.7 3.2 %collective-permute-start.5 = (f32[104,128]{1,0:T(8,128)S(1)}, f32[104,128]{1,0:T(8,128)S(1)}, u32[]{:S(2)}, u32[]{:S(2)}) collective-permute-start(f32[104,128]{1,0:T(8,128)S(1)} %get-tuple-element.29), channel_id=1, source_target_pairs={{0,3},{1,2},{2,1},{3,0},{4,7},{5,6},{6,5},{7,4},{8,11},{9,10},{10,... | collective-permute-start | bytes 159752 | tf_op jit(solution)/shard_map/ppermute | solution.py:579
  78.9 3.5 %collective-permute-start.6 = (f32[2,104,512]{2,1,0:T(8,128)S(1)}, f32[2,104,512]{2,1,0:T(8,128)S(1)}, u32[]{:S(2)}, u32[]{:S(2)}) collective-permute-start(f32[2,104,512]{2,1,0:T(8,128)S(1)} %get-tuple-element.31), channel_id=1, source_target_pairs={{4,8},{8,4},{12,16},{16,12},{20,24},{24,20},{28,32},{32,28},{36,40... | collective-permute-start | bytes 1277960 | tf_op jit(solution)/shard_map/ppermute | solution.py:581
  82.4 1.6 %shard_map.79.body_ref = f32[2,8,100,512]{3,2,1,0:T(8,128)S(1)} custom-call(f32[2,8,104,512]{3,2,1,0:T(8,128)S(1)} %get-tuple-element.30.field, f32[4,8,100,512]{3,2,1,0:T(8,128)S(1)} %get-tuple-element.22.courant_ref, s32[8,512]{1,0:T(8,128)S(1)} %copy-done), custom_call_target="tpu_custom_call" | custom-call | flops 3000000000 | bytes 8000000 | tf_op jit(solution)/shard_map/pallas_call | solution.py:378
  84.0 0.0 collective-permute-done.4.pair_ref
  84.0 0.0 collective-permute-done.5.other_ref
  84.0 0.0 collective-permute-done.7.near_in
  84.0 2.7 %shard_map.80.part_ref = f32[2,100,8,512]{3,2,1,0:T(8,128)} custom-call(s32[2]{0:T(128)S(1)} %pad_add_fusion.odd_ref, f32[104,128]{1,0:T(8,128)S(1)} %collective-permute-done.4.pair_ref, f32[104,128]{1,0:T(8,128)S(1)} %collective-permute-done.5.other_ref, f32[2,8,104,512]{3,2,1,0:T(8,128)S(1)} %get-tuple-element.30.field, ...), custom_call_target="tpu_custom_call" | custom-call | flops 3000000000 | bytes 8000000 | tf_op jit(solution)/shard_map/pallas_call | solution.py:543
  86.7 3.7 %collective-permute-done.6.far_in = f32[2,104,512]{2,1,0:T(8,128)S(1)} collective-permute-done((f32[2,104,512]{2,1,0:T(8,128)S(1)}, f32[2,104,512]{2,1,0:T(8,128)S(1)}, u32[]{:S(2)}, u32[]{:S(2)}) %collective-permute-start.6) | collective-permute-done | bytes 426016 | tf_op jit(solution)/shard_map/ppermute | solution.py:581
  90.4 1.8 %shard_map.81 = f32[2,100,8,512]{3,2,1,0:T(8,128)} custom-call(s32[2]{0:T(128)S(1)} %pad_add_fusion.odd_ref, f32[104,128]{1,0:T(8,128)S(1)} %collective-permute-done.4.pair_ref, f32[104,128]{1,0:T(8,128)S(1)} %collective-permute-done.5.other_ref, f32[2,8,104,512]{3,2,1,0:T(8,128)S(1)} %get-tuple-element.30.field, ...), custom_call_target="tpu_custom_call", output_to_operand_aliasing={{}: (7, {})} | custom-call | tf_op jit(solution)/shard_map/pallas_call | solution.py:553
  (5 shorter events, 0.1 us)
Async XLA Ops:
  0.0 18.6 %copy-start.1 = (f32[8,100,100]{2,0,1:T(8,128)S(1)}, f32[8,100,100]{2,0,1:T(8,128)}, u32[]{:S(2)}) copy-start(f32[8,100,100]{2,0,1:T(8,128)} %param.9) | copy-start | bytes 960004
  8.1 40.7 %all-to-all-start = ((f32[4224,1,128]{2,1,0:T(1,128)}), f32[4224,1,128]{2,1,0:T(1,128)S(1)}, u32[]{:S(2)}, u32[]{:S(2)}) async-start(f32[4224,1,128]{2,1,0:T(1,128)} %shard_map.73), calls=%async_computation | async-start | bytes 4325376 | tf_op jit(solution)/shard_map/all_to_all | solution.py:592
  28.5 38.4 %copy-start = (s32[8,512]{1,0:T(8,128)S(1)}, s32[8,512]{1,0:T(8,128)}, u32[]{:S(2)}) copy-start(s32[8,512]{1,0:T(8,128)} %mask_ref.11) | copy-start | bytes 49156
  58.0 10.5 %collective-permute-start.3 = (f32[2,104,512]{2,1,0:T(8,128)S(1)}, f32[2,104,512]{2,1,0:T(8,128)S(1)}, u32[]{:S(2)}, u32[]{:S(2)}) collective-permute-start(f32[2,104,512]{2,1,0:T(8,128)S(1)} %get-tuple-element.24), channel_id=1, source_target_pairs={{0,4},{4,0},{8,12},{12,8},{16,20},{20,16},{24,28},{28,24},{32,36},... | collective-permute-start | bytes 1277960 | tf_op jit(solution)/shard_map/ppermute | solution.py:582
  59.3 9.2 %collective-permute-start = (f32[104,128]{1,0:T(8,128)S(1)}, f32[104,128]{1,0:T(8,128)S(1)}, u32[]{:S(2)}, u32[]{:S(2)}) collective-permute-start(f32[104,128]{1,0:T(8,128)S(1)} %get-tuple-element.19), channel_id=1, source_target_pairs={{0,1},{1,0},{2,3},{3,2},{4,5},{5,4},{6,7},{7,6},{8,9},{9,8},{10,11... | collective-permute-start | bytes 159752 | tf_op jit(solution)/shard_map/ppermute | solution.py:580
  62.5 6.0 %collective-permute-start.1 = (f32[104,128]{1,0:T(8,128)S(1)}, f32[104,128]{1,0:T(8,128)S(1)}, u32[]{:S(2)}, u32[]{:S(2)}) collective-permute-start(f32[104,128]{1,0:T(8,128)S(1)} %get-tuple-element.20), channel_id=1, source_target_pairs={{0,3},{1,2},{2,1},{3,0},{4,7},{5,6},{6,5},{7,4},{8,11},{9,10},{10,... | collective-permute-start | bytes 159752 | tf_op jit(solution)/shard_map/ppermute | solution.py:579
  62.5 11.5 %collective-permute-start.2 = (f32[2,104,512]{2,1,0:T(8,128)S(1)}, f32[2,104,512]{2,1,0:T(8,128)S(1)}, u32[]{:S(2)}, u32[]{:S(2)}) collective-permute-start(f32[2,104,512]{2,1,0:T(8,128)S(1)} %get-tuple-element.23), channel_id=1, source_target_pairs={{4,8},{8,4},{12,16},{16,12},{20,24},{24,20},{28,32},{32,28},{36,40... | collective-permute-start | bytes 1277960 | tf_op jit(solution)/shard_map/ppermute | solution.py:581
  75.4 8.6 %collective-permute-start.7 = (f32[2,104,512]{2,1,0:T(8,128)S(1)}, f32[2,104,512]{2,1,0:T(8,128)S(1)}, u32[]{:S(2)}, u32[]{:S(2)}) collective-permute-start(f32[2,104,512]{2,1,0:T(8,128)S(1)} %get-tuple-element.32), channel_id=1, source_target_pairs={{0,4},{4,0},{8,12},{12,8},{16,20},{20,16},{24,28},{28,24},{32,36},... | collective-permute-start | bytes 1277960 | tf_op jit(solution)/shard_map/ppermute | solution.py:582
  75.5 8.5 %collective-permute-start.4 = (f32[104,128]{1,0:T(8,128)S(1)}, f32[104,128]{1,0:T(8,128)S(1)}, u32[]{:S(2)}, u32[]{:S(2)}) collective-permute-start(f32[104,128]{1,0:T(8,128)S(1)} %get-tuple-element.28), channel_id=1, source_target_pairs={{0,1},{1,0},{2,3},{3,2},{4,5},{5,4},{6,7},{7,6},{8,9},{9,8},{10,11... | collective-permute-start | bytes 159752 | tf_op jit(solution)/shard_map/ppermute | solution.py:580
  75.7 8.3 %collective-permute-start.5 = (f32[104,128]{1,0:T(8,128)S(1)}, f32[104,128]{1,0:T(8,128)S(1)}, u32[]{:S(2)}, u32[]{:S(2)}) collective-permute-start(f32[104,128]{1,0:T(8,128)S(1)} %get-tuple-element.29), channel_id=1, source_target_pairs={{0,3},{1,2},{2,1},{3,0},{4,7},{5,6},{6,5},{7,4},{8,11},{9,10},{10,... | collective-permute-start | bytes 159752 | tf_op jit(solution)/shard_map/ppermute | solution.py:579
  78.9 11.5 %collective-permute-start.6 = (f32[2,104,512]{2,1,0:T(8,128)S(1)}, f32[2,104,512]{2,1,0:T(8,128)S(1)}, u32[]{:S(2)}, u32[]{:S(2)}) collective-permute-start(f32[2,104,512]{2,1,0:T(8,128)S(1)} %get-tuple-element.31), channel_id=1, source_target_pairs={{4,8},{8,4},{12,16},{16,12},{20,24},{24,20},{28,32},{32,28},{36,40... | collective-permute-start | bytes 1277960 | tf_op jit(solution)/shard_map/ppermute | solution.py:581
